TPU v7x, 32 devices: a whole 2x2x4 slice. The times are simulated.
32 devices in a mesh: rows: 8 (over z, y), seq: 4 (over x, core).
Axes of the slice: x: 2, y: 2, z: 4, core: 2. Of those that a mesh axis runs over, the one named last changes fastest.
Arguments:
- hidden_in: bfloat16 [2, 16, 1024, 768], P(None, 'rows', 'seq'), may hold values from -6 to 6
- segments: int32 [2, 16, 1024], P(None, 'rows', 'seq'), may hold values from 0 to 1, as said below
- grad_mask: int32 [2, 16, 1024], P(None, 'rows', 'seq'), may hold values 0 or 1
- grad_out: bfloat16 [2, 16, 1024, 768], P(None, 'rows', 'seq'), may hold values from -6 to 6
- query_proj: bfloat16 [768, 768], replicated, may hold values from -0.21875 to 0.21875
- query_bias: bfloat16 [768], replicated, may hold values from -3 to 3
- key_proj: bfloat16 [768, 768], replicated, may hold values from -0.21875 to 0.21875
- value_proj: bfloat16 [768, 768], replicated, may hold values from -0.21875 to 0.21875
- value_bias: bfloat16 [768], replicated, may hold values from -3 to 3
- output_proj: bfloat16 [768, 768], replicated, may hold values from -0.875 to 0.875
- output_bias: bfloat16 [768], replicated, may hold values from -1.75 to 1.75
- first_gain: bfloat16 [768], replicated, may hold values from 0.25 to 1.75
- first_shift: bfloat16 [768], replicated, may hold values from -3 to 3
- expand_proj: bfloat16 [768, 3072], replicated, may hold values from -0.21875 to 0.21875
- expand_bias: bfloat16 [3072], replicated, may hold values from -3 to 3
- shrink_proj: bfloat16 [3072, 768], replicated, may hold values from -0.109375 to 0.109375
- shrink_bias: bfloat16 [768], replicated, may hold values from -1.75 to 1.75
- second_gain: bfloat16 [768], replicated, may hold values from 0.25 to 1.75
- second_shift: bfloat16 [768], replicated, may hold values from -3 to 3
Outputs:
- layer_out: bfloat16 [2, 16, 1024, 768], P(None, 'rows', 'seq')
- grad_in: bfloat16 [2, 16, 1024, 768], P(None, 'rows', 'seq')
- query_proj_grad: float32 [768, 768], replicated
- query_bias_grad: float32 [768], replicated
- key_proj_grad: float32 [768, 768], replicated
- value_proj_grad: float32 [768, 768], replicated
- value_bias_grad: float32 [768], replicated
- output_proj_grad: float32 [768, 768], replicated
- output_bias_grad: float32 [768], replicated
- first_gain_grad: float32 [768], replicated
- first_shift_grad: float32 [768], replicated
- expand_proj_grad: float32 [768, 3072], replicated
- expand_bias_grad: float32 [3072], replicated
- shrink_proj_grad: float32 [3072, 768], replicated
- shrink_bias_grad: float32 [768], replicated
- second_gain_grad: float32 [768], replicated
- second_shift_grad: float32 [768], replicated
Inputs may be any that keep to these rules, and one draw needn't show every extreme that they name: `segments`: in every row the segment numbers are 0 up to a cut and 1 after it; both occur in every row.
All inputs are finite; a program needn't handle non-finite values. No bound on the sum of `grad_mask` on one device may be relied on, other than what follows from the above.
Results may differ from a plain program's by a relative error of at most 0.013.
Values may be sent and summed in bfloat16 or wider, within the bound.
No kernel may reach another device: no remote copies, remote signals or barrier semaphores. Data moves between devices by JAX's collectives and lax.ppermute only.
A program may use at most 320 MiB of HBM per device.

v0:
```python
import functools

import jax
import jax.numpy as jnp
from jax import lax
from jax.experimental import pallas as pl
from jax.experimental.pallas import tpu as pltpu
from jax.sharding import PartitionSpec as P

DH = 64
PAIR = 128
MASKED = 1e30
F32 = jnp.float32
BF16 = jnp.bfloat16
NT = (((1,), (1,)), ((), ()))
NN = (((1,), (0,)), ((), ()))
BRIEF = pl.CostEstimate(flops=1, bytes_accessed=1, transcendentals=0)


def left_dot(first, second):
    return lax.dot_general(first, second, (((0,), (0,)), ((), ())), preferred_element_type=F32)


def right_dot(first, second):
    return lax.dot_general(first, second, NT, preferred_element_type=F32)


def split_three(values):
    high = values.astype(BF16)
    rest = values - high.astype(F32)
    middle = rest.astype(BF16)
    low = (rest - middle.astype(F32)).astype(BF16)
    return high.astype(F32), middle.astype(F32), low.astype(F32)


def own_lanes(shape, head):
    lane = lax.broadcasted_iota(jnp.int32, shape, 1)
    own = lane < DH if head == 0 else lane >= DH
    return own, lane % DH


def key_features(lane, seg):
    return jnp.where(
        lane < 3,
        1.0,
        jnp.where(lane == 3, -MASKED * (1.0 - seg), jnp.where(lane == 4, -MASKED * seg, 0.0)),
    ).astype(BF16)


def forward_kernel(q_ref, k_ref, v_ref, seg_q_ref, seg_k_ref, mixed_ref, query_ref, *, block):
    queries = q_ref.shape[0]
    keys = k_ref.shape[0]
    for head in range(2):
        own_k, lane_k = own_lanes((keys, PAIR), head)
        key_side = jnp.where(own_k, k_ref[...], key_features(lane_k, seg_k_ref[...].astype(F32)))
        value_side = jnp.where(own_k, v_ref[...], jnp.ones((), BF16))
        own_q, lane_q = own_lanes((block, PAIR), head)
        for start in range(0, queries, block):
            here = slice(start, start + block)
            q = q_ref[here, :]
            seg = seg_q_ref[here, :].astype(F32)
            seg_side = jnp.where(lane_q == 3, seg, jnp.where(lane_q == 4, 1.0 - seg, 0.0))
            query_side = jnp.where(own_q, q, seg_side.astype(BF16))
            scores = lax.dot_general(query_side, key_side, NT, preferred_element_type=F32)
            peak = jnp.max(scores, -1, keepdims=True)
            raised = jnp.exp(scores - peak).astype(BF16)
            summed = lax.dot_general(raised, value_side, NN, preferred_element_type=F32)
            total = summed[:, DH : DH + 1] if head == 0 else summed[:, 0:1]
            mixed = (summed / total).astype(BF16)
            shift = jnp.broadcast_to(-(peak + jnp.log(total)), (block, PAIR))
            high, middle, low = split_three(shift)
            extra = jnp.where(
                lane_q == 0,
                high,
                jnp.where(lane_q == 1, middle, jnp.where(lane_q == 2, low, seg_side)),
            )
            query_ref[head, here, :] = jnp.where(own_q, q, extra.astype(BF16))
            if head == 0:
                mixed_ref[here, :] = mixed
            else:
                mixed_ref[here, :] = jnp.where(own_q, mixed, mixed_ref[here, :])


def attention_forward(q, k, v, seg_q, seg_k):
    queries, width = q.shape
    keys = k.shape[0]
    pairs = width // PAIR
    column = lambda i: (0, i)
    whole = lambda i: (0, 0)
    return pl.pallas_call(
        functools.partial(forward_kernel, block=min(512, queries)),
        grid=(pairs,),
        in_specs=[
            pl.BlockSpec((queries, PAIR), column),
            pl.BlockSpec((keys, PAIR), column),
            pl.BlockSpec((keys, PAIR), column),
            pl.BlockSpec((queries, PAIR), whole),
            pl.BlockSpec((keys, PAIR), whole),
        ],
        out_specs=[
            pl.BlockSpec((queries, PAIR), column),
            pl.BlockSpec((2, queries, PAIR), lambda i: (i, 0, 0)),
        ],
        out_shape=[
            pltpu.HBM((queries, width), BF16),
            pltpu.HBM((2 * pairs, queries, PAIR), BF16),
        ],
        compiler_params=pltpu.CompilerParams(vmem_limit_bytes=24 * 2**20),
        cost_estimate=BRIEF,
        name="attention_forward",
    )(q, k, v, seg_q, seg_k)


def backward_kernel(
    query_ref, k_ref, v_ref, seg_k_ref, mixed_ref, d_mixed_ref, *refs, block
):
    dq_ref, dk_ref, dv_ref, dqt = refs[-4:]
    queries = mixed_ref.shape[0]
    keys = k_ref.shape[0]
    d_mixed = d_mixed_ref[...]
    product = d_mixed.astype(F32) * mixed_ref[...].astype(F32)
    for head in range(2):
        own_q, lane_q = own_lanes((queries, PAIR), head)
        own_k, lane_k = own_lanes((block, PAIR), head)
        delta = -jnp.sum(jnp.where(own_q, product, 0.0), -1, keepdims=True)
        high, middle, low = split_three(jnp.broadcast_to(delta, (queries, PAIR)))
        extra = jnp.where(
            lane_q == 0, high, jnp.where(lane_q == 1, middle, jnp.where(lane_q == 2, low, 0.0))
        )
        d_side = jnp.where(own_q, d_mixed, extra.astype(BF16))
        query_side = query_ref[head]
        ones = jnp.where(lane_k < 3, 1.0, 0.0).astype(BF16)
        for start in range(0, keys, block):
            here = slice(start, start + block)
            k = k_ref[here, :]
            seg = seg_k_ref[here, :].astype(F32)
            key_side = jnp.where(own_k, k, key_features(lane_k, seg))
            value_side = jnp.where(own_k, v_ref[here, :], ones)
            shifted = lax.dot_general(key_side, query_side, NT, preferred_element_type=F32)
            probs = jnp.exp(shifted)
            d_probs = lax.dot_general(value_side, d_side, NT, preferred_element_type=F32)
            d_scores = (probs * d_probs).astype(BF16)
            dv = lax.dot_general(probs.astype(BF16), d_mixed, NN, preferred_element_type=F32)
            dk = lax.dot_general(d_scores, query_side, NN, preferred_element_type=F32)
            turned = k.T[head * DH : (head + 1) * DH, :]
            dq = lax.dot_general(turned, d_scores, NN, preferred_element_type=F32)
            mine = slice(head * DH, (head + 1) * DH)
            if start == 0:
                dqt[mine, :] = dq
            else:
                dqt[mine, :] += dq
            dv = dv.astype(dv_ref.dtype)
            dk = dk.astype(dk_ref.dtype)
            if head == 0:
                dk_ref[here, :] = dk
                dv_ref[here, :] = dv
            else:
                dk_ref[here, :] = jnp.where(own_k, dk, dk_ref[here, :])
                dv_ref[here, :] = jnp.where(own_k, dv, dv_ref[here, :])
    dq_ref[...] = (dqt[...] * 0.125).astype(BF16).T


def attention_backward(query_side, k, v, seg_k, mixed, d_mixed, kept, first, count, before):
    queries, width = mixed.shape
    keys = k.shape[0]
    column = lambda i: (0, i + first)
    held = [] if before is None else list(before)
    return pl.pallas_call(
        functools.partial(backward_kernel, block=min(512, keys)),
        grid=(count,),
        in_specs=[
            pl.BlockSpec((2, queries, PAIR), lambda i: (i + first, 0, 0)),
            pl.BlockSpec((keys, PAIR), column),
            pl.BlockSpec((keys, PAIR), column),
            pl.BlockSpec((keys, PAIR), lambda i: (0, 0)),
            pl.BlockSpec((queries, PAIR), column),
            pl.BlockSpec((queries, PAIR), column),
        ]
        + [pl.BlockSpec(memory_space=pl.ANY)] * len(held),
        out_specs=[
            pl.BlockSpec((queries, PAIR), column),
            pl.BlockSpec((keys, PAIR), column),
            pl.BlockSpec((keys, PAIR), column),
        ],
        input_output_aliases={6 + i: i for i in range(len(held))},
        out_shape=[
            pltpu.HBM((queries, width), BF16),
            pltpu.HBM((keys, width), kept),
            pltpu.HBM((keys, width), kept),
        ],
        scratch_shapes=[pltpu.VMEM((PAIR, queries), F32)],
        compiler_params=pltpu.CompilerParams(vmem_limit_bytes=24 * 2**20),
        cost_estimate=BRIEF,
        name="attention_backward",
    )(in_hbm(query_side), k, v, seg_k, in_hbm(mixed), in_hbm(d_mixed), *map(in_hbm, held))


def dot(first, second, dims=NN):
    return lax.dot_general(first, second, dims, preferred_element_type=F32)


def gelu_pair(values):
    below = 0.5 + 0.5 * lax.erf(values * 0.7071067811865476)
    density = jnp.exp(-0.5 * values * values) * 0.3989422804014327
    return values * below, below + values * density


def normalise(values):
    centred = values - jnp.mean(values, -1, keepdims=True)
    scale = lax.rsqrt(jnp.mean(centred * centred, -1, keepdims=True) + 1e-06)
    return centred * scale, scale


def norm_back(upstream, hat, scale, gain):
    d_hat = upstream * gain
    return scale * (
        d_hat
        - jnp.mean(d_hat, -1, keepdims=True)
        - hat * jnp.mean(d_hat * hat, -1, keepdims=True)
    )


def stack_rows(rows):
    filler = jnp.zeros((8 - len(rows), rows[0].shape[1]), F32)
    return jnp.concatenate(rows + [filler], 0)


def feed_forward_kernel(
    inputs_ref,
    mixed_ref,
    output_proj_ref,
    output_bias_ref,
    gain_one_ref,
    shift_one_ref,
    expand_ref,
    expand_bias_ref,
    shrink_ref,
    shrink_bias_ref,
    gain_two_ref,
    shift_two_ref,
    *refs,
    steps,
    held,
):
    upstream_refs = refs[:held]
    hat_out, scale_ref, normed_out, active_t_ref, slope_ref = refs[held : held + 5]
    d_down_ref, sums_ref = refs[held + 5 : held + 7]
    out_refs = refs[held + 7 : 2 * held + 7]
    total, hat_ref, normed_ref, sems = refs[2 * held + 7 :]
    block = total.shape[0] // held
    early = [
        pltpu.make_async_copy(hat_ref, hat_out, sems.at[0]),
        pltpu.make_async_copy(normed_ref, normed_out, sems.at[1]),
    ]
    step = pl.program_id(0)
    tokens = total.shape[0]
    pieces = [slice(start, start + block) for start in range(0, tokens, block)]

    @pl.when(step == 0)
    def _():
        for here in pieces:
            first_sum = (
                inputs_ref[here, :].astype(F32)
                + dot(mixed_ref[here, :], output_proj_ref[...])
                + output_bias_ref[...].astype(F32)
            )
            hat, scale = normalise(first_sum)
            hat_ref[here, :] = hat.astype(BF16)
            scale_ref[here, :] = jnp.broadcast_to(scale, (block, PAIR))
            normed = gain_one_ref[...].astype(F32) * hat + shift_one_ref[...].astype(F32)
            normed_ref[here, :] = normed.astype(BF16)
            total[here, :] = normed + shrink_bias_ref[...].astype(F32)
        for copy in early:
            copy.start()

    for here in pieces:
        expanded = dot(normed_ref[here, :], expand_ref[...]) + expand_bias_ref[...].astype(F32)
        active, slope = gelu_pair(expanded)
        active = active.astype(BF16)
        slope_ref[here, :] = slope.astype(BF16)
        active_t_ref[:, here] = active.T
        total[here, :] += dot(active, shrink_ref[...])

    @pl.when(step == steps - 1)
    def _():
        gain = gain_two_ref[...].astype(F32)
        d_gain = jnp.zeros((1, total.shape[1]), F32)
        d_shift = d_gain
        d_bias = d_gain
        for here, upstream_ref, out_ref in zip(pieces, upstream_refs, out_refs):
            hat, scale = normalise(total[here, :])
            out_ref[...] = (gain * hat + shift_two_ref[...].astype(F32)).astype(BF16)
            upstream = upstream_ref[...].astype(F32)
            d_gain += jnp.sum(upstream * hat, 0, keepdims=True)
            d_shift += jnp.sum(upstream, 0, keepdims=True)
            d_down = norm_back(upstream, hat, scale, gain).astype(BF16)
            d_down_ref[here, :] = d_down
            d_bias += jnp.sum(d_down.astype(F32), 0, keepdims=True)
        sums_ref[...] = stack_rows([d_gain, d_shift, d_bias])
        for copy in early:
            copy.wait()


def in_hbm(values):
    return pltpu.with_memory_space_constraint(values, pltpu.HBM)


def hbm_shapes(*pairs):
    return [pltpu.HBM(shape, dtype) for shape, dtype in pairs]


def fixed(*shape):
    return pl.BlockSpec(shape, lambda i: (0,) * len(shape), pipeline_mode=pl.Buffered(1))


def shapes(*pairs):
    return [jax.ShapeDtypeStruct(shape, dtype) for shape, dtype in pairs]


def feed_forward(inputs, mixed, upstream, weights, block=768):
    tokens, width = inputs.shape
    units = weights[4].shape[1]
    steps = units // block
    held = len(upstream)
    piece = tokens // held
    row = fixed(1, width)
    return pl.pallas_call(
        functools.partial(feed_forward_kernel, steps=steps, held=held),
        grid=(steps,),
        in_specs=[fixed(tokens, width)] * 2
        + [fixed(width, width), row, row, row]
        + [
            pl.BlockSpec((width, block), lambda i: (0, i)),
            pl.BlockSpec((1, block), lambda i: (0, i)),
            pl.BlockSpec((block, width), lambda i: (i, 0)),
            row,
            row,
            row,
        ]
        + [fixed(piece, width)] * held,
        out_specs=[
            pl.BlockSpec(memory_space=pl.ANY),
            fixed(tokens, PAIR),
            pl.BlockSpec(memory_space=pl.ANY),
            pl.BlockSpec((block, tokens), lambda i: (i, 0)),
            pl.BlockSpec((tokens, block), lambda i: (0, i)),
            fixed(tokens, width),
            fixed(8, width),
        ]
        + [fixed(piece, width)] * held,
        out_shape=hbm_shapes(
            ((tokens, width), BF16),
            ((tokens, PAIR), F32),
            ((tokens, width), BF16),
            ((units, tokens), BF16),
            ((tokens, units), BF16),
            ((tokens, width), BF16),
            ((8, width), F32),
        )
        + shapes(*[((piece, width), BF16)] * held),
        scratch_shapes=[
            pltpu.VMEM((tokens, width), F32),
            pltpu.VMEM((tokens, width), BF16),
            pltpu.VMEM((tokens, width), BF16),
            pltpu.SemaphoreType.DMA((2,)),
        ],
        compiler_params=pltpu.CompilerParams(vmem_limit_bytes=36 * 2**20),
        cost_estimate=BRIEF,
        name="feed_forward",
    )(inputs, in_hbm(mixed), *map(in_hbm, weights), *upstream)


def feed_back_kernel(
    which_ref,
    d_down_ref,
    slope_ref,
    active_t_ref,
    shrink_ref,
    expand_ref,
    normed_ref,
    *refs,
    steps,
    block,
    last,
):
    step = pl.program_id(0)
    if last:
        gain_ref, *late_refs = refs[:5]
        grads_ref, bias_ref, d_attn_ref, d_mixed_ref, sums_ref = refs[5:10]
        turned, total, hat_ref, scale_ref, output_proj_ref, sems = refs[10:]
        late = [
            pltpu.make_async_copy(source, target, sems.at[index])
            for index, (source, target) in enumerate(
                zip(late_refs, (d_attn_ref, hat_ref, scale_ref, output_proj_ref))
            )
        ]

        @pl.when(step == 0)
        def _():
            for copy in late:
                copy.start()

    else:
        grads_ref, bias_ref, total_ref, turned, total = refs
    tokens = total.shape[0]
    pieces = [slice(start, start + block) for start in range(0, tokens, block)]

    @pl.when(step == 0)
    def _():
        total[...] = jnp.zeros_like(total)
        bias_ref[...] = jnp.zeros_like(bias_ref)

    bias = jnp.zeros((1, slope_ref.shape[1]), F32)
    for here in pieces:
        d_active = dot(d_down_ref[here, :], shrink_ref[...], NT)
        d_expand = (d_active * slope_ref[here, :].astype(F32)).astype(BF16)
        turned[:, here] = d_expand.T
        bias += jnp.sum(d_expand.astype(F32), 0, keepdims=True)
        total[here, :] += dot(d_expand, expand_ref[...], NT)
    row = lax.broadcasted_iota(jnp.int32, bias_ref.shape, 0)
    bias_ref[...] = jnp.where(row == step, bias, bias_ref[...])
    grads_ref[0] = dot(active_t_ref[...], d_down_ref[...]).astype(BF16)
    grads_ref[1] = dot(turned[...], normed_ref[...]).astype(BF16)

    if not last:

        @pl.when(step == steps - 1)
        def _():
            total_ref[...] = total[...].astype(BF16)

    else:

        @pl.when(step == steps - 1)
        def _():
            for copy in late:
                copy.wait()
            gain = gain_ref[...].astype(F32)
            d_gain = jnp.zeros((1, total.shape[1]), F32)
            d_shift = d_gain
            d_bias = d_gain
            for here in pieces:
                d_normed = total[here, :] + (
                    d_down_ref[here, :].astype(F32) + d_attn_ref[here, :].astype(F32)
                )
                hat = hat_ref[here, :].astype(F32)
                d_gain += jnp.sum(d_normed * hat, 0, keepdims=True)
                d_shift += jnp.sum(d_normed, 0, keepdims=True)
                d_attn = norm_back(d_normed, hat, scale_ref[here, :][:, 0:1], gain).astype(BF16)
                d_attn_ref[here, :] = d_attn
                d_bias += jnp.sum(d_attn.astype(F32), 0, keepdims=True)
                d_mixed_ref[here, :] = dot(d_attn, output_proj_ref[...], NT).astype(BF16)
            sums_ref[...] = stack_rows([d_gain, d_shift, d_bias])


def feed_back(which, d_down, slope, active_t, shrink, expand, normed, norm, block=512):
    tokens, width = d_down.shape
    half = slope.shape[1] // 2
    steps = half // block
    last = norm is not None
    at = lambda i, which: which[0] * steps + i
    whole = lambda *shape: pl.BlockSpec(
        shape, lambda i, which: (0,) * len(shape), pipeline_mode=pl.Buffered(1)
    )
    in_specs = [
        whole(tokens, width),
        pl.BlockSpec((tokens, block), lambda i, which: (0, at(i, which))),
        pl.BlockSpec((block, tokens), lambda i, which: (at(i, which), 0)),
        pl.BlockSpec((block, width), lambda i, which: (at(i, which), 0)),
        pl.BlockSpec((width, block), lambda i, which: (0, at(i, which))),
        whole(tokens, width),
    ]
    out_specs = [
        pl.BlockSpec((2, block, width), lambda i, which: (0, i, 0)),
        whole(8, block),
    ]
    out_shape = hbm_shapes(((2, half, width), BF16), ((8, block), F32))
    scratch = [pltpu.VMEM((block, tokens), BF16), pltpu.VMEM((tokens, width), F32)]
    extra = ()
    if last:
        gain, *late = norm
        extra = (gain, *map(in_hbm, late))
        in_specs += [whole(1, width)] + [pl.BlockSpec(memory_space=pl.ANY)] * len(late)
        out_specs += [whole(tokens, width)] * 2 + [whole(8, width)]
        out_shape += hbm_shapes(
            ((tokens, width), BF16), ((tokens, width), BF16), ((8, width), F32)
        )
        scratch += [
            pltpu.VMEM((tokens, width), BF16),
            pltpu.VMEM((tokens, PAIR), F32),
            pltpu.VMEM((width, width), BF16),
            pltpu.SemaphoreType.DMA((4,)),
        ]
    else:
        out_specs.append(whole(tokens, width))
        out_shape += hbm_shapes(((tokens, width), BF16))
    return pl.pallas_call(
        functools.partial(feed_back_kernel, steps=steps, block=min(512, tokens), last=last),
        grid_spec=pltpu.PrefetchScalarGridSpec(
            num_scalar_prefetch=1,
            grid=(steps,),
            in_specs=in_specs,
            out_specs=out_specs,
            scratch_shapes=scratch,
        ),
        out_shape=out_shape,
        compiler_params=pltpu.CompilerParams(vmem_limit_bytes=44 * 2**20),
        cost_estimate=BRIEF,
        name="feed_back_last" if last else "feed_back",
    )(which, *map(in_hbm, (d_down, slope, active_t, shrink, expand, normed)), *extra)


def pack_kernel(at_ref, flat_ref, marks_ref, *refs, order):
    outs, sems = refs[:-1], refs[-1]
    piece = flat_ref.shape[1]
    for part, out_ref in zip(order, outs):
        marks = marks_ref[pl.ds(at_ref[0] ^ part, 1), :].astype(F32)
        out_ref[piece:, :] = jnp.zeros((MARK_ROWS, out_ref.shape[1]), BF16)
        out_ref[piece:, 0:piece] = jnp.broadcast_to(marks, (MARK_ROWS, piece)).astype(BF16)
    copies = [
        pltpu.make_async_copy(
            flat_ref.at[at_ref[0] ^ part], out_ref.at[pl.ds(0, piece)], sems.at[index]
        )
        for index, (part, out_ref) in enumerate(zip(order, outs))
    ]
    for copy in copies:
        copy.start()
    for copy in copies:
        copy.wait()


MARK_ROWS = 16


def pack(at, flat, marks, order):
    held, piece, width = flat.shape
    vmem = pl.BlockSpec(memory_space=pltpu.VMEM)
    return pl.pallas_call(
        functools.partial(pack_kernel, order=order),
        in_specs=[
            pl.BlockSpec(memory_space=pltpu.SMEM),
            pl.BlockSpec(memory_space=pl.ANY),
            vmem,
        ],
        out_specs=[vmem] * held,
        out_shape=shapes(*[((piece + MARK_ROWS, width), BF16)] * held),
        scratch_shapes=[pltpu.SemaphoreType.DMA((held,))],
        compiler_params=pltpu.CompilerParams(vmem_limit_bytes=16 * 2**20),
        cost_estimate=BRIEF,
        name="pack",
    )(at, in_hbm(flat), marks)


def unpack_kernel(*refs):
    parts, (rows_ref, marks_ref) = refs[:-2], refs[-2:]
    piece = rows_ref.shape[0] // len(parts)
    for index, ref in enumerate(parts):
        here = slice(index * piece, (index + 1) * piece)
        rows_ref[here, :] = ref[0:piece, :]
        marks = ref[piece:, 0:piece].astype(F32)[0:1, :]
        marks_ref[here, :] = jnp.broadcast_to(marks, (PAIR, piece)).T.astype(BF16)


def unpack(parts):
    width = parts[0].shape[1]
    tokens = len(parts) * (parts[0].shape[0] - MARK_ROWS)
    return pl.pallas_call(
        unpack_kernel,
        grid=(1,),
        in_specs=[fixed(*part.shape) for part in parts],
        out_specs=[fixed(tokens, width), fixed(tokens, PAIR)],
        out_shape=hbm_shapes(((tokens, width), BF16), ((tokens, PAIR), BF16)),
        compiler_params=pltpu.CompilerParams(vmem_limit_bytes=16 * 2**20),
        cost_estimate=BRIEF,
        name="unpack",
    )(*parts)


def weight_kernel(
    core_ref,
    first_sums_ref,
    second_sums_ref,
    own_bias_ref,
    other_bias_ref,
    *refs,
    steps,
):
    sources, (other_ref, own_ref, small_ref) = refs[:6], refs[6:9]
    targets, (inputs_t, mixed_t, sems) = refs[9:15], refs[15:]
    inputs_ref, dq_ref, dk_ref, dv_ref, mixed_ref, d_attn_ref = targets
    copies = [
        pltpu.make_async_copy(source, target, sems.at[index])
        for index, (source, target) in enumerate(zip(sources, targets))
    ]
    for copy in copies:
        copy.start()
    count = inputs_ref.shape[1] // 2
    core = core_ref[0]
    for ref in (other_ref, own_ref):
        if ref.shape[0] > 4 * count:
            ref[4 * count :, :] = jnp.zeros((ref.shape[0] - 4 * count, ref.shape[1]), BF16)
    copies[0].wait()
    inputs_t[...] = inputs_ref[...].T
    for at, right_ref in enumerate((dq_ref, dk_ref, dv_ref, d_attn_ref)):
        copies[at + 1].wait()
        left_ref = inputs_t
        if at == 3:
            copies[5].wait()
            mixed_t[...] = mixed_ref[...].T
            left_ref = mixed_t
        for half, out_ref in ((1 - core, other_ref), (core, own_ref)):
            rows = pl.ds(pl.multiple_of(half * count, PAIR), count)
            out_ref[at * count : (at + 1) * count, :] = dot(left_ref[rows, :], right_ref[...]).astype(
                BF16
            )
    small_ref[...] = jnp.zeros_like(small_ref)
    small_ref[0:1, :] = jnp.sum(dq_ref[...].astype(F32), 0, keepdims=True)
    small_ref[1:2, :] = jnp.sum(dv_ref[...].astype(F32), 0, keepdims=True)
    small_ref[2:5, :] = first_sums_ref[0:3, :]
    small_ref[5:8, :] = second_sums_ref[0:3, :]
    block = own_bias_ref.shape[1]
    own, other = own_bias_ref[0:steps, :], other_bias_ref[0:steps, :]
    small_ref[8 : 8 + steps, 0:block] = jnp.where(core == 0, own, other)
    small_ref[8 + steps : 8 + 2 * steps, 0:block] = jnp.where(core == 0, other, own)


def weight_halves(core, values, unit, sums, steps):
    tokens, width = values[0].shape
    rows = -(-2 * width // unit) * unit
    vmem = pl.BlockSpec(memory_space=pltpu.VMEM)
    anywhere = pl.BlockSpec(memory_space=pl.ANY)
    return pl.pallas_call(
        functools.partial(weight_kernel, steps=steps),
        in_specs=[pl.BlockSpec(memory_space=pltpu.SMEM)] + [vmem] * 4 + [anywhere] * 6,
        out_specs=[vmem] * 3,
        out_shape=shapes(
            ((rows, width), BF16), ((rows, width), BF16), ((SMALL, width), F32)
        ),
        scratch_shapes=[pltpu.VMEM((tokens, width), BF16)] * 6
        + [pltpu.VMEM((width, tokens), BF16)] * 2
        + [pltpu.SemaphoreType.DMA((6,))],
        compiler_params=pltpu.CompilerParams(vmem_limit_bytes=32 * 2**20),
        cost_estimate=BRIEF,
        name="weight_halves",
    )(core, *sums, *map(in_hbm, values))


def input_grad_kernel(*refs, held):
    sources, outs = refs[:7], refs[7 : 7 + held]
    (d_attn, *factors), sems = refs[7 + held : 14 + held], refs[-1]
    copies = [
        pltpu.make_async_copy(source, target, sems.at[index])
        for index, (source, target) in enumerate(zip(sources, (d_attn, *factors)))
    ]
    for copy in copies:
        copy.start()
    piece = outs[0].shape[0]
    total = None
    for index in range(3):
        for copy in copies[2 * index + 1 : 2 * index + 3]:
            copy.wait()
    copies[0].wait()
    for number, out_ref in enumerate(outs):
        here = slice(number * piece, (number + 1) * piece)
        total = d_attn[here, :].astype(F32)
        for index in range(3):
            total += dot(factors[2 * index][here, :], factors[2 * index + 1][...], NT)
        out_ref[...] = total.astype(BF16)


def input_grad(d_attn, factors, held):
    tokens, width = d_attn.shape
    anywhere = pl.BlockSpec(memory_space=pl.ANY)
    values = [d_attn] + [value for pair in factors for value in pair]
    return pl.pallas_call(
        functools.partial(input_grad_kernel, held=held),
        in_specs=[anywhere] * 7,
        out_specs=[pl.BlockSpec(memory_space=pltpu.VMEM)] * held,
        out_shape=shapes(*[((tokens // held, width), BF16)] * held),
        scratch_shapes=[pltpu.VMEM(value.shape, BF16) for value in values]
        + [pltpu.SemaphoreType.DMA((7,))],
        compiler_params=pltpu.CompilerParams(vmem_limit_bytes=24 * 2**20),
        cost_estimate=BRIEF,
        name="input_grad",
    )(*map(in_hbm, values))


def feed_out_kernel(which_ref, half_ref, *refs, steps):
    del which_ref
    shrink_ref, expand_ref = refs[-2:]

    @pl.when(pl.program_id(0) < steps)
    def _():
        shrink_ref[...] = half_ref[...].astype(F32)

    @pl.when(pl.program_id(0) >= steps)
    def _():
        expand_ref[...] = half_ref[...].T.astype(F32)


def feed_out(which, values, before=(), block=512):
    width = values.shape[1]
    half = values.shape[0] // 2
    steps = half // block
    return pl.pallas_call(
        functools.partial(feed_out_kernel, steps=steps),
        grid_spec=pltpu.PrefetchScalarGridSpec(
            num_scalar_prefetch=1,
            grid=(2 * steps,),
            in_specs=[pl.BlockSpec((block, width), lambda i, which: (i, 0))]
            + [pl.BlockSpec(memory_space=pl.ANY)] * len(before),
            out_specs=[
                pl.BlockSpec(
                    (block, width),
                    lambda i, which: (which[0] * steps + jnp.minimum(i, steps - 1), 0),
                ),
                pl.BlockSpec(
                    (width, block),
                    lambda i, which: (0, which[0] * steps + jnp.maximum(i - steps, 0)),
                ),
            ],
        ),
        out_shape=shapes(((2 * half, width), F32), ((width, 2 * half), F32)),
        input_output_aliases={2 + i: i for i in range(len(before))},
        compiler_params=pltpu.CompilerParams(vmem_limit_bytes=16 * 2**20),
        cost_estimate=BRIEF,
        name="feed_out",
    )(which, values, *before)


def attn_out_kernel(which_ref, half_ref, *refs):
    del which_ref
    for index, out_ref in enumerate(refs[-4:]):

        @pl.when(pl.program_id(0) == index)
        def _(out_ref=out_ref):
            out_ref[...] = half_ref[...].astype(F32)


def attn_out(which, values, before=()):
    width = values.shape[1]
    half = width // 2
    return pl.pallas_call(
        attn_out_kernel,
        grid_spec=pltpu.PrefetchScalarGridSpec(
            num_scalar_prefetch=1,
            grid=(4,),
            in_specs=[pl.BlockSpec((half, width), lambda i, which: (i, 0))]
            + [pl.BlockSpec(memory_space=pl.ANY)] * len(before),
            out_specs=[pl.BlockSpec((half, width), lambda i, which: (which[0], 0))] * 4,
        ),
        out_shape=shapes(*[((width, width), F32)] * 4),
        input_output_aliases={2 + i: i for i in range(len(before))},
        compiler_params=pltpu.CompilerParams(vmem_limit_bytes=24 * 2**20),
        cost_estimate=BRIEF,
        name="attn_out",
    )(which, values, *before)


def place_kernel(at_ref, *refs):
    del at_ref
    out_ref = refs[-1]
    for index, ref in enumerate(refs[:-1]):

        @pl.when(pl.program_id(0) == index)
        def _(ref=ref):
            out_ref[0] = ref[...]


def place(at, parts):
    piece, width = parts[0].shape
    held = len(parts)
    return pl.pallas_call(
        place_kernel,
        grid_spec=pltpu.PrefetchScalarGridSpec(
            num_scalar_prefetch=1,
            grid=(held,),
            in_specs=[pl.BlockSpec((piece, width), lambda i, at: (0, 0))] * held,
            out_specs=pl.BlockSpec((1, piece, width), lambda i, at: (at[0] ^ i, 0, 0)),
        ),
        out_shape=jax.ShapeDtypeStruct((held, piece, width), BF16),
        compiler_params=pltpu.CompilerParams(vmem_limit_bytes=16 * 2**20),
        cost_estimate=BRIEF,
        name="place",
    )(at, *parts)


def rows_of(ref, which, count, base=0):
    return ref[pl.ds(pl.multiple_of(base + which * count, 16), count), :]


def sum_of(terms):
    return functools.reduce(lambda a, b: a + b, [t.astype(F32) for t in terms]).astype(BF16)


def scatter_kernel(bits_ref, *refs, groups):
    outs = refs[-2 * groups :]
    ins = refs[: -2 * groups]
    together = len(ins) == 2
    base = 0
    for group in range(groups):
        terms = ins if together else ins[2 * group : 2 * group + 2]
        sent_ref, kept_ref = outs[2 * group : 2 * group + 2]
        count = kept_ref.shape[0]
        here = bits_ref[group]
        sent_ref[...] = sum_of([rows_of(term, 1 - here, count, base) for term in terms])
        kept_ref[...] = sum_of([rows_of(term, here, count, base) for term in terms])
        if together:
            base += 2 * count


def local_call(kernel, bits, values, out_shape, name):
    vmem = pl.BlockSpec(memory_space=pltpu.VMEM)
    return pl.pallas_call(
        kernel,
        in_specs=[pl.BlockSpec(memory_space=pltpu.SMEM)] + [vmem] * len(values),
        out_specs=[vmem] * len(out_shape),
        out_shape=out_shape,
        compiler_params=pltpu.CompilerParams(vmem_limit_bytes=24 * 2**20),
        cost_estimate=BRIEF,
        name=name,
    )(bits, *values)


def scatter_local(bits, pairs, counts=None):
    if counts is None:
        counts = [kept.shape[0] for kept, _ in pairs]
    groups = len(counts)
    counts = [count // 2 for count in counts]
    width = pairs[0][0].shape[1]
    outs = local_call(
        functools.partial(scatter_kernel, groups=groups),
        bits,
        [value for pair in pairs for value in pair],
        shapes(*[((count, width), BF16) for count in counts for _ in range(2)]),
        "scatter_local",
    )
    return [outs[2 * i : 2 * i + 2] for i in range(groups)]


def scatter_first_kernel(bits_ref, own_at, got_at, *refs, counts):
    outs, (own, got, sems) = refs[:-3], refs[-3:]
    spans = []
    base = 0
    for group, count in enumerate(counts):
        for kept in range(2):
            half = bits_ref[group] if kept else 1 - bits_ref[group]
            start = pl.multiple_of(base + half * (count // 2), 16)
            spans.append((start, count // 2, outs[2 * group + kept]))
        base += count
    spans = spans[0::2] + spans[1::2]
    copies = []
    for index, (start, count, _) in enumerate(spans):
        rows = pl.ds(start, count)
        for which, (source, target) in enumerate(((own_at, own), (got_at, got))):
            copies.append(
                pltpu.make_async_copy(source.at[rows], target.at[rows], sems.at[2 * index + which])
            )
            copies[-1].start()
    for index, (start, count, out_ref) in enumerate(spans):
        for copy in copies[2 * index : 2 * index + 2]:
            copy.wait()
        rows = pl.ds(start, count)
        out_ref[...] = sum_of([own[rows, :], got[rows, :]])


def scatter_first(bits, own, got, counts):
    rows, width = own.shape
    anywhere = pl.BlockSpec(memory_space=pl.ANY)
    vmem = pl.BlockSpec(memory_space=pltpu.VMEM)
    outs = pl.pallas_call(
        functools.partial(scatter_first_kernel, counts=counts),
        in_specs=[pl.BlockSpec(memory_space=pltpu.SMEM), anywhere, anywhere],
        out_specs=[vmem] * (2 * len(counts)),
        out_shape=shapes(*[((count // 2, width), BF16) for count in counts for _ in range(2)]),
        scratch_shapes=[pltpu.VMEM((rows, width), BF16)] * 2
        + [pltpu.SemaphoreType.DMA((4 * len(counts),))],
        compiler_params=pltpu.CompilerParams(vmem_limit_bytes=24 * 2**20),
        cost_estimate=BRIEF,
        name="scatter_first",
    )(bits, in_hbm(own), in_hbm(got))
    return [outs[2 * group : 2 * group + 2] for group in range(len(counts))]


SMALL = 16


def put_small(ref, at, values):
    ref[at : at + SMALL, :] = values.astype(BF16)


def get_small(ref, at):
    return ref[at : at + SMALL, :].astype(F32)


def settle_kernel(bits_ref, *refs, groups, small):
    del bits_ref
    ins, outs = refs[: 2 * groups], refs[2 * groups + small :]
    for group in range(groups):
        count = ins[2 * group].shape[0]
        outs[group][0:count, :] = sum_of([ins[2 * group][...], ins[2 * group + 1][...]])
        if small and group == 0:
            put_small(outs[group], count, refs[2 * groups][...])


def settle_local(bits, pairs, small):
    width = pairs[0][0].shape[1]
    counts = [kept.shape[0] for kept, _ in pairs]
    if small is not None:
        counts[0] += SMALL
    return local_call(
        functools.partial(settle_kernel, groups=len(pairs), small=int(small is not None)),
        bits,
        [value for pair in pairs for value in pair] + ([] if small is None else [small]),
        shapes(*[((count, width), BF16) for count in counts]),
        "settle_local",
    )


def add_kernel(bits_ref, *refs, groups, small):
    del bits_ref
    ins, outs = refs[: 2 * groups], refs[2 * groups :]
    for group in range(groups):
        own_ref, got_ref = ins[2 * group : 2 * group + 2]
        extra = SMALL if small and group == 0 else 0
        count = own_ref.shape[0] - extra
        outs[group][0:count, :] = sum_of([own_ref[0:count, :], got_ref[0:count, :]])
        if extra:
            put_small(outs[group], count, get_small(own_ref, count) + get_small(got_ref, count))


def add_local(bits, pairs, small):
    return local_call(
        functools.partial(add_kernel, groups=len(pairs), small=small),
        bits,
        [value for pair in pairs for value in pair],
        shapes(*[(own.shape, BF16) for own, _ in pairs]),
        "add_local",
    )


def join_kernel(bits_ref, *refs, groups, small, merged, pieces):
    ins, outs = refs[: 2 * pieces * groups], list(refs[2 * pieces * groups :])
    parts = len(outs) // groups
    base = 0
    for group in range(groups):
        owns = ins[2 * pieces * group : 2 * pieces * group + 2 * pieces : 2]
        gots = ins[2 * pieces * group + 1 : 2 * pieces * group + 2 * pieces : 2]
        extra = SMALL if small and group == 0 else 0
        count = owns[0].shape[0] - extra
        here = bits_ref[group]
        if parts > 1:
            for half, out_ref in enumerate(outs[2 * group : 2 * group + 2]):

                @pl.when(here == half)
                def _(out_ref=out_ref):
                    out_ref[...] = owns[0][...]

                @pl.when(here != half)
                def _(out_ref=out_ref):
                    out_ref[...] = gots[0][...]

            continue
        out_ref = outs[0 if merged else group]
        whole = count * pieces
        for half, refs_of in ((here, owns), (1 - here, gots)):
            for index, ref in enumerate(refs_of):
                start = pl.multiple_of(base + half * whole + index * count, 16)
                out_ref[pl.ds(start, count), :] = ref[0:count, :]
        if extra:
            at = out_ref.shape[0] - SMALL if merged else base + 2 * whole
            put_small(out_ref, at, get_small(owns[0], count) + get_small(gots[0], count))
        if merged:
            base += 2 * whole


def join_local(bits, arrived, small, merged, parts=1):
    width = arrived[0][0].shape[1]
    pieces = len(arrived[0]) // 2
    counts = [2 * pieces * group[0].shape[0] for group in arrived]
    if small:
        counts[0] -= SMALL
    if merged:
        counts = [sum(counts)]
    counts = [count // parts for count in counts for _ in range(parts)]
    return local_call(
        functools.partial(
            join_kernel, groups=len(arrived), small=small, merged=merged, pieces=pieces
        ),
        bits,
        [value for group in arrived for value in group],
        shapes(*[((count, width), BF16) for count in counts]),
        "join_local",
    )


def tie(*values):
    return lax.optimization_barrier(values)


def pick(which, parts):
    if len(parts) == 1:
        return parts[0]
    half = len(parts) // 2
    return jnp.where(which < half, pick(which, parts[:half]), pick(which - half, parts[half:]))


def column_sum(values):
    return jnp.sum(values.astype(F32), 0)


class Stage:
    def __init__(self, sizes, bits):
        self.bits = bits
        rows, seq = sizes
        self.pairs = []
        for index in range(rows * seq):
            axis, bit = bits[index & 1]
            self.pairs.append((index, index ^ ((1 << bit) * (seq if axis == "rows" else 1))))

    def here(self):
        first, second = [(lax.axis_index(axis) >> bit) & 1 for axis, bit in self.bits]
        if self.bits[0] == self.bits[1]:
            return first
        return jnp.where(lax.axis_index("seq") & 1 == 0, first, second)

    def swap(self, values):
        return lax.ppermute(values, ("rows", "seq"), self.pairs)


def total_over_chips(own, got, core_stage, orders, small=None, near=False):
    depth = len(orders[0][1])
    groups = range(len(orders))

    def bits_at(step):
        return jnp.stack([stages[step].here() for _, stages in orders]).astype(jnp.int32)

    def pairs_of(flat):
        return [flat[i : i + 2] for i in range(0, len(flat), 2)]

    def send(step, values, keep):
        flat = []
        for group in groups:
            flat += [keep[group], orders[group][1][step].swap(values[group])]
        return flat

    counts = [count for count, _ in orders]
    if near:
        parts = scatter_local(bits_at(0), [[own, got]], counts)
    else:
        parts = scatter_first(bits_at(0), own, got, counts)
    last = depth - 1 if near else depth
    for step in range(1, last + 1):
        flat = yield send(step - 1, [p[0] for p in parts], [p[1] for p in parts])
        if step < last:
            parts = scatter_local(bits_at(step), pairs_of(flat))
    values = settle_local(bits_at(0), pairs_of(flat), small)
    if near:
        flat = yield send(last, values, values)
        values = add_local(bits_at(0), pairs_of(flat), small is not None)
    carried = small is not None
    for step in reversed(range(last)):
        flat = yield send(step, values, values)
        parts = 2 if step == 1 and not carried else 1
        values = join_local(bits_at(step), pairs_of(flat), carried, step == 0, parts)
        if parts > 1:
            lower = yield send(0, values[0::2], values[0::2])
            upper = yield send(0, values[1::2], values[1::2])
            arrived = [list(low) + list(high) for low, high in zip(pairs_of(lower), pairs_of(upper))]
            values = join_local(bits_at(0), arrived, carried, True)
            break
    both = yield [values[0], core_stage.swap(values[0])]
    return both


def arriving(values):
    values = yield values
    return values[1::2]


class Flow:
    def __init__(self, steps, left):
        self.steps = steps
        self.left = left
        self.pending = next(steps)
        self.result = None


class Timetable:
    def __init__(self):
        self.flows = []

    def open(self, steps, left=1):
        self.flows.append(Flow(steps, left))
        return self.flows[-1]

    def advance(self, moving, *values):
        flows = [flow for flow in self.flows if flow.result is None]
        held = [flow.pending if flow in moving else flow.pending[0::2] for flow in flows]
        tied = list(tie(*values, *[value for part in held for value in part]))
        values, tied = tied[: len(values)], tied[len(values) :]
        for flow, part in zip(flows, held):
            back, tied = tied[: len(part)], tied[len(part) :]
            if flow not in moving:
                flow.pending[0::2] = back
                continue
            flow.left -= 1
            try:
                flow.pending = flow.steps.send(back)
            except StopIteration as end:
                flow.result = end.value
        return self.settle(*values) if moving and values else values

    def settle(self, *values):
        return self.advance([], *values)


def solution(mesh):
    seq_size = mesh.shape["seq"]
    rows_size = mesh.shape["rows"]
    seq_bits = seq_size.bit_length() - 1
    rows_bits = rows_size.bit_length() - 1
    off_chip = [("seq", bit) for bit in range(1, seq_bits)]
    off_chip += [("rows", bit) for bit in range(rows_bits)]
    first, *middle, ahead, final = off_chip
    sizes = (rows_size, seq_size)
    core_stage = Stage(sizes, [("seq", 0)] * 2)
    straight = [first] + middle + [ahead, final]
    turned = middle + [ahead, first, final]
    spun = [ahead, first] + middle + [final]
    wide = [Stage(sizes, bits) for bits in zip(straight, turned)]
    slim = [Stage(sizes, bits) for bits in zip(spun, spun)]

    def body(
        hidden_in,
        segments,
        grad_mask,
        grad_out,
        query_proj,
        query_bias,
        key_proj,
        value_proj,
        value_bias,
        output_proj,
        output_bias,
        first_gain,
        first_shift,
        expand_proj,
        expand_bias,
        shrink_proj,
        shrink_bias,
        second_gain,
        second_shift,
    ):
        micro, rows_here, piece, width = hidden_in.shape
        held = micro * rows_here
        sharers = seq_size // held
        tokens = held * piece
        source_at = lax.axis_index("seq") % held
        core = core_stage.here()
        core_at = core.reshape(1).astype(jnp.int32)

        def trade(to_rows, part):
            there = [(s, (s % held ^ part) * sharers + s // held) for s in range(seq_size)]
            return there if to_rows else [(b, a) for a, b in there]

        def to_rows(values):
            return [
                lax.ppermute(
                    lax.dynamic_index_in_dim(values, source_at ^ part, 0, False),
                    "seq",
                    trade(True, part),
                )
                for part in range(held)
            ]

        def send_pieces(values):
            return [
                value
                for part in range(held)
                for value in (values[part], lax.ppermute(values[part], "seq", trade(False, part)))
            ]

        def place_pieces(parts):
            at = source_at.reshape(1).astype(jnp.int32)
            return place(at, parts).reshape((micro, rows_here) + parts[0].shape)

        same_row = [[r * sharers + g for g in range(sharers)] for r in range(held)]

        def all_keys(values):
            if sharers == 1:
                return values
            return lax.all_gather(values, "seq", axis=0, tiled=True, axis_index_groups=same_row)

        def own_keys(values):
            if sharers == 1:
                return values
            return lax.psum_scatter(
                values, "seq", scatter_dimension=0, tiled=True, axis_index_groups=same_row
            ).astype(BF16)

        order = tuple(reversed(range(held)))
        packed = pack(
            source_at.reshape(1).astype(jnp.int32),
            hidden_in.reshape(held, piece, width),
            segments.reshape(held, piece),
            order,
        )
        arrived = [
            lax.ppermute(value, "seq", trade(True, part)) for part, value in zip(order, packed)
        ]
        inputs, seg_q = unpack(arrived[::-1])
        masked = (grad_out * grad_mask[..., None].astype(BF16)).reshape(held, piece, width)
        masked, inputs, seg_q = tie(masked, inputs, seg_q)
        upstream = to_rows(masked)

        queries = (
            (dot(inputs, query_proj) + query_bias.astype(F32)) * 0.125
        ).astype(BF16)
        keys = all_keys(dot(inputs, key_proj).astype(BF16))
        values = all_keys((dot(inputs, value_proj) + value_bias.astype(F32)).astype(BF16))
        seg_k = all_keys(seg_q)
        mixed, query_side = attention_forward(queries, keys, values, seg_q, seg_k)
        row = lambda vector: vector.reshape(1, -1)
        hat, scale, normed, active_t, slope, d_down, second_sums, *result = feed_forward(
            inputs,
            mixed,
            upstream,
            (
                output_proj,
                row(output_bias),
                row(first_gain),
                row(first_shift),
                expand_proj,
                row(expand_bias),
                shrink_proj,
                row(shrink_bias),
                row(second_gain),
                row(second_shift),
            ),
        )
        table = Timetable()
        advance = table.advance
        layer_flow = table.open(arriving(send_pieces(result)))

        def chips(own, got, orders, small=None):
            near = small is not None
            steps = total_over_chips(own, got, core_stage, orders, small, near)
            return table.open(steps, 2 * len(wide) + (0 if near else 2))

        back = functools.partial(
            feed_back,
            slope=slope,
            active_t=active_t,
            shrink=shrink_proj,
            expand=expand_proj,
            normed=normed,
        )
        other, other_bias, d_normed = back(1 - core_at, d_down, norm=None)
        half = other.shape[1]
        got = core_stage.swap(other.reshape(2 * half, width))
        own, own_bias, d_attn, d_mixed, first_sums = back(
            core_at, d_down, norm=(row(first_gain), d_normed, hat, scale, output_proj)
        )
        own, got, d_mixed = advance([layer_flow], own.reshape(2 * half, width), got, d_mixed)
        unit = 16 << len(off_chip)

        def thirds(count):
            less = count // unit // 3 * unit
            return [(count - less, wide)] + ([(less, slim)] if less else [])

        feed_flow = chips(own, got, thirds(2 * half))

        pairs = width // PAIR
        kept = BF16 if sharers == 1 else F32
        grads = None
        for first, last in ((0, pairs),):
            grads = attention_backward(
                query_side, keys, values, seg_k, mixed, d_mixed, kept, first, last - first, grads
            )
            *grads, d_mixed = advance([feed_flow], *grads, d_mixed)

        d_query, d_keys, d_values = grads
        d_key = own_keys(d_keys)
        d_value = own_keys(d_values)
        steps = half // other_bias.shape[1]
        other, own, small = weight_halves(
            core_at,
            (inputs, d_query, d_key, d_value, mixed, d_attn),
            unit,
            (first_sums, second_sums, own_bias, other_bias),
            steps,
        )
        other, own, small, d_query, d_key, d_value = advance(
            [feed_flow], other, own, small, d_query, d_key, d_value
        )
        got = core_stage.swap(other)
        d_input = input_grad(
            d_attn, ((d_query, query_proj), (d_key, key_proj), (d_value, value_proj)), held
        )
        own, got, small, *d_input = advance([feed_flow], own, got, small, *d_input)
        attn_flow = chips(own, got, [(own.shape[0], wide)], small)
        piece_flow = table.open(arriving(send_pieces(d_input)))

        both = [feed_flow, attn_flow]
        layer_out = place_pieces(list(map(in_hbm, layer_flow.result)))
        (layer_out,) = advance(both, layer_out)
        advance(both + [piece_flow])
        grad_in = place_pieces(piece_flow.result)
        (grad_in,) = advance(both, grad_in)
        while feed_flow.left > 1:
            advance(both)
        feed_grads = feed_out(core_at, feed_flow.pending[0])
        feed_grads = advance(both, *feed_grads)
        feed_grads = feed_out(1 - core_at, feed_flow.result[1], feed_grads)
        while attn_flow.left > 1:
            feed_grads = advance([attn_flow], *feed_grads)
        attn_grads = attn_out(core_at, attn_flow.pending[0])
        attn_grads = advance([attn_flow], *attn_grads)
        own, got = attn_flow.result
        attn_grads = attn_out(1 - core_at, got, attn_grads)
        totals = own[-SMALL:].astype(F32) + got[-SMALL:].astype(F32)
        shrink_grad, expand_grad = feed_grads
        expand_bias_grad = totals[8 : 8 + 2 * steps, : other_bias.shape[1]].reshape(-1)
        return (
            layer_out,
            grad_in,
            attn_grads[0],
            totals[0],
            attn_grads[1],
            attn_grads[2],
            totals[1],
            attn_grads[3],
            totals[4],
            totals[2],
            totals[3],
            expand_grad,
            expand_bias_grad,
            shrink_grad,
            totals[7],
            totals[5],
            totals[6],
        )

    split = P(None, "rows", "seq", None)
    whole = P()
    return jax.shard_map(
        body,
        mesh=mesh,
        in_specs=(split, P(None, "rows", "seq"), P(None, "rows", "seq"), split) + (whole,) * 15,
        out_specs=(split, split) + (whole,) * 15,
        check_vma=False,
    )
```

profile of v0, /device:TPU:0, one launch (start us, length us, event | category | flops | bytes accessed | tf_op | source)
XLA Modules:
  0.0 316.5 jit_solution(12708593569380838251)
XLA Ops:
  11.9 4.6 %collective-permute-done.2.refs_2_ = bf16[272,768]{1,0:T(8,128)(2,1)S(1)} collective-permute-done((bf16[272,768]{1,0:T(8,128)(2,1)S(1)}, bf16[272,768]{1,0:T(8,128)(2,1)S(1)}, u32[]{:S(2)}, u32[]{:S(2)}) %collective-permute-start.2) | collective-permute-done | bytes 417824 | tf_op jit(solution)/shard_map/ppermute | solution.py:1209
  16.5 8.4 %collective-permute-done.3.refs_3_ = bf16[272,768]{1,0:T(8,128)(2,1)S(1)} collective-permute-done((bf16[272,768]{1,0:T(8,128)(2,1)S(1)}, bf16[272,768]{1,0:T(8,128)(2,1)S(1)}, u32[]{:S(2)}, u32[]{:S(2)}) %collective-permute-start.3) | collective-permute-done | bytes 417824 | tf_op jit(solution)/shard_map/ppermute | solution.py:1209
  32.8 22.4 %attention_forward.1 = (bf16[1024,768]{1,0:T(8,128)(2,1)}, bf16[12,1024,128]{2,1,0:T(8,128)(2,1)}) custom-call(bf16[1024,768]{1,0:T(8,128)(2,1)S(1)} %multiply_convert_fusion.q_ref, bf16[1024,768]{1,0:T(8,128)(2,1)S(1)} %convolution_convert_fusion.k_ref, bf16[1024,768]{1,0:T(8,128)(2,1)S(1)} %add_convert_fusion.v_ref, bf16[1024,128]{1,0:T(8,128)(2,1)S(1)} %copy-done.3, ...), custom_call_target="tpu_custom_call" | custom-call | flops 1 | bytes 1 | tf_op jit(solution)/shard_map/attention_forward/pallas_call | solution.py:90
  55.2 23.5 %feed_forward.1 = (bf16[1024,768]{1,0:T(8,128)(2,1)}, f32[1024,128]{1,0:T(8,128)}, bf16[1024,768]{1,0:T(8,128)(2,1)}, bf16[3072,1024]{1,0:T(8,128)(2,1)}, bf16[1...) custom-call(bf16[1024,768]{1,0:T(8,128)(2,1)S(1)} %copy-done, ...), custom_call_target="tpu_custom_call" | custom-call | flops 1 | bytes 1 | tf_op jit(solution)/shard_map/feed_forward/pallas_call | solution.py:327
  78.7 16.7 %feed_back.1 = (bf16[2,1536,768]{2,1,0:T(8,128)(2,1)}, f32[8,512]{1,0:T(8,128)}, bf16[1024,768]{1,0:T(8,128)(2,1)}) custom-call(s32[1]{0:T(128)S(6)} %sub.2.which_ref, bf16[1024,768]{1,0:T(8,128)(2,1)} %get-tuple-element.239.d_down_ref, bf16[1024,3072]{1,0:T(8,128)(2,1)} %get-tuple-element.240.slope_ref, bf16[3072,1024]{1,0:T(8,128)(2,1)} %get-tuple-element.241.active_t_ref, ...), custom_call_target="tpu_custom_call" | custom-call | flops 1 | bytes 1 | tf_op jit(solution)/shard_map/feed_back/pallas_call | solution.py:496
  98.8 19.7 %feed_back_last.1 = (bf16[2,1536,768]{2,1,0:T(8,128)(2,1)}, f32[8,512]{1,0:T(8,128)}, bf16[1024,768]{1,0:T(8,128)(2,1)}, bf16[1024,768]{1,0:T(8,128)(2,1)}, f32[8,768]{1,0:T(8,128)}) custom-call(s32[1]{0:T(128)} %bitcast.1.which_ref.core_ref, bf16[1024,768]{1,0:T(8,128)(2,1)} %get-tuple-element.239.d_down_ref, ...), custom_call_target="tpu_custom_call" | custom-call | flops 1 | bytes 1 | tf_op jit(solution)/shard_map/feed_back_last/pallas_call | solution.py:496
  118.7 4.9 %scatter_first.1 = (bf16[1024,768]{1,0:T(8,128)(2,1)S(1)}, bf16[1024,768]{1,0:T(8,128)(2,1)S(1)}, bf16[512,768]{1,0:T(8,128)(2,1)S(1)}, bf16[512,768]{1,0:T(8,128)(2,1)S(1)}) custom-call(s32[2]{0:T(128)S(1)} %get-tuple-element.453.bits_ref, bf16[3072,768]{1,0:T(8,128)(2,1)} %bitcast.30, bf16[3072,768]{1,0:T(8,128)(2,1)} %collective-permute-done.8.got_at), custom_call_target="tpu_custom_call" | custom-call | flops 1 | bytes 1 | tf_op jit(solution)/shard_map/scatter_first/pallas_call | solution.py:870
  126.9 36.0 %attention_backward.1 = (bf16[1024,768]{1,0:T(8,128)(2,1)}, bf16[1024,768]{1,0:T(8,128)(2,1)}, bf16[1024,768]{1,0:T(8,128)(2,1)}) custom-call(bf16[12,1024,128]{2,1,0:T(8,128)(2,1)} %get-tuple-element.261.query_ref, bf16[1024,768]{1,0:T(8,128)(2,1)S(1)} %convolution_convert_fusion.k_ref, bf16[1024,768]{1,0:T(8,128)(2,1)S(1)} %copy-done.2, ...), custom_call_target="tpu_custom_call" | custom-call | flops 1 | bytes 1 | tf_op jit(solution)/shard_map/attention_backward/pallas_call | solution.py:168
  166.9 8.0 %weight_halves.1 = (bf16[1536,768]{1,0:T(8,128)(2,1)S(1)}, bf16[1536,768]{1,0:T(8,128)(2,1)S(1)}, f32[16,768]{1,0:T(8,128)S(1)}) custom-call(s32[1]{0:T(128)} %bitcast.1.which_ref.core_ref, f32[8,768]{1,0:T(8,128)S(1)} %copy-done.6, f32[8,768]{1,0:T(8,128)S(1)} %copy-done.5, f32[8,512]{1,0:T(8,128)S(1)} %copy-done.8, f32[8,512]{1,0:T(8,128)S(1)} %copy-done.7, ...), custom_call_target="tpu_custom_call" | custom-call | flops 1 | bytes 1 | tf_op jit(solution)/shard_map/weight_halves/pallas_call | solution.py:631
  179.7 7.8 %input_grad.1 = (bf16[256,768]{1,0:T(8,128)(2,1)S(1)}, bf16[256,768]{1,0:T(8,128)(2,1)S(1)}, bf16[256,768]{1,0:T(8,128)(2,1)S(1)}, bf16[256,768]{1,0:T(8,128)(2,1)S(1)}) custom-call(bf16[1024,768]{1,0:T(8,128)(2,1)} %get-tuple-element.287.refs_5_.refs_0_, bf16[1024,768]{1,0:T(8,128)(2,1)} %get-tuple-element.310.refs_1_, bf16[768,768]{1,0:T(8,128)(2,1)} %refs_2_.1, ...), custom_call_target="tpu_custom_call" | custom-call | flops 1 | bytes 1 | tf_op jit(solution)/shard_map/input_grad/pallas_call | solution.py:674
  192.5 3.0 place.2
  195.6 9.7 %collective-permute-done.21.refs_3_ = bf16[64,768]{1,0:T(8,128)(2,1)S(1)} collective-permute-done((bf16[64,768]{1,0:T(8,128)(2,1)S(1)}, bf16[64,768]{1,0:T(8,128)(2,1)S(1)}, u32[]{:S(2)}, u32[]{:S(2)}) %collective-permute-start.21) | collective-permute-done | bytes 98336 | tf_op jit(solution)/shard_map/ppermute | solution.py:1027
  212.4 6.4 %collective-permute-done.28.refs_2_ = bf16[256,768]{1,0:T(8,128)(2,1)S(1)} collective-permute-done((bf16[256,768]{1,0:T(8,128)(2,1)S(1)}, bf16[256,768]{1,0:T(8,128)(2,1)S(1)}, u32[]{:S(2)}, u32[]{:S(2)}) %collective-permute-start.28) | collective-permute-done | bytes 393248 | tf_op jit(solution)/shard_map/ppermute | solution.py:1180
  218.9 7.7 %collective-permute-done.29.refs_3_ = bf16[256,768]{1,0:T(8,128)(2,1)S(1)} collective-permute-done((bf16[256,768]{1,0:T(8,128)(2,1)S(1)}, bf16[256,768]{1,0:T(8,128)(2,1)S(1)}, u32[]{:S(2)}, u32[]{:S(2)}) %collective-permute-start.29) | collective-permute-done | bytes 393248 | tf_op jit(solution)/shard_map/ppermute | solution.py:1180
  231.8 4.1 %collective-permute-done.31.refs_3_ = bf16[128,768]{1,0:T(8,128)(2,1)S(1)} collective-permute-done((bf16[128,768]{1,0:T(8,128)(2,1)S(1)}, bf16[128,768]{1,0:T(8,128)(2,1)S(1)}, u32[]{:S(2)}, u32[]{:S(2)}) %collective-permute-start.31) | collective-permute-done | bytes 196640 | tf_op jit(solution)/shard_map/ppermute | solution.py:1027
  242.7 10.8 %collective-permute-done.35.refs_1_ = bf16[208,768]{1,0:T(8,128)(2,1)S(1)} collective-permute-done((bf16[208,768]{1,0:T(8,128)(2,1)S(1)}, bf16[208,768]{1,0:T(8,128)(2,1)S(1)}, u32[]{:S(2)}, u32[]{:S(2)}) %collective-permute-start.35) | collective-permute-done | bytes 319520 | tf_op jit(solution)/shard_map/ppermute | solution.py:1027
  255.3 3.3 %collective-permute-start.37 = (bf16[256,768]{1,0:T(8,128)(2,1)S(1)}, bf16[256,768]{1,0:T(8,128)(2,1)S(1)}, u32[]{:S(2)}, u32[]{:S(2)}) collective-permute-start(bf16[256,768]{1,0:T(8,128)(2,1)S(1)} %get-tuple-element.405.refs_4_), channel_id=1, source_target_pairs={{0,8},{1,9},{2,10},{3,11},{4,12},{5,13},{6,14},{7,15},{8,0},{9,1},... | collective-permute-start | bytes 1179656 | tf_op jit(solution)/shard_map/ppermute | solution.py:1027
  260.2 11.9 %collective-permute-done.38.refs_1_ = bf16[208,768]{1,0:T(8,128)(2,1)S(1)} collective-permute-done((bf16[208,768]{1,0:T(8,128)(2,1)S(1)}, bf16[208,768]{1,0:T(8,128)(2,1)S(1)}, u32[]{:S(2)}, u32[]{:S(2)}) %collective-permute-start.38) | collective-permute-done | bytes 319520 | tf_op jit(solution)/shard_map/ppermute | solution.py:1027
  275.8 10.0 %collective-permute-done.40.refs_7_ = bf16[256,768]{1,0:T(8,128)(2,1)S(1)} collective-permute-done((bf16[256,768]{1,0:T(8,128)(2,1)S(1)}, bf16[256,768]{1,0:T(8,128)(2,1)S(1)}, u32[]{:S(2)}, u32[]{:S(2)}) %collective-permute-start.40) | collective-permute-done | bytes 393248 | tf_op jit(solution)/shard_map/ppermute | solution.py:1027
  289.0 5.2 %feed_out.2 = (f32[3072,768]{1,0:T(8,128)}, f32[768,3072]{1,0:T(8,128)}) custom-call(s32[1]{0:T(128)} %bitcast.1.which_ref.core_ref, bf16[3072,768]{1,0:T(8,128)(2,1)S(1)} %join_local.11.half_ref), custom_call_target="tpu_custom_call" | custom-call | flops 1 | bytes 1 | tf_op jit(solution)/shard_map/feed_out/pallas_call | solution.py:704
  294.1 10.2 %collective-permute-done.43.refs_1_ = bf16[784,768]{1,0:T(8,128)(2,1)S(1)} collective-permute-done((bf16[784,768]{1,0:T(8,128)(2,1)S(1)}, bf16[784,768]{1,0:T(8,128)(2,1)S(1)}, u32[]{:S(2)}, u32[]{:S(2)}) %collective-permute-start.43) | collective-permute-done | bytes 1204256 | tf_op jit(solution)/shard_map/ppermute | solution.py:1027
  304.6 2.6 attn_out.2
  307.3 5.1 %feed_out.3 = (f32[3072,768]{1,0:T(8,128)}, f32[768,3072]{1,0:T(8,128)}) custom-call(s32[1]{0:T(128)S(6)} %sub.2.which_ref, bf16[3072,768]{1,0:T(8,128)(2,1)S(1)} %collective-permute-done.42.half_ref, f32[3072,768]{1,0:T(8,128)} %get-tuple-element.437.refs_0_, f32[768,3072]{1,0:T(8,128)} %get-tuple-element.438.refs_1_), custom_call_target="tpu_custom_call", output_to_operand_aliasing={{0}: (2, {}), {1}: (3, {})} | custom-call | flops 1 | bytes 1 | tf_op jit(solution)/shard_map/feed_out/pallas_call | solution.py:704
  313.7 2.6 attn_out.3
  (172 shorter events, 70.1 us)
Async XLA Ops:
  6.0 18.9 %collective-permute-start.3 = (bf16[272,768]{1,0:T(8,128)(2,1)S(1)}, bf16[272,768]{1,0:T(8,128)(2,1)S(1)}, u32[]{:S(2)}, u32[]{:S(2)}) collective-permute-start(bf16[272,768]{1,0:T(8,128)(2,1)S(1)} %get-tuple-element.232), channel_id=1, source_target_pairs={{0,3},{1,2},{2,1},{3,0},{4,7},{5,6},{6,5},{7,4},{8,11},{9,10},{10,... | collective-permute-start | bytes 1253384 | tf_op jit(solution)/shard_map/ppermute | solution.py:1209
  26.5 28.7 %collective-permute-start.7 = (bf16[256,768]{1,0:T(8,128)(2,1)S(1)}, bf16[256,768]{1,0:T(8,128)(2,1)S(1)}, u32[]{:S(2)}, u32[]{:S(2)}) collective-permute-start(bf16[256,768]{1,0:T(8,128)(2,1)S(1)} %get-tuple-element.449), channel_id=1, source_target_pairs={{0,3},{1,2},{2,1},{3,0},{4,7},{5,6},{6,5},{7,4},{8,11},{9,10},{10,... | collective-permute-start | bytes 1179656 | tf_op jit(solution)/shard_map/ppermute | solution.py:1168
  28.0 27.2 %collective-permute-start.6 = (bf16[256,768]{1,0:T(8,128)(2,1)S(1)}, bf16[256,768]{1,0:T(8,128)(2,1)S(1)}, u32[]{:S(2)}, u32[]{:S(2)}) collective-permute-start(bf16[256,768]{1,0:T(8,128)(2,1)S(1)} %get-tuple-element.450), channel_id=1, source_target_pairs={{0,2},{1,3},{2,0},{3,1},{4,6},{5,7},{6,4},{7,5},{8,10},{9,11},{10,... | collective-permute-start | bytes 1179656 | tf_op jit(solution)/shard_map/ppermute | solution.py:1168
  28.3 26.9 %collective-permute-start.5 = (bf16[256,768]{1,0:T(8,128)(2,1)S(1)}, bf16[256,768]{1,0:T(8,128)(2,1)S(1)}, u32[]{:S(2)}, u32[]{:S(2)}) collective-permute-start(bf16[256,768]{1,0:T(8,128)(2,1)S(1)} %get-tuple-element.451), channel_id=1, source_target_pairs={{0,1},{1,0},{2,3},{3,2},{4,5},{5,4},{6,7},{7,6},{8,9},{9,8},{10,11... | collective-permute-start | bytes 1179656 | tf_op jit(solution)/shard_map/ppermute | solution.py:1168
  28.4 26.8 %collective-permute-start.4 = (bf16[256,768]{1,0:T(8,128)(2,1)S(1)}, bf16[256,768]{1,0:T(8,128)(2,1)S(1)}, u32[]{:S(2)}, u32[]{:S(2)}) collective-permute-start(bf16[256,768]{1,0:T(8,128)(2,1)S(1)} %get-tuple-element.452), channel_id=1, source_target_pairs={{0,0},{1,1},{2,2},{3,3},{4,4},{5,5},{6,6},{7,7},{8,8},{9,9},{10,10... | collective-permute-start | bytes 1179656 | tf_op jit(solution)/shard_map/ppermute | solution.py:1168
  95.4 23.2 %collective-permute-start.8 = (bf16[3072,768]{1,0:T(8,128)(2,1)}, bf16[3072,768]{1,0:T(8,128)(2,1)}, u32[]{:S(2)}, u32[]{:S(2)}) collective-permute-start(bf16[3072,768]{1,0:T(8,128)(2,1)} %bitcast.34), channel_id=1, source_target_pairs={{0,1},{1,0},{2,3},{3,2},{4,5},{5,4},{6,7},{7,6},{8,9},{9,8},{10,11... | collective-permute-start | bytes 14155784 | tf_op jit(solution)/shard_map/ppermute | solution.py:1027
  95.8 22.7 %collective-permute-start.9 = (bf16[256,768]{1,0:T(8,128)(2,1)}, bf16[256,768]{1,0:T(8,128)(2,1)S(1)}, u32[]{:S(2)}, u32[]{:S(2)}) collective-permute-start(bf16[256,768]{1,0:T(8,128)(2,1)} %get-tuple-element.249), channel_id=1, source_target_pairs={{0,0},{1,1},{2,2},{3,3},{4,4},{5,5},{6,6},{7,7},{8,8},{9,9},{10,10... | collective-permute-start | bytes 1179656 | tf_op jit(solution)/shard_map/ppermute | solution.py:1180
  96.8 21.7 %collective-permute-start.10 = (bf16[256,768]{1,0:T(8,128)(2,1)}, bf16[256,768]{1,0:T(8,128)(2,1)S(1)}, u32[]{:S(2)}, u32[]{:S(2)}) collective-permute-start(bf16[256,768]{1,0:T(8,128)(2,1)} %get-tuple-element.250), channel_id=1, source_target_pairs={{1,0},{0,1},{3,2},{2,3},{5,4},{4,5},{7,6},{6,7},{9,8},{8,9},{11,10... | collective-permute-start | bytes 1179656 | tf_op jit(solution)/shard_map/ppermute | solution.py:1180
  97.0 21.6 %collective-permute-start.11 = (bf16[256,768]{1,0:T(8,128)(2,1)}, bf16[256,768]{1,0:T(8,128)(2,1)S(1)}, u32[]{:S(2)}, u32[]{:S(2)}) collective-permute-start(bf16[256,768]{1,0:T(8,128)(2,1)} %get-tuple-element.251), channel_id=1, source_target_pairs={{2,0},{3,1},{0,2},{1,3},{6,4},{7,5},{4,6},{5,7},{10,8},{11,9},{8,1... | collective-permute-start | bytes 1179656 | tf_op jit(solution)/shard_map/ppermute | solution.py:1180
  98.6 20.0 %collective-permute-start.12 = (bf16[256,768]{1,0:T(8,128)(2,1)}, bf16[256,768]{1,0:T(8,128)(2,1)S(1)}, u32[]{:S(2)}, u32[]{:S(2)}) collective-permute-start(bf16[256,768]{1,0:T(8,128)(2,1)} %get-tuple-element.252), channel_id=1, source_target_pairs={{3,0},{2,1},{1,2},{0,3},{7,4},{6,5},{5,6},{4,7},{11,8},{10,9},{9,1... | collective-permute-start | bytes 1179656 | tf_op jit(solution)/shard_map/ppermute | solution.py:1180
  123.6 39.3 %collective-permute-start.13 = (bf16[1024,768]{1,0:T(8,128)(2,1)S(1)}, bf16[1024,768]{1,0:T(8,128)(2,1)S(1)}, u32[]{:S(2)}, u32[]{:S(2)}) collective-permute-start(bf16[1024,768]{1,0:T(8,128)(2,1)S(1)} %get-tuple-element.272), channel_id=1, source_target_pairs={{0,2},{1,5},{2,0},{3,7},{4,6},{5,1},{6,4},{7,3},{8,10},{9,13},{10,... | collective-permute-start | bytes 4718600 | tf_op jit(solution)/shard_map/ppermute | solution.py:1027
  125.4 37.5 %collective-permute-start.14 = (bf16[512,768]{1,0:T(8,128)(2,1)S(1)}, bf16[512,768]{1,0:T(8,128)(2,1)S(1)}, u32[]{:S(2)}, u32[]{:S(2)}) collective-permute-start(bf16[512,768]{1,0:T(8,128)(2,1)S(1)} %get-tuple-element.274), channel_id=1, source_target_pairs={{0,8},{1,9},{2,10},{3,11},{4,12},{5,13},{6,14},{7,15},{8,0},{9,1},... | collective-permute-start | bytes 2359304 | tf_op jit(solution)/shard_map/ppermute | solution.py:1027
  188.7 16.5 %collective-permute-start.22 = (bf16[768,768]{1,0:T(8,128)(2,1)S(1)}, bf16[768,768]{1,0:T(8,128)(2,1)S(1)}, u32[]{:S(2)}, u32[]{:S(2)}) collective-permute-start(bf16[768,768]{1,0:T(8,128)(2,1)S(1)} %get-tuple-element.341), channel_id=1, source_target_pairs={{0,2},{1,5},{2,0},{3,7},{4,6},{5,1},{6,4},{7,3},{8,10},{9,13},{10,... | collective-permute-start | bytes 3538952 | tf_op jit(solution)/shard_map/ppermute | solution.py:1027
  189.6 15.7 %collective-permute-start.20 = (bf16[128,768]{1,0:T(8,128)(2,1)S(1)}, bf16[128,768]{1,0:T(8,128)(2,1)S(1)}, u32[]{:S(2)}, u32[]{:S(2)}) collective-permute-start(bf16[128,768]{1,0:T(8,128)(2,1)S(1)} %get-tuple-element.335), channel_id=1, source_target_pairs={{0,16},{1,17},{2,18},{3,19},{4,20},{5,21},{6,22},{7,23},{8,24},{9,... | collective-permute-start | bytes 589832 | tf_op jit(solution)/shard_map/ppermute | solution.py:1027
  205.5 21.0 %collective-permute-start.25 = (bf16[384,768]{1,0:T(8,128)(2,1)S(1)}, bf16[384,768]{1,0:T(8,128)(2,1)S(1)}, u32[]{:S(2)}, u32[]{:S(2)}) collective-permute-start(bf16[384,768]{1,0:T(8,128)(2,1)S(1)} %get-tuple-element.360), channel_id=1, source_target_pairs={{0,4},{1,9},{2,6},{3,11},{4,0},{5,13},{6,2},{7,15},{8,12},{9,1},{1... | collective-permute-start | bytes 1769480 | tf_op jit(solution)/shard_map/ppermute | solution.py:1027
  208.3 18.2 %collective-permute-start.29 = (bf16[256,768]{1,0:T(8,128)(2,1)S(1)}, bf16[256,768]{1,0:T(8,128)(2,1)S(1)}, u32[]{:S(2)}, u32[]{:S(2)}) collective-permute-start(bf16[256,768]{1,0:T(8,128)(2,1)S(1)} %get-tuple-element.345), channel_id=1, source_target_pairs={{3,0},{2,1},{1,2},{0,3},{7,4},{6,5},{5,6},{4,7},{11,8},{10,9},{9,1... | collective-permute-start | bytes 1179656 | tf_op jit(solution)/shard_map/ppermute | solution.py:1180
  209.5 17.1 %collective-permute-start.23 = (bf16[128,768]{1,0:T(8,128)(2,1)S(1)}, bf16[128,768]{1,0:T(8,128)(2,1)S(1)}, u32[]{:S(2)}, u32[]{:S(2)}) collective-permute-start(bf16[128,768]{1,0:T(8,128)(2,1)S(1)} %get-tuple-element.365.refs_0_), channel_id=1, source_target_pairs={{0,16},{1,17},{2,18},{3,19},{4,20},{5,21},{6,22},{7,23},{8,24},{9,... | collective-permute-start | bytes 589832 | tf_op jit(solution)/shard_map/ppermute | solution.py:1027
  211.4 15.1 %collective-permute-start.24 = (bf16[64,768]{1,0:T(8,128)(2,1)S(1)}, bf16[64,768]{1,0:T(8,128)(2,1)S(1)}, u32[]{:S(2)}, u32[]{:S(2)}) collective-permute-start(bf16[64,768]{1,0:T(8,128)(2,1)S(1)} %get-tuple-element.367.refs_2_), channel_id=1, source_target_pairs={{0,16},{1,17},{2,18},{3,19},{4,20},{5,21},{6,22},{7,23},{8,24},{9,... | collective-permute-start | bytes 294920 | tf_op jit(solution)/shard_map/ppermute | solution.py:1027
  238.8 14.8 %collective-permute-start.33 = (bf16[512,768]{1,0:T(8,128)(2,1)S(1)}, bf16[512,768]{1,0:T(8,128)(2,1)S(1)}, u32[]{:S(2)}, u32[]{:S(2)}) collective-permute-start(bf16[512,768]{1,0:T(8,128)(2,1)S(1)} %get-tuple-element.389.refs_0_), channel_id=1, source_target_pairs={{0,4},{1,9},{2,6},{3,11},{4,0},{5,13},{6,2},{7,15},{8,12},{9,1},{1... | collective-permute-start | bytes 2359304 | tf_op jit(solution)/shard_map/ppermute | solution.py:1027
  254.5 17.6 %collective-permute-start.36 = (bf16[512,768]{1,0:T(8,128)(2,1)S(1)}, bf16[512,768]{1,0:T(8,128)(2,1)S(1)}, u32[]{:S(2)}, u32[]{:S(2)}) collective-permute-start(bf16[512,768]{1,0:T(8,128)(2,1)S(1)} %get-tuple-element.397.refs_0_), channel_id=1, source_target_pairs={{0,2},{1,5},{2,0},{3,7},{4,6},{5,1},{6,4},{7,3},{8,10},{9,13},{10,... | collective-permute-start | bytes 2359304 | tf_op jit(solution)/shard_map/ppermute | solution.py:1027
  255.3 16.8 %collective-permute-start.37 = (bf16[256,768]{1,0:T(8,128)(2,1)S(1)}, bf16[256,768]{1,0:T(8,128)(2,1)S(1)}, u32[]{:S(2)}, u32[]{:S(2)}) collective-permute-start(bf16[256,768]{1,0:T(8,128)(2,1)S(1)} %get-tuple-element.405.refs_4_), channel_id=1, source_target_pairs={{0,8},{1,9},{2,10},{3,11},{4,12},{5,13},{6,14},{7,15},{8,0},{9,1},... | collective-permute-start | bytes 1179656 | tf_op jit(solution)/shard_map/ppermute | solution.py:1027
  258.8 27.1 %collective-permute-start.39 = (bf16[512,768]{1,0:T(8,128)(2,1)S(1)}, bf16[512,768]{1,0:T(8,128)(2,1)S(1)}, u32[]{:S(2)}, u32[]{:S(2)}) collective-permute-start(bf16[512,768]{1,0:T(8,128)(2,1)S(1)} %get-tuple-element.403.refs_2_), channel_id=1, source_target_pairs={{0,2},{1,5},{2,0},{3,7},{4,6},{5,1},{6,4},{7,3},{8,10},{9,13},{10,... | collective-permute-start | bytes 2359304 | tf_op jit(solution)/shard_map/ppermute | solution.py:1027
  286.7 17.7 %collective-permute-start.42 = (bf16[3072,768]{1,0:T(8,128)(2,1)S(1)}, bf16[3072,768]{1,0:T(8,128)(2,1)S(1)}, u32[]{:S(2)}, u32[]{:S(2)}) collective-permute-start(bf16[3072,768]{1,0:T(8,128)(2,1)S(1)} %join_local.11.half_ref), channel_id=1, source_target_pairs={{0,1},{1,0},{2,3},{3,2},{4,5},{5,4},{6,7},{7,6},{8,9},{9,8},{10,11... | collective-permute-start | bytes 14155784 | tf_op jit(solution)/shard_map/ppermute | solution.py:1027
  287.8 16.5 %collective-permute-start.43 = (bf16[784,768]{1,0:T(8,128)(2,1)S(1)}, bf16[784,768]{1,0:T(8,128)(2,1)S(1)}, u32[]{:S(2)}, u32[]{:S(2)}) collective-permute-start(bf16[784,768]{1,0:T(8,128)(2,1)S(1)} %join_local.12.refs_0_), channel_id=1, source_target_pairs={{0,2},{1,5},{2,0},{3,7},{4,6},{5,1},{6,4},{7,3},{8,10},{9,13},{10,... | collective-permute-start | bytes 3612680 | tf_op jit(solution)/shard_map/ppermute | solution.py:1027
  (47 other events, 373.9 us)
where the time goes:
time: 321 us; the launch traced here: 317 us
  Pallas kernels  170 us (53%)
  waiting for transfers between devices  88.1 us (27%)
  starting transfers between devices  44.3 us (14%)
  local copies, waits for them, and re-layouts  6.34 us (2%)
  matrix products  4.18 us (1%)
    ppermute x29, waiting for transfers between devices, swap(): return lax.ppermute(values, ('rows', 'seq'), self.pairs)  60.9 us
    pallas_call x2, Pallas kernels, feed_back(): pl.pallas_call(functools.partial(feed_back_kernel, steps=steps, block=min...  36.4 us
    pallas_call x1, Pallas kernels, attention_backward(): pl.pallas_call(functools.partial(backward_kernel, block=min(512, keys)),...  36 us
    ppermute x29, starting transfers between devices, swap(): return lax.ppermute(values, ('rows', 'seq'), self.pairs)  34.3 us
    pallas_call x1, Pallas kernels, feed_forward(): pl.pallas_call(functools.partial(feed_forward_kernel, steps=steps, held=h...  23.5 us
    pallas_call x1, Pallas kernels, attention_forward(): pl.pallas_call(functools.partial(forward_kernel, block=min(512, queries))...  22.4 us
    ppermute x8, waiting for transfers between devices, send_pieces(): lax.ppermute(values[part], 'seq', trade(False, part))  14.1 us
    ppermute x4, waiting for transfers between devices, body(): lax.ppermute(value, 'seq', trade(True, part))  13.1 us
  transfers between devices with their start and end apart: 45, of which 13 were waited for; matrix products, arithmetic and copies ran while one was open for 3% of the time, Pallas kernels for 36%

commit v1 on v0

--- a/solution.py
+++ b/solution.py
@@ -646,7 +646,7 @@
 
 def input_grad_kernel(*refs, held):
     sources, outs = refs[:7], refs[7 : 7 + held]
-    (d_attn, *factors), sems = refs[7 + held : 14 + held], refs[-1]
+    (d_attn, *factors), total, sems = refs[7 + held : 14 + held], refs[-2], refs[-1]
     copies = [
         pltpu.make_async_copy(source, target, sems.at[index])
         for index, (source, target) in enumerate(zip(sources, (d_attn, *factors)))
@@ -654,17 +654,19 @@
     for copy in copies:
         copy.start()
     piece = outs[0].shape[0]
-    total = None
+    copies[0].wait()
     for index in range(3):
         for copy in copies[2 * index + 1 : 2 * index + 3]:
             copy.wait()
-    copies[0].wait()
-    for number, out_ref in enumerate(outs):
-        here = slice(number * piece, (number + 1) * piece)
-        total = d_attn[here, :].astype(F32)
-        for index in range(3):
-            total += dot(factors[2 * index][here, :], factors[2 * index + 1][...], NT)
-        out_ref[...] = total.astype(BF16)
+        left, right = factors[2 * index : 2 * index + 2]
+        for number, out_ref in enumerate(outs):
+            here = slice(number * piece, (number + 1) * piece)
+            before = d_attn[here, :].astype(F32) if index == 0 else total[here, :]
+            value = before + dot(left[here, :], right[...], NT)
+            if index < 2:
+                total[here, :] = value
+            else:
+                out_ref[...] = value.astype(BF16)
 
 
 def input_grad(d_attn, factors, held):
@@ -677,7 +679,7 @@
         out_specs=[pl.BlockSpec(memory_space=pltpu.VMEM)] * held,
         out_shape=shapes(*[((tokens // held, width), BF16)] * held),
         scratch_shapes=[pltpu.VMEM(value.shape, BF16) for value in values]
-        + [pltpu.SemaphoreType.DMA((7,))],
+        + [pltpu.VMEM((tokens, width), F32), pltpu.SemaphoreType.DMA((7,))],
         compiler_params=pltpu.CompilerParams(vmem_limit_bytes=24 * 2**20),
         cost_estimate=BRIEF,
         name="input_grad",

time: 321 us -> 319 us (level)
  no operation moved by 1% of the time
where the time goes in v1:
time: 319 us; the launch traced here: 315 us
  Pallas kernels  169 us (53%)
  waiting for transfers between devices  87.8 us (28%)
  starting transfers between devices  44.3 us (14%)
  local copies, waits for them, and re-layouts  6.34 us (2%)
  matrix products  4.18 us (1%)
    ppermute x29, waiting for transfers between devices, swap(): return lax.ppermute(values, ('rows', 'seq'), self.pairs)  60.6 us
    pallas_call x2, Pallas kernels, feed_back(): pl.pallas_call(functools.partial(feed_back_kernel, steps=steps, block=min...  36.5 us
    pallas_call x1, Pallas kernels, attention_backward(): pl.pallas_call(functools.partial(backward_kernel, block=min(512, keys)),...  36 us
    ppermute x29, starting transfers between devices, swap(): return lax.ppermute(values, ('rows', 'seq'), self.pairs)  34.4 us
    pallas_call x1, Pallas kernels, feed_forward(): pl.pallas_call(functools.partial(feed_forward_kernel, steps=steps, held=h...  23.5 us
    pallas_call x1, Pallas kernels, attention_forward(): pl.pallas_call(functools.partial(forward_kernel, block=min(512, queries))...  22.5 us
    ppermute x8, waiting for transfers between devices, send_pieces(): lax.ppermute(values[part], 'seq', trade(False, part))  14.1 us
    ppermute x4, waiting for transfers between devices, body(): lax.ppermute(value, 'seq', trade(True, part))  13.1 us
  transfers between devices with their start and end apart: 45, of which 13 were waited for; matrix products, arithmetic and copies ran while one was open for 3% of the time, Pallas kernels for 36%

profile of v1, /device:TPU:0, one launch (start us, length us, event | category | flops | bytes accessed | tf_op | source)
XLA Modules:
  0.0 315.2 jit_solution(16523302262919854461)
XLA Ops:
  11.9 4.6 %collective-permute-done.2.refs_2_ = bf16[272,768]{1,0:T(8,128)(2,1)S(1)} collective-permute-done((bf16[272,768]{1,0:T(8,128)(2,1)S(1)}, bf16[272,768]{1,0:T(8,128)(2,1)S(1)}, u32[]{:S(2)}, u32[]{:S(2)}) %collective-permute-start.2) | collective-permute-done | bytes 417824 | tf_op jit(solution)/shard_map/ppermute | solution.py:1211
  16.5 8.4 %collective-permute-done.3.refs_3_ = bf16[272,768]{1,0:T(8,128)(2,1)S(1)} collective-permute-done((bf16[272,768]{1,0:T(8,128)(2,1)S(1)}, bf16[272,768]{1,0:T(8,128)(2,1)S(1)}, u32[]{:S(2)}, u32[]{:S(2)}) %collective-permute-start.3) | collective-permute-done | bytes 417824 | tf_op jit(solution)/shard_map/ppermute | solution.py:1211
  32.8 22.5 %attention_forward.1 = (bf16[1024,768]{1,0:T(8,128)(2,1)}, bf16[12,1024,128]{2,1,0:T(8,128)(2,1)}) custom-call(bf16[1024,768]{1,0:T(8,128)(2,1)S(1)} %multiply_convert_fusion.q_ref, bf16[1024,768]{1,0:T(8,128)(2,1)S(1)} %convolution_convert_fusion.k_ref, bf16[1024,768]{1,0:T(8,128)(2,1)S(1)} %add_convert_fusion.v_ref, bf16[1024,128]{1,0:T(8,128)(2,1)S(1)} %copy-done.3, ...), custom_call_target="tpu_custom_call" | custom-call | flops 1 | bytes 1 | tf_op jit(solution)/shard_map/attention_forward/pallas_call | solution.py:90
  55.3 23.5 %feed_forward.1 = (bf16[1024,768]{1,0:T(8,128)(2,1)}, f32[1024,128]{1,0:T(8,128)}, bf16[1024,768]{1,0:T(8,128)(2,1)}, bf16[3072,1024]{1,0:T(8,128)(2,1)}, bf16[1...) custom-call(bf16[1024,768]{1,0:T(8,128)(2,1)S(1)} %copy-done, ...), custom_call_target="tpu_custom_call" | custom-call | flops 1 | bytes 1 | tf_op jit(solution)/shard_map/feed_forward/pallas_call | solution.py:327
  78.8 16.7 %feed_back.1 = (bf16[2,1536,768]{2,1,0:T(8,128)(2,1)}, f32[8,512]{1,0:T(8,128)}, bf16[1024,768]{1,0:T(8,128)(2,1)}) custom-call(s32[1]{0:T(128)S(6)} %sub.2.which_ref, bf16[1024,768]{1,0:T(8,128)(2,1)} %get-tuple-element.239.d_down_ref, bf16[1024,3072]{1,0:T(8,128)(2,1)} %get-tuple-element.240.slope_ref, bf16[3072,1024]{1,0:T(8,128)(2,1)} %get-tuple-element.241.active_t_ref, ...), custom_call_target="tpu_custom_call" | custom-call | flops 1 | bytes 1 | tf_op jit(solution)/shard_map/feed_back/pallas_call | solution.py:496
  98.9 19.7 %feed_back_last.1 = (bf16[2,1536,768]{2,1,0:T(8,128)(2,1)}, f32[8,512]{1,0:T(8,128)}, bf16[1024,768]{1,0:T(8,128)(2,1)}, bf16[1024,768]{1,0:T(8,128)(2,1)}, f32[8,768]{1,0:T(8,128)}) custom-call(s32[1]{0:T(128)} %bitcast.1.which_ref.core_ref, bf16[1024,768]{1,0:T(8,128)(2,1)} %get-tuple-element.239.d_down_ref, ...), custom_call_target="tpu_custom_call" | custom-call | flops 1 | bytes 1 | tf_op jit(solution)/shard_map/feed_back_last/pallas_call | solution.py:496
  118.8 4.9 %scatter_first.1 = (bf16[1024,768]{1,0:T(8,128)(2,1)S(1)}, bf16[1024,768]{1,0:T(8,128)(2,1)S(1)}, bf16[512,768]{1,0:T(8,128)(2,1)S(1)}, bf16[512,768]{1,0:T(8,128)(2,1)S(1)}) custom-call(s32[2]{0:T(128)S(1)} %get-tuple-element.453.bits_ref, bf16[3072,768]{1,0:T(8,128)(2,1)} %bitcast.30, bf16[3072,768]{1,0:T(8,128)(2,1)} %collective-permute-done.8.got_at), custom_call_target="tpu_custom_call" | custom-call | flops 1 | bytes 1 | tf_op jit(solution)/shard_map/scatter_first/pallas_call | solution.py:872
  127.0 36.0 %attention_backward.1 = (bf16[1024,768]{1,0:T(8,128)(2,1)}, bf16[1024,768]{1,0:T(8,128)(2,1)}, bf16[1024,768]{1,0:T(8,128)(2,1)}) custom-call(bf16[12,1024,128]{2,1,0:T(8,128)(2,1)} %get-tuple-element.261.query_ref, bf16[1024,768]{1,0:T(8,128)(2,1)S(1)} %convolution_convert_fusion.k_ref, bf16[1024,768]{1,0:T(8,128)(2,1)S(1)} %copy-done.2, ...), custom_call_target="tpu_custom_call" | custom-call | flops 1 | bytes 1 | tf_op jit(solution)/shard_map/attention_backward/pallas_call | solution.py:168
  167.0 8.0 %weight_halves.1 = (bf16[1536,768]{1,0:T(8,128)(2,1)S(1)}, bf16[1536,768]{1,0:T(8,128)(2,1)S(1)}, f32[16,768]{1,0:T(8,128)S(1)}) custom-call(s32[1]{0:T(128)} %bitcast.1.which_ref.core_ref, f32[8,768]{1,0:T(8,128)S(1)} %copy-done.6, f32[8,768]{1,0:T(8,128)S(1)} %copy-done.5, f32[8,512]{1,0:T(8,128)S(1)} %copy-done.8, f32[8,512]{1,0:T(8,128)S(1)} %copy-done.7, ...), custom_call_target="tpu_custom_call" | custom-call | flops 1 | bytes 1 | tf_op jit(solution)/shard_map/weight_halves/pallas_call | solution.py:631
  179.8 6.6 %input_grad.1 = (bf16[256,768]{1,0:T(8,128)(2,1)S(1)}, bf16[256,768]{1,0:T(8,128)(2,1)S(1)}, bf16[256,768]{1,0:T(8,128)(2,1)S(1)}, bf16[256,768]{1,0:T(8,128)(2,1)S(1)}) custom-call(bf16[1024,768]{1,0:T(8,128)(2,1)} %get-tuple-element.287.refs_5_.refs_0_, bf16[1024,768]{1,0:T(8,128)(2,1)} %get-tuple-element.310.refs_1_, bf16[768,768]{1,0:T(8,128)(2,1)} %refs_2_.1, ...), custom_call_target="tpu_custom_call" | custom-call | flops 1 | bytes 1 | tf_op jit(solution)/shard_map/input_grad/pallas_call | solution.py:676
  191.4 3.0 place.2
  194.5 9.7 %collective-permute-done.21.refs_3_ = bf16[64,768]{1,0:T(8,128)(2,1)S(1)} collective-permute-done((bf16[64,768]{1,0:T(8,128)(2,1)S(1)}, bf16[64,768]{1,0:T(8,128)(2,1)S(1)}, u32[]{:S(2)}, u32[]{:S(2)}) %collective-permute-start.21) | collective-permute-done | bytes 98336 | tf_op jit(solution)/shard_map/ppermute | solution.py:1029
  211.4 6.4 %collective-permute-done.28.refs_2_ = bf16[256,768]{1,0:T(8,128)(2,1)S(1)} collective-permute-done((bf16[256,768]{1,0:T(8,128)(2,1)S(1)}, bf16[256,768]{1,0:T(8,128)(2,1)S(1)}, u32[]{:S(2)}, u32[]{:S(2)}) %collective-permute-start.28) | collective-permute-done | bytes 393248 | tf_op jit(solution)/shard_map/ppermute | solution.py:1182
  217.8 7.7 %collective-permute-done.29.refs_3_ = bf16[256,768]{1,0:T(8,128)(2,1)S(1)} collective-permute-done((bf16[256,768]{1,0:T(8,128)(2,1)S(1)}, bf16[256,768]{1,0:T(8,128)(2,1)S(1)}, u32[]{:S(2)}, u32[]{:S(2)}) %collective-permute-start.29) | collective-permute-done | bytes 393248 | tf_op jit(solution)/shard_map/ppermute | solution.py:1182
  230.9 3.9 %collective-permute-done.31.refs_3_ = bf16[128,768]{1,0:T(8,128)(2,1)S(1)} collective-permute-done((bf16[128,768]{1,0:T(8,128)(2,1)S(1)}, bf16[128,768]{1,0:T(8,128)(2,1)S(1)}, u32[]{:S(2)}, u32[]{:S(2)}) %collective-permute-start.31) | collective-permute-done | bytes 196640 | tf_op jit(solution)/shard_map/ppermute | solution.py:1029
  241.7 10.8 %collective-permute-done.35.refs_1_ = bf16[208,768]{1,0:T(8,128)(2,1)S(1)} collective-permute-done((bf16[208,768]{1,0:T(8,128)(2,1)S(1)}, bf16[208,768]{1,0:T(8,128)(2,1)S(1)}, u32[]{:S(2)}, u32[]{:S(2)}) %collective-permute-start.35) | collective-permute-done | bytes 319520 | tf_op jit(solution)/shard_map/ppermute | solution.py:1029
  254.0 3.3 %collective-permute-start.37 = (bf16[256,768]{1,0:T(8,128)(2,1)S(1)}, bf16[256,768]{1,0:T(8,128)(2,1)S(1)}, u32[]{:S(2)}, u32[]{:S(2)}) collective-permute-start(bf16[256,768]{1,0:T(8,128)(2,1)S(1)} %get-tuple-element.405.refs_4_), channel_id=1, source_target_pairs={{0,8},{1,9},{2,10},{3,11},{4,12},{5,13},{6,14},{7,15},{8,0},{9,1},... | collective-permute-start | bytes 1179656 | tf_op jit(solution)/shard_map/ppermute | solution.py:1029
  258.9 11.9 %collective-permute-done.38.refs_1_ = bf16[208,768]{1,0:T(8,128)(2,1)S(1)} collective-permute-done((bf16[208,768]{1,0:T(8,128)(2,1)S(1)}, bf16[208,768]{1,0:T(8,128)(2,1)S(1)}, u32[]{:S(2)}, u32[]{:S(2)}) %collective-permute-start.38) | collective-permute-done | bytes 319520 | tf_op jit(solution)/shard_map/ppermute | solution.py:1029
  274.5 10.0 %collective-permute-done.40.refs_7_ = bf16[256,768]{1,0:T(8,128)(2,1)S(1)} collective-permute-done((bf16[256,768]{1,0:T(8,128)(2,1)S(1)}, bf16[256,768]{1,0:T(8,128)(2,1)S(1)}, u32[]{:S(2)}, u32[]{:S(2)}) %collective-permute-start.40) | collective-permute-done | bytes 393248 | tf_op jit(solution)/shard_map/ppermute | solution.py:1029
  287.7 5.2 %feed_out.2 = (f32[3072,768]{1,0:T(8,128)}, f32[768,3072]{1,0:T(8,128)}) custom-call(s32[1]{0:T(128)} %bitcast.1.which_ref.core_ref, bf16[3072,768]{1,0:T(8,128)(2,1)S(1)} %join_local.11.half_ref), custom_call_target="tpu_custom_call" | custom-call | flops 1 | bytes 1 | tf_op jit(solution)/shard_map/feed_out/pallas_call | solution.py:706
  292.9 10.2 %collective-permute-done.43.refs_1_ = bf16[784,768]{1,0:T(8,128)(2,1)S(1)} collective-permute-done((bf16[784,768]{1,0:T(8,128)(2,1)S(1)}, bf16[784,768]{1,0:T(8,128)(2,1)S(1)}, u32[]{:S(2)}, u32[]{:S(2)}) %collective-permute-start.43) | collective-permute-done | bytes 1204256 | tf_op jit(solution)/shard_map/ppermute | solution.py:1029
  303.3 2.6 attn_out.2
  306.0 5.1 %feed_out.3 = (f32[3072,768]{1,0:T(8,128)}, f32[768,3072]{1,0:T(8,128)}) custom-call(s32[1]{0:T(128)S(6)} %sub.2.which_ref, bf16[3072,768]{1,0:T(8,128)(2,1)S(1)} %collective-permute-done.42.half_ref, f32[3072,768]{1,0:T(8,128)} %get-tuple-element.437.refs_0_, f32[768,3072]{1,0:T(8,128)} %get-tuple-element.438.refs_1_), custom_call_target="tpu_custom_call", output_to_operand_aliasing={{0}: (2, {}), {1}: (3, {})} | custom-call | flops 1 | bytes 1 | tf_op jit(solution)/shard_map/feed_out/pallas_call | solution.py:706
  312.4 2.6 attn_out.3
  (172 shorter events, 70.2 us)
Async XLA Ops:
  6.0 18.9 %collective-permute-start.3 = (bf16[272,768]{1,0:T(8,128)(2,1)S(1)}, bf16[272,768]{1,0:T(8,128)(2,1)S(1)}, u32[]{:S(2)}, u32[]{:S(2)}) collective-permute-start(bf16[272,768]{1,0:T(8,128)(2,1)S(1)} %get-tuple-element.232), channel_id=1, source_target_pairs={{0,3},{1,2},{2,1},{3,0},{4,7},{5,6},{6,5},{7,4},{8,11},{9,10},{10,... | collective-permute-start | bytes 1253384 | tf_op jit(solution)/shard_map/ppermute | solution.py:1211
  26.5 28.8 %collective-permute-start.7 = (bf16[256,768]{1,0:T(8,128)(2,1)S(1)}, bf16[256,768]{1,0:T(8,128)(2,1)S(1)}, u32[]{:S(2)}, u32[]{:S(2)}) collective-permute-start(bf16[256,768]{1,0:T(8,128)(2,1)S(1)} %get-tuple-element.449), channel_id=1, source_target_pairs={{0,3},{1,2},{2,1},{3,0},{4,7},{5,6},{6,5},{7,4},{8,11},{9,10},{10,... | collective-permute-start | bytes 1179656 | tf_op jit(solution)/shard_map/ppermute | solution.py:1170
  28.0 27.3 %collective-permute-start.6 = (bf16[256,768]{1,0:T(8,128)(2,1)S(1)}, bf16[256,768]{1,0:T(8,128)(2,1)S(1)}, u32[]{:S(2)}, u32[]{:S(2)}) collective-permute-start(bf16[256,768]{1,0:T(8,128)(2,1)S(1)} %get-tuple-element.450), channel_id=1, source_target_pairs={{0,2},{1,3},{2,0},{3,1},{4,6},{5,7},{6,4},{7,5},{8,10},{9,11},{10,... | collective-permute-start | bytes 1179656 | tf_op jit(solution)/shard_map/ppermute | solution.py:1170
  28.3 27.0 %collective-permute-start.5 = (bf16[256,768]{1,0:T(8,128)(2,1)S(1)}, bf16[256,768]{1,0:T(8,128)(2,1)S(1)}, u32[]{:S(2)}, u32[]{:S(2)}) collective-permute-start(bf16[256,768]{1,0:T(8,128)(2,1)S(1)} %get-tuple-element.451), channel_id=1, source_target_pairs={{0,1},{1,0},{2,3},{3,2},{4,5},{5,4},{6,7},{7,6},{8,9},{9,8},{10,11... | collective-permute-start | bytes 1179656 | tf_op jit(solution)/shard_map/ppermute | solution.py:1170
  28.4 26.8 %collective-permute-start.4 = (bf16[256,768]{1,0:T(8,128)(2,1)S(1)}, bf16[256,768]{1,0:T(8,128)(2,1)S(1)}, u32[]{:S(2)}, u32[]{:S(2)}) collective-permute-start(bf16[256,768]{1,0:T(8,128)(2,1)S(1)} %get-tuple-element.452), channel_id=1, source_target_pairs={{0,0},{1,1},{2,2},{3,3},{4,4},{5,5},{6,6},{7,7},{8,8},{9,9},{10,10... | collective-permute-start | bytes 1179656 | tf_op jit(solution)/shard_map/ppermute | solution.py:1170
  95.5 23.2 %collective-permute-start.8 = (bf16[3072,768]{1,0:T(8,128)(2,1)}, bf16[3072,768]{1,0:T(8,128)(2,1)}, u32[]{:S(2)}, u32[]{:S(2)}) collective-permute-start(bf16[3072,768]{1,0:T(8,128)(2,1)} %bitcast.34), channel_id=1, source_target_pairs={{0,1},{1,0},{2,3},{3,2},{4,5},{5,4},{6,7},{7,6},{8,9},{9,8},{10,11... | collective-permute-start | bytes 14155784 | tf_op jit(solution)/shard_map/ppermute | solution.py:1029
  95.9 22.7 %collective-permute-start.9 = (bf16[256,768]{1,0:T(8,128)(2,1)}, bf16[256,768]{1,0:T(8,128)(2,1)S(1)}, u32[]{:S(2)}, u32[]{:S(2)}) collective-permute-start(bf16[256,768]{1,0:T(8,128)(2,1)} %get-tuple-element.249), channel_id=1, source_target_pairs={{0,0},{1,1},{2,2},{3,3},{4,4},{5,5},{6,6},{7,7},{8,8},{9,9},{10,10... | collective-permute-start | bytes 1179656 | tf_op jit(solution)/shard_map/ppermute | solution.py:1182
  96.9 21.7 %collective-permute-start.10 = (bf16[256,768]{1,0:T(8,128)(2,1)}, bf16[256,768]{1,0:T(8,128)(2,1)S(1)}, u32[]{:S(2)}, u32[]{:S(2)}) collective-permute-start(bf16[256,768]{1,0:T(8,128)(2,1)} %get-tuple-element.250), channel_id=1, source_target_pairs={{1,0},{0,1},{3,2},{2,3},{5,4},{4,5},{7,6},{6,7},{9,8},{8,9},{11,10... | collective-permute-start | bytes 1179656 | tf_op jit(solution)/shard_map/ppermute | solution.py:1182
  97.1 21.6 %collective-permute-start.11 = (bf16[256,768]{1,0:T(8,128)(2,1)}, bf16[256,768]{1,0:T(8,128)(2,1)S(1)}, u32[]{:S(2)}, u32[]{:S(2)}) collective-permute-start(bf16[256,768]{1,0:T(8,128)(2,1)} %get-tuple-element.251), channel_id=1, source_target_pairs={{2,0},{3,1},{0,2},{1,3},{6,4},{7,5},{4,6},{5,7},{10,8},{11,9},{8,1... | collective-permute-start | bytes 1179656 | tf_op jit(solution)/shard_map/ppermute | solution.py:1182
  98.7 20.0 %collective-permute-start.12 = (bf16[256,768]{1,0:T(8,128)(2,1)}, bf16[256,768]{1,0:T(8,128)(2,1)S(1)}, u32[]{:S(2)}, u32[]{:S(2)}) collective-permute-start(bf16[256,768]{1,0:T(8,128)(2,1)} %get-tuple-element.252), channel_id=1, source_target_pairs={{3,0},{2,1},{1,2},{0,3},{7,4},{6,5},{5,6},{4,7},{11,8},{10,9},{9,1... | collective-permute-start | bytes 1179656 | tf_op jit(solution)/shard_map/ppermute | solution.py:1182
  123.7 39.3 %collective-permute-start.13 = (bf16[1024,768]{1,0:T(8,128)(2,1)S(1)}, bf16[1024,768]{1,0:T(8,128)(2,1)S(1)}, u32[]{:S(2)}, u32[]{:S(2)}) collective-permute-start(bf16[1024,768]{1,0:T(8,128)(2,1)S(1)} %get-tuple-element.272), channel_id=1, source_target_pairs={{0,2},{1,5},{2,0},{3,7},{4,6},{5,1},{6,4},{7,3},{8,10},{9,13},{10,... | collective-permute-start | bytes 4718600 | tf_op jit(solution)/shard_map/ppermute | solution.py:1029
  125.5 37.5 %collective-permute-start.14 = (bf16[512,768]{1,0:T(8,128)(2,1)S(1)}, bf16[512,768]{1,0:T(8,128)(2,1)S(1)}, u32[]{:S(2)}, u32[]{:S(2)}) collective-permute-start(bf16[512,768]{1,0:T(8,128)(2,1)S(1)} %get-tuple-element.274), channel_id=1, source_target_pairs={{0,8},{1,9},{2,10},{3,11},{4,12},{5,13},{6,14},{7,15},{8,0},{9,1},... | collective-permute-start | bytes 2359304 | tf_op jit(solution)/shard_map/ppermute | solution.py:1029
  187.6 16.5 %collective-permute-start.22 = (bf16[768,768]{1,0:T(8,128)(2,1)S(1)}, bf16[768,768]{1,0:T(8,128)(2,1)S(1)}, u32[]{:S(2)}, u32[]{:S(2)}) collective-permute-start(bf16[768,768]{1,0:T(8,128)(2,1)S(1)} %get-tuple-element.341), channel_id=1, source_target_pairs={{0,2},{1,5},{2,0},{3,7},{4,6},{5,1},{6,4},{7,3},{8,10},{9,13},{10,... | collective-permute-start | bytes 3538952 | tf_op jit(solution)/shard_map/ppermute | solution.py:1029
  188.5 15.7 %collective-permute-start.20 = (bf16[128,768]{1,0:T(8,128)(2,1)S(1)}, bf16[128,768]{1,0:T(8,128)(2,1)S(1)}, u32[]{:S(2)}, u32[]{:S(2)}) collective-permute-start(bf16[128,768]{1,0:T(8,128)(2,1)S(1)} %get-tuple-element.335), channel_id=1, source_target_pairs={{0,16},{1,17},{2,18},{3,19},{4,20},{5,21},{6,22},{7,23},{8,24},{9,... | collective-permute-start | bytes 589832 | tf_op jit(solution)/shard_map/ppermute | solution.py:1029
  204.4 21.0 %collective-permute-start.25 = (bf16[384,768]{1,0:T(8,128)(2,1)S(1)}, bf16[384,768]{1,0:T(8,128)(2,1)S(1)}, u32[]{:S(2)}, u32[]{:S(2)}) collective-permute-start(bf16[384,768]{1,0:T(8,128)(2,1)S(1)} %get-tuple-element.360), channel_id=1, source_target_pairs={{0,4},{1,9},{2,6},{3,11},{4,0},{5,13},{6,2},{7,15},{8,12},{9,1},{1... | collective-permute-start | bytes 1769480 | tf_op jit(solution)/shard_map/ppermute | solution.py:1029
  207.3 18.2 %collective-permute-start.29 = (bf16[256,768]{1,0:T(8,128)(2,1)S(1)}, bf16[256,768]{1,0:T(8,128)(2,1)S(1)}, u32[]{:S(2)}, u32[]{:S(2)}) collective-permute-start(bf16[256,768]{1,0:T(8,128)(2,1)S(1)} %get-tuple-element.345), channel_id=1, source_target_pairs={{3,0},{2,1},{1,2},{0,3},{7,4},{6,5},{5,6},{4,7},{11,8},{10,9},{9,1... | collective-permute-start | bytes 1179656 | tf_op jit(solution)/shard_map/ppermute | solution.py:1182
  208.4 17.1 %collective-permute-start.23 = (bf16[128,768]{1,0:T(8,128)(2,1)S(1)}, bf16[128,768]{1,0:T(8,128)(2,1)S(1)}, u32[]{:S(2)}, u32[]{:S(2)}) collective-permute-start(bf16[128,768]{1,0:T(8,128)(2,1)S(1)} %get-tuple-element.365.refs_0_), channel_id=1, source_target_pairs={{0,16},{1,17},{2,18},{3,19},{4,20},{5,21},{6,22},{7,23},{8,24},{9,... | collective-permute-start | bytes 589832 | tf_op jit(solution)/shard_map/ppermute | solution.py:1029
  210.3 15.1 %collective-permute-start.24 = (bf16[64,768]{1,0:T(8,128)(2,1)S(1)}, bf16[64,768]{1,0:T(8,128)(2,1)S(1)}, u32[]{:S(2)}, u32[]{:S(2)}) collective-permute-start(bf16[64,768]{1,0:T(8,128)(2,1)S(1)} %get-tuple-element.367.refs_2_), channel_id=1, source_target_pairs={{0,16},{1,17},{2,18},{3,19},{4,20},{5,21},{6,22},{7,23},{8,24},{9,... | collective-permute-start | bytes 294920 | tf_op jit(solution)/shard_map/ppermute | solution.py:1029
  237.7 14.8 %collective-permute-start.33 = (bf16[512,768]{1,0:T(8,128)(2,1)S(1)}, bf16[512,768]{1,0:T(8,128)(2,1)S(1)}, u32[]{:S(2)}, u32[]{:S(2)}) collective-permute-start(bf16[512,768]{1,0:T(8,128)(2,1)S(1)} %get-tuple-element.389.refs_0_), channel_id=1, source_target_pairs={{0,4},{1,9},{2,6},{3,11},{4,0},{5,13},{6,2},{7,15},{8,12},{9,1},{1... | collective-permute-start | bytes 2359304 | tf_op jit(solution)/shard_map/ppermute | solution.py:1029
  253.2 17.6 %collective-permute-start.36 = (bf16[512,768]{1,0:T(8,128)(2,1)S(1)}, bf16[512,768]{1,0:T(8,128)(2,1)S(1)}, u32[]{:S(2)}, u32[]{:S(2)}) collective-permute-start(bf16[512,768]{1,0:T(8,128)(2,1)S(1)} %get-tuple-element.397.refs_0_), channel_id=1, source_target_pairs={{0,2},{1,5},{2,0},{3,7},{4,6},{5,1},{6,4},{7,3},{8,10},{9,13},{10,... | collective-permute-start | bytes 2359304 | tf_op jit(solution)/shard_map/ppermute | solution.py:1029
  254.0 16.8 %collective-permute-start.37 = (bf16[256,768]{1,0:T(8,128)(2,1)S(1)}, bf16[256,768]{1,0:T(8,128)(2,1)S(1)}, u32[]{:S(2)}, u32[]{:S(2)}) collective-permute-start(bf16[256,768]{1,0:T(8,128)(2,1)S(1)} %get-tuple-element.405.refs_4_), channel_id=1, source_target_pairs={{0,8},{1,9},{2,10},{3,11},{4,12},{5,13},{6,14},{7,15},{8,0},{9,1},... | collective-permute-start | bytes 1179656 | tf_op jit(solution)/shard_map/ppermute | solution.py:1029
  257.5 27.1 %collective-permute-start.39 = (bf16[512,768]{1,0:T(8,128)(2,1)S(1)}, bf16[512,768]{1,0:T(8,128)(2,1)S(1)}, u32[]{:S(2)}, u32[]{:S(2)}) collective-permute-start(bf16[512,768]{1,0:T(8,128)(2,1)S(1)} %get-tuple-element.403.refs_2_), channel_id=1, source_target_pairs={{0,2},{1,5},{2,0},{3,7},{4,6},{5,1},{6,4},{7,3},{8,10},{9,13},{10,... | collective-permute-start | bytes 2359304 | tf_op jit(solution)/shard_map/ppermute | solution.py:1029
  285.4 17.7 %collective-permute-start.42 = (bf16[3072,768]{1,0:T(8,128)(2,1)S(1)}, bf16[3072,768]{1,0:T(8,128)(2,1)S(1)}, u32[]{:S(2)}, u32[]{:S(2)}) collective-permute-start(bf16[3072,768]{1,0:T(8,128)(2,1)S(1)} %join_local.11.half_ref), channel_id=1, source_target_pairs={{0,1},{1,0},{2,3},{3,2},{4,5},{5,4},{6,7},{7,6},{8,9},{9,8},{10,11... | collective-permute-start | bytes 14155784 | tf_op jit(solution)/shard_map/ppermute | solution.py:1029
  286.5 16.5 %collective-permute-start.43 = (bf16[784,768]{1,0:T(8,128)(2,1)S(1)}, bf16[784,768]{1,0:T(8,128)(2,1)S(1)}, u32[]{:S(2)}, u32[]{:S(2)}) collective-permute-start(bf16[784,768]{1,0:T(8,128)(2,1)S(1)} %join_local.12.refs_0_), channel_id=1, source_target_pairs={{0,2},{1,5},{2,0},{3,7},{4,6},{5,1},{6,4},{7,3},{8,10},{9,13},{10,... | collective-permute-start | bytes 3612680 | tf_op jit(solution)/shard_map/ppermute | solution.py:1029
  (47 other events, 370.4 us)

commit v2 on v1

--- a/solution.py
+++ b/solution.py
@@ -1175,10 +1175,10 @@
                 for part in range(held)
             ]
 
-        def send_pieces(values):
+        def send_pieces(values, chosen=range(held)):
             return [
                 value
-                for part in range(held)
+                for part in chosen
                 for value in (values[part], lax.ppermute(values[part], "seq", trade(False, part)))
             ]
 
@@ -1301,13 +1301,20 @@
         )
         own, got, small, *d_input = advance([feed_flow], own, got, small, *d_input)
         attn_flow = chips(own, got, [(own.shape[0], wide)], small)
-        piece_flow = table.open(arriving(send_pieces(d_input)))
+        held_back = held // 2
+        soon = [part for part in range(held) if part != held_back]
+        piece_flow = table.open(arriving(send_pieces(d_input, soon)))
+        last_flow = table.open(arriving(send_pieces(d_input, [held_back])))
 
         both = [feed_flow, attn_flow]
         layer_out = place_pieces(list(map(in_hbm, layer_flow.result)))
         (layer_out,) = advance(both, layer_out)
         advance(both + [piece_flow])
-        grad_in = place_pieces(piece_flow.result)
+        advance(both)
+        advance(both + [last_flow])
+        arrived = list(piece_flow.result)
+        arrived.insert(held_back, last_flow.result[0])
+        grad_in = place_pieces(arrived)
         (grad_in,) = advance(both, grad_in)
         while feed_flow.left > 1:
             advance(both)

time: 319 us -> 317 us (level)
  transfers between devices with their start and end apart: 45 -> 45, of which waited for: 13 -> 16; matrix products, arithmetic and copies ran while one was open for 3% -> 3% of each run, Pallas kernels for 36% -> 36%
where the time goes in v2:
time: 317 us; the launch traced here: 313 us
  Pallas kernels  169 us (53%)
  waiting for transfers between devices  88.3 us (28%)
  starting transfers between devices  41.9 us (13%)
  local copies, waits for them, and re-layouts  6.34 us (2%)
  matrix products  4.18 us (1%)
    ppermute x29, waiting for transfers between devices, swap(): return lax.ppermute(values, ('rows', 'seq'), self.pairs)  60.8 us
    pallas_call x2, Pallas kernels, feed_back(): pl.pallas_call(functools.partial(feed_back_kernel, steps=steps, block=min...  36.4 us
    pallas_call x1, Pallas kernels, attention_backward(): pl.pallas_call(functools.partial(backward_kernel, block=min(512, keys)),...  36 us
    ppermute x29, starting transfers between devices, swap(): return lax.ppermute(values, ('rows', 'seq'), self.pairs)  31.6 us
    pallas_call x1, Pallas kernels, feed_forward(): pl.pallas_call(functools.partial(feed_forward_kernel, steps=steps, held=h...  23.5 us
    pallas_call x1, Pallas kernels, attention_forward(): pl.pallas_call(functools.partial(forward_kernel, block=min(512, queries))...  22.4 us
    ppermute x8, waiting for transfers between devices, send_pieces(): lax.ppermute(values[part], 'seq', trade(False, part))  14.5 us
    ppermute x4, waiting for transfers between devices, body(): lax.ppermute(value, 'seq', trade(True, part))  13.1 us
  transfers between devices with their start and end apart: 45, of which 16 were waited for; matrix products, arithmetic and copies ran while one was open for 3% of the time, Pallas kernels for 36%

profile of v2, /device:TPU:0, one launch (start us, length us, event | category | flops | bytes accessed | tf_op | source)
XLA Modules:
  0.0 313.2 jit_solution(13105686726733234511)
XLA Ops:
  11.9 4.6 %collective-permute-done.2.refs_2_ = bf16[272,768]{1,0:T(8,128)(2,1)S(1)} collective-permute-done((bf16[272,768]{1,0:T(8,128)(2,1)S(1)}, bf16[272,768]{1,0:T(8,128)(2,1)S(1)}, u32[]{:S(2)}, u32[]{:S(2)}) %collective-permute-start.2) | collective-permute-done | bytes 417824 | tf_op jit(solution)/shard_map/ppermute | solution.py:1211
  16.5 8.4 %collective-permute-done.3.refs_3_ = bf16[272,768]{1,0:T(8,128)(2,1)S(1)} collective-permute-done((bf16[272,768]{1,0:T(8,128)(2,1)S(1)}, bf16[272,768]{1,0:T(8,128)(2,1)S(1)}, u32[]{:S(2)}, u32[]{:S(2)}) %collective-permute-start.3) | collective-permute-done | bytes 417824 | tf_op jit(solution)/shard_map/ppermute | solution.py:1211
  32.8 22.4 %attention_forward.1 = (bf16[1024,768]{1,0:T(8,128)(2,1)}, bf16[12,1024,128]{2,1,0:T(8,128)(2,1)}) custom-call(bf16[1024,768]{1,0:T(8,128)(2,1)S(1)} %multiply_convert_fusion.q_ref, bf16[1024,768]{1,0:T(8,128)(2,1)S(1)} %convolution_convert_fusion.k_ref, bf16[1024,768]{1,0:T(8,128)(2,1)S(1)} %add_convert_fusion.v_ref, bf16[1024,128]{1,0:T(8,128)(2,1)S(1)} %copy-done.3, ...), custom_call_target="tpu_custom_call" | custom-call | flops 1 | bytes 1 | tf_op jit(solution)/shard_map/attention_forward/pallas_call | solution.py:90
  55.2 23.5 %feed_forward.1 = (bf16[1024,768]{1,0:T(8,128)(2,1)}, f32[1024,128]{1,0:T(8,128)}, bf16[1024,768]{1,0:T(8,128)(2,1)}, bf16[3072,1024]{1,0:T(8,128)(2,1)}, bf16[1...) custom-call(bf16[1024,768]{1,0:T(8,128)(2,1)S(1)} %copy-done, ...), custom_call_target="tpu_custom_call" | custom-call | flops 1 | bytes 1 | tf_op jit(solution)/shard_map/feed_forward/pallas_call | solution.py:327
  78.7 16.7 %feed_back.1 = (bf16[2,1536,768]{2,1,0:T(8,128)(2,1)}, f32[8,512]{1,0:T(8,128)}, bf16[1024,768]{1,0:T(8,128)(2,1)}) custom-call(s32[1]{0:T(128)S(6)} %sub.2.which_ref, bf16[1024,768]{1,0:T(8,128)(2,1)} %get-tuple-element.239.d_down_ref, bf16[1024,3072]{1,0:T(8,128)(2,1)} %get-tuple-element.240.slope_ref, bf16[3072,1024]{1,0:T(8,128)(2,1)} %get-tuple-element.241.active_t_ref, ...), custom_call_target="tpu_custom_call" | custom-call | flops 1 | bytes 1 | tf_op jit(solution)/shard_map/feed_back/pallas_call | solution.py:496
  98.8 19.7 %feed_back_last.1 = (bf16[2,1536,768]{2,1,0:T(8,128)(2,1)}, f32[8,512]{1,0:T(8,128)}, bf16[1024,768]{1,0:T(8,128)(2,1)}, bf16[1024,768]{1,0:T(8,128)(2,1)}, f32[8,768]{1,0:T(8,128)}) custom-call(s32[1]{0:T(128)} %bitcast.1.which_ref.core_ref, bf16[1024,768]{1,0:T(8,128)(2,1)} %get-tuple-element.239.d_down_ref, ...), custom_call_target="tpu_custom_call" | custom-call | flops 1 | bytes 1 | tf_op jit(solution)/shard_map/feed_back_last/pallas_call | solution.py:496
  118.7 4.9 %scatter_first.1 = (bf16[1024,768]{1,0:T(8,128)(2,1)S(1)}, bf16[1024,768]{1,0:T(8,128)(2,1)S(1)}, bf16[512,768]{1,0:T(8,128)(2,1)S(1)}, bf16[512,768]{1,0:T(8,128)(2,1)S(1)}) custom-call(s32[2]{0:T(128)S(1)} %get-tuple-element.453.bits_ref, bf16[3072,768]{1,0:T(8,128)(2,1)} %bitcast.30, bf16[3072,768]{1,0:T(8,128)(2,1)} %collective-permute-done.8.got_at), custom_call_target="tpu_custom_call" | custom-call | flops 1 | bytes 1 | tf_op jit(solution)/shard_map/scatter_first/pallas_call | solution.py:872
  126.9 36.0 %attention_backward.1 = (bf16[1024,768]{1,0:T(8,128)(2,1)}, bf16[1024,768]{1,0:T(8,128)(2,1)}, bf16[1024,768]{1,0:T(8,128)(2,1)}) custom-call(bf16[12,1024,128]{2,1,0:T(8,128)(2,1)} %get-tuple-element.261.query_ref, bf16[1024,768]{1,0:T(8,128)(2,1)S(1)} %convolution_convert_fusion.k_ref, bf16[1024,768]{1,0:T(8,128)(2,1)S(1)} %copy-done.2, ...), custom_call_target="tpu_custom_call" | custom-call | flops 1 | bytes 1 | tf_op jit(solution)/shard_map/attention_backward/pallas_call | solution.py:168
  166.9 8.0 %weight_halves.1 = (bf16[1536,768]{1,0:T(8,128)(2,1)S(1)}, bf16[1536,768]{1,0:T(8,128)(2,1)S(1)}, f32[16,768]{1,0:T(8,128)S(1)}) custom-call(s32[1]{0:T(128)} %bitcast.1.which_ref.core_ref, f32[8,768]{1,0:T(8,128)S(1)} %copy-done.6, f32[8,768]{1,0:T(8,128)S(1)} %copy-done.5, f32[8,512]{1,0:T(8,128)S(1)} %copy-done.8, f32[8,512]{1,0:T(8,128)S(1)} %copy-done.7, ...), custom_call_target="tpu_custom_call" | custom-call | flops 1 | bytes 1 | tf_op jit(solution)/shard_map/weight_halves/pallas_call | solution.py:631
  179.7 6.6 %input_grad.1 = (bf16[256,768]{1,0:T(8,128)(2,1)S(1)}, bf16[256,768]{1,0:T(8,128)(2,1)S(1)}, bf16[256,768]{1,0:T(8,128)(2,1)S(1)}, bf16[256,768]{1,0:T(8,128)(2,1)S(1)}) custom-call(bf16[1024,768]{1,0:T(8,128)(2,1)} %get-tuple-element.287.refs_5_.refs_0_, bf16[1024,768]{1,0:T(8,128)(2,1)} %get-tuple-element.310.refs_1_, bf16[768,768]{1,0:T(8,128)(2,1)} %refs_2_.1, ...), custom_call_target="tpu_custom_call" | custom-call | flops 1 | bytes 1 | tf_op jit(solution)/shard_map/input_grad/pallas_call | solution.py:676
  191.3 3.2 %place.2 = bf16[4,256,768]{2,1,0:T(8,128)(2,1)} custom-call(s32[1]{0:T(128)} %bitcast.at_ref, bf16[256,768]{1,0:T(8,128)(2,1)} %copy-done.12, bf16[256,768]{1,0:T(8,128)(2,1)} %copy-done.13, bf16[256,768]{1,0:T(8,128)(2,1)} %copy-done.14, bf16[256,768]{1,0:T(8,128)(2,1)} %copy-done.15), custom_call_target="tpu_custom_call" | custom-call | flops 1 | bytes 1 | tf_op jit(solution)/shard_map/place/pallas_call | solution.py:774
  194.6 9.5 %collective-permute-done.21.refs_3_ = bf16[64,768]{1,0:T(8,128)(2,1)S(1)} collective-permute-done((bf16[64,768]{1,0:T(8,128)(2,1)S(1)}, bf16[64,768]{1,0:T(8,128)(2,1)S(1)}, u32[]{:S(2)}, u32[]{:S(2)}) %collective-permute-start.21) | collective-permute-done | bytes 98336 | tf_op jit(solution)/shard_map/ppermute | solution.py:1029
  211.0 5.8 %collective-permute-done.28.refs_3_ = bf16[256,768]{1,0:T(8,128)(2,1)S(1)} collective-permute-done((bf16[256,768]{1,0:T(8,128)(2,1)S(1)}, bf16[256,768]{1,0:T(8,128)(2,1)S(1)}, u32[]{:S(2)}, u32[]{:S(2)}) %collective-permute-start.28) | collective-permute-done | bytes 393248 | tf_op jit(solution)/shard_map/ppermute | solution.py:1182
  216.8 7.5 %collective-permute-done.24.refs_3_ = bf16[64,768]{1,0:T(8,128)(2,1)S(1)} collective-permute-done((bf16[64,768]{1,0:T(8,128)(2,1)S(1)}, bf16[64,768]{1,0:T(8,128)(2,1)S(1)}, u32[]{:S(2)}, u32[]{:S(2)}) %collective-permute-start.24) | collective-permute-done | bytes 98336 | tf_op jit(solution)/shard_map/ppermute | solution.py:1029
  227.8 5.0 %collective-permute-done.30.refs_3_ = bf16[128,768]{1,0:T(8,128)(2,1)S(1)} collective-permute-done((bf16[128,768]{1,0:T(8,128)(2,1)S(1)}, bf16[128,768]{1,0:T(8,128)(2,1)S(1)}, u32[]{:S(2)}, u32[]{:S(2)}) %collective-permute-start.30) | collective-permute-done | bytes 196640 | tf_op jit(solution)/shard_map/ppermute | solution.py:1029
  232.8 3.0 collective-permute-done.31.refs_1_
  240.7 8.6 %collective-permute-done.35.refs_2_ = bf16[256,768]{1,0:T(8,128)(2,1)S(1)} collective-permute-done((bf16[256,768]{1,0:T(8,128)(2,1)S(1)}, bf16[256,768]{1,0:T(8,128)(2,1)S(1)}, u32[]{:S(2)}, u32[]{:S(2)}) %collective-permute-start.35) | collective-permute-done | bytes 393248 | tf_op jit(solution)/shard_map/ppermute | solution.py:1182
  249.3 4.8 %collective-permute-done.34.refs_1_ = bf16[208,768]{1,0:T(8,128)(2,1)S(1)} collective-permute-done((bf16[208,768]{1,0:T(8,128)(2,1)S(1)}, bf16[208,768]{1,0:T(8,128)(2,1)S(1)}, u32[]{:S(2)}, u32[]{:S(2)}) %collective-permute-start.34) | collective-permute-done | bytes 319520 | tf_op jit(solution)/shard_map/ppermute | solution.py:1029
  261.3 7.8 %collective-permute-done.38.refs_1_ = bf16[208,768]{1,0:T(8,128)(2,1)S(1)} collective-permute-done((bf16[208,768]{1,0:T(8,128)(2,1)S(1)}, bf16[208,768]{1,0:T(8,128)(2,1)S(1)}, u32[]{:S(2)}, u32[]{:S(2)}) %collective-permute-start.38) | collective-permute-done | bytes 319520 | tf_op jit(solution)/shard_map/ppermute | solution.py:1029
  274.0 9.5 %collective-permute-done.40.refs_7_ = bf16[256,768]{1,0:T(8,128)(2,1)S(1)} collective-permute-done((bf16[256,768]{1,0:T(8,128)(2,1)S(1)}, bf16[256,768]{1,0:T(8,128)(2,1)S(1)}, u32[]{:S(2)}, u32[]{:S(2)}) %collective-permute-start.40) | collective-permute-done | bytes 393248 | tf_op jit(solution)/shard_map/ppermute | solution.py:1029
  285.6 5.2 %feed_out.2 = (f32[3072,768]{1,0:T(8,128)}, f32[768,3072]{1,0:T(8,128)}) custom-call(s32[1]{0:T(128)} %bitcast.1.which_ref.core_ref, bf16[3072,768]{1,0:T(8,128)(2,1)S(1)} %join_local.11.half_ref), custom_call_target="tpu_custom_call" | custom-call | flops 1 | bytes 1 | tf_op jit(solution)/shard_map/feed_out/pallas_call | solution.py:706
  290.7 10.4 %collective-permute-done.43.refs_1_ = bf16[784,768]{1,0:T(8,128)(2,1)S(1)} collective-permute-done((bf16[784,768]{1,0:T(8,128)(2,1)S(1)}, bf16[784,768]{1,0:T(8,128)(2,1)S(1)}, u32[]{:S(2)}, u32[]{:S(2)}) %collective-permute-start.43) | collective-permute-done | bytes 1204256 | tf_op jit(solution)/shard_map/ppermute | solution.py:1029
  301.3 2.6 attn_out.2
  304.0 5.1 %feed_out.3 = (f32[3072,768]{1,0:T(8,128)}, f32[768,3072]{1,0:T(8,128)}) custom-call(s32[1]{0:T(128)S(6)} %sub.2.which_ref, bf16[3072,768]{1,0:T(8,128)(2,1)S(1)} %collective-permute-done.42.half_ref, f32[3072,768]{1,0:T(8,128)} %get-tuple-element.437.refs_0_, f32[768,3072]{1,0:T(8,128)} %get-tuple-element.438.refs_1_), custom_call_target="tpu_custom_call", output_to_operand_aliasing={{0}: (2, {}), {1}: (3, {})} | custom-call | flops 1 | bytes 1 | tf_op jit(solution)/shard_map/feed_out/pallas_call | solution.py:706
  (172 shorter events, 72.7 us)
Async XLA Ops:
  6.0 18.9 %collective-permute-start.3 = (bf16[272,768]{1,0:T(8,128)(2,1)S(1)}, bf16[272,768]{1,0:T(8,128)(2,1)S(1)}, u32[]{:S(2)}, u32[]{:S(2)}) collective-permute-start(bf16[272,768]{1,0:T(8,128)(2,1)S(1)} %get-tuple-element.232), channel_id=1, source_target_pairs={{0,3},{1,2},{2,1},{3,0},{4,7},{5,6},{6,5},{7,4},{8,11},{9,10},{10,... | collective-permute-start | bytes 1253384 | tf_op jit(solution)/shard_map/ppermute | solution.py:1211
  26.5 28.7 %collective-permute-start.7 = (bf16[256,768]{1,0:T(8,128)(2,1)S(1)}, bf16[256,768]{1,0:T(8,128)(2,1)S(1)}, u32[]{:S(2)}, u32[]{:S(2)}) collective-permute-start(bf16[256,768]{1,0:T(8,128)(2,1)S(1)} %get-tuple-element.449), channel_id=1, source_target_pairs={{0,3},{1,2},{2,1},{3,0},{4,7},{5,6},{6,5},{7,4},{8,11},{9,10},{10,... | collective-permute-start | bytes 1179656 | tf_op jit(solution)/shard_map/ppermute | solution.py:1170
  28.0 27.2 %collective-permute-start.6 = (bf16[256,768]{1,0:T(8,128)(2,1)S(1)}, bf16[256,768]{1,0:T(8,128)(2,1)S(1)}, u32[]{:S(2)}, u32[]{:S(2)}) collective-permute-start(bf16[256,768]{1,0:T(8,128)(2,1)S(1)} %get-tuple-element.450), channel_id=1, source_target_pairs={{0,2},{1,3},{2,0},{3,1},{4,6},{5,7},{6,4},{7,5},{8,10},{9,11},{10,... | collective-permute-start | bytes 1179656 | tf_op jit(solution)/shard_map/ppermute | solution.py:1170
  28.3 26.9 %collective-permute-start.5 = (bf16[256,768]{1,0:T(8,128)(2,1)S(1)}, bf16[256,768]{1,0:T(8,128)(2,1)S(1)}, u32[]{:S(2)}, u32[]{:S(2)}) collective-permute-start(bf16[256,768]{1,0:T(8,128)(2,1)S(1)} %get-tuple-element.451), channel_id=1, source_target_pairs={{0,1},{1,0},{2,3},{3,2},{4,5},{5,4},{6,7},{7,6},{8,9},{9,8},{10,11... | collective-permute-start | bytes 1179656 | tf_op jit(solution)/shard_map/ppermute | solution.py:1170
  28.4 26.8 %collective-permute-start.4 = (bf16[256,768]{1,0:T(8,128)(2,1)S(1)}, bf16[256,768]{1,0:T(8,128)(2,1)S(1)}, u32[]{:S(2)}, u32[]{:S(2)}) collective-permute-start(bf16[256,768]{1,0:T(8,128)(2,1)S(1)} %get-tuple-element.452), channel_id=1, source_target_pairs={{0,0},{1,1},{2,2},{3,3},{4,4},{5,5},{6,6},{7,7},{8,8},{9,9},{10,10... | collective-permute-start | bytes 1179656 | tf_op jit(solution)/shard_map/ppermute | solution.py:1170
  95.4 23.2 %collective-permute-start.8 = (bf16[3072,768]{1,0:T(8,128)(2,1)}, bf16[3072,768]{1,0:T(8,128)(2,1)}, u32[]{:S(2)}, u32[]{:S(2)}) collective-permute-start(bf16[3072,768]{1,0:T(8,128)(2,1)} %bitcast.34), channel_id=1, source_target_pairs={{0,1},{1,0},{2,3},{3,2},{4,5},{5,4},{6,7},{7,6},{8,9},{9,8},{10,11... | collective-permute-start | bytes 14155784 | tf_op jit(solution)/shard_map/ppermute | solution.py:1029
  95.8 22.7 %collective-permute-start.9 = (bf16[256,768]{1,0:T(8,128)(2,1)}, bf16[256,768]{1,0:T(8,128)(2,1)S(1)}, u32[]{:S(2)}, u32[]{:S(2)}) collective-permute-start(bf16[256,768]{1,0:T(8,128)(2,1)} %get-tuple-element.249), channel_id=1, source_target_pairs={{0,0},{1,1},{2,2},{3,3},{4,4},{5,5},{6,6},{7,7},{8,8},{9,9},{10,10... | collective-permute-start | bytes 1179656 | tf_op jit(solution)/shard_map/ppermute | solution.py:1182
  96.8 21.7 %collective-permute-start.10 = (bf16[256,768]{1,0:T(8,128)(2,1)}, bf16[256,768]{1,0:T(8,128)(2,1)S(1)}, u32[]{:S(2)}, u32[]{:S(2)}) collective-permute-start(bf16[256,768]{1,0:T(8,128)(2,1)} %get-tuple-element.250), channel_id=1, source_target_pairs={{1,0},{0,1},{3,2},{2,3},{5,4},{4,5},{7,6},{6,7},{9,8},{8,9},{11,10... | collective-permute-start | bytes 1179656 | tf_op jit(solution)/shard_map/ppermute | solution.py:1182
  97.0 21.6 %collective-permute-start.11 = (bf16[256,768]{1,0:T(8,128)(2,1)}, bf16[256,768]{1,0:T(8,128)(2,1)S(1)}, u32[]{:S(2)}, u32[]{:S(2)}) collective-permute-start(bf16[256,768]{1,0:T(8,128)(2,1)} %get-tuple-element.251), channel_id=1, source_target_pairs={{2,0},{3,1},{0,2},{1,3},{6,4},{7,5},{4,6},{5,7},{10,8},{11,9},{8,1... | collective-permute-start | bytes 1179656 | tf_op jit(solution)/shard_map/ppermute | solution.py:1182
  98.6 20.0 %collective-permute-start.12 = (bf16[256,768]{1,0:T(8,128)(2,1)}, bf16[256,768]{1,0:T(8,128)(2,1)S(1)}, u32[]{:S(2)}, u32[]{:S(2)}) collective-permute-start(bf16[256,768]{1,0:T(8,128)(2,1)} %get-tuple-element.252), channel_id=1, source_target_pairs={{3,0},{2,1},{1,2},{0,3},{7,4},{6,5},{5,6},{4,7},{11,8},{10,9},{9,1... | collective-permute-start | bytes 1179656 | tf_op jit(solution)/shard_map/ppermute | solution.py:1182
  123.6 39.3 %collective-permute-start.13 = (bf16[1024,768]{1,0:T(8,128)(2,1)S(1)}, bf16[1024,768]{1,0:T(8,128)(2,1)S(1)}, u32[]{:S(2)}, u32[]{:S(2)}) collective-permute-start(bf16[1024,768]{1,0:T(8,128)(2,1)S(1)} %get-tuple-element.272), channel_id=1, source_target_pairs={{0,2},{1,5},{2,0},{3,7},{4,6},{5,1},{6,4},{7,3},{8,10},{9,13},{10,... | collective-permute-start | bytes 4718600 | tf_op jit(solution)/shard_map/ppermute | solution.py:1029
  125.4 37.5 %collective-permute-start.14 = (bf16[512,768]{1,0:T(8,128)(2,1)S(1)}, bf16[512,768]{1,0:T(8,128)(2,1)S(1)}, u32[]{:S(2)}, u32[]{:S(2)}) collective-permute-start(bf16[512,768]{1,0:T(8,128)(2,1)S(1)} %get-tuple-element.274), channel_id=1, source_target_pairs={{0,8},{1,9},{2,10},{3,11},{4,12},{5,13},{6,14},{7,15},{8,0},{9,1},... | collective-permute-start | bytes 2359304 | tf_op jit(solution)/shard_map/ppermute | solution.py:1029
  187.5 16.5 %collective-permute-start.22 = (bf16[768,768]{1,0:T(8,128)(2,1)S(1)}, bf16[768,768]{1,0:T(8,128)(2,1)S(1)}, u32[]{:S(2)}, u32[]{:S(2)}) collective-permute-start(bf16[768,768]{1,0:T(8,128)(2,1)S(1)} %get-tuple-element.341), channel_id=1, source_target_pairs={{0,2},{1,5},{2,0},{3,7},{4,6},{5,1},{6,4},{7,3},{8,10},{9,13},{10,... | collective-permute-start | bytes 3538952 | tf_op jit(solution)/shard_map/ppermute | solution.py:1029
  188.4 15.7 %collective-permute-start.20 = (bf16[128,768]{1,0:T(8,128)(2,1)S(1)}, bf16[128,768]{1,0:T(8,128)(2,1)S(1)}, u32[]{:S(2)}, u32[]{:S(2)}) collective-permute-start(bf16[128,768]{1,0:T(8,128)(2,1)S(1)} %get-tuple-element.335), channel_id=1, source_target_pairs={{0,16},{1,17},{2,18},{3,19},{4,20},{5,21},{6,22},{7,23},{8,24},{9,... | collective-permute-start | bytes 589832 | tf_op jit(solution)/shard_map/ppermute | solution.py:1029
  204.3 19.9 %collective-permute-start.25 = (bf16[384,768]{1,0:T(8,128)(2,1)S(1)}, bf16[384,768]{1,0:T(8,128)(2,1)S(1)}, u32[]{:S(2)}, u32[]{:S(2)}) collective-permute-start(bf16[384,768]{1,0:T(8,128)(2,1)S(1)} %get-tuple-element.360), channel_id=1, source_target_pairs={{0,4},{1,9},{2,6},{3,11},{4,0},{5,13},{6,2},{7,15},{8,12},{9,1},{1... | collective-permute-start | bytes 1769480 | tf_op jit(solution)/shard_map/ppermute | solution.py:1029
  208.0 16.3 %collective-permute-start.23 = (bf16[128,768]{1,0:T(8,128)(2,1)S(1)}, bf16[128,768]{1,0:T(8,128)(2,1)S(1)}, u32[]{:S(2)}, u32[]{:S(2)}) collective-permute-start(bf16[128,768]{1,0:T(8,128)(2,1)S(1)} %get-tuple-element.363.refs_0_), channel_id=1, source_target_pairs={{0,16},{1,17},{2,18},{3,19},{4,20},{5,21},{6,22},{7,23},{8,24},{9,... | collective-permute-start | bytes 589832 | tf_op jit(solution)/shard_map/ppermute | solution.py:1029
  209.9 14.3 %collective-permute-start.24 = (bf16[64,768]{1,0:T(8,128)(2,1)S(1)}, bf16[64,768]{1,0:T(8,128)(2,1)S(1)}, u32[]{:S(2)}, u32[]{:S(2)}) collective-permute-start(bf16[64,768]{1,0:T(8,128)(2,1)S(1)} %get-tuple-element.365.refs_2_), channel_id=1, source_target_pairs={{0,16},{1,17},{2,18},{3,19},{4,20},{5,21},{6,22},{7,23},{8,24},{9,... | collective-permute-start | bytes 294920 | tf_op jit(solution)/shard_map/ppermute | solution.py:1029
  236.5 18.1 %collective-permute-start.32 = (bf16[512,768]{1,0:T(8,128)(2,1)S(1)}, bf16[512,768]{1,0:T(8,128)(2,1)S(1)}, u32[]{:S(2)}, u32[]{:S(2)}) collective-permute-start(bf16[512,768]{1,0:T(8,128)(2,1)S(1)} %get-tuple-element.384.refs_0_), channel_id=1, source_target_pairs={{0,4},{1,9},{2,6},{3,11},{4,0},{5,13},{6,2},{7,15},{8,12},{9,1},{1... | collective-permute-start | bytes 2359304 | tf_op jit(solution)/shard_map/ppermute | solution.py:1029
  237.9 16.7 %collective-permute-start.33 = (bf16[256,768]{1,0:T(8,128)(2,1)S(1)}, bf16[256,768]{1,0:T(8,128)(2,1)S(1)}, u32[]{:S(2)}, u32[]{:S(2)}) collective-permute-start(bf16[256,768]{1,0:T(8,128)(2,1)S(1)} %get-tuple-element.386.refs_2_), channel_id=1, source_target_pairs={{0,2},{1,3},{2,0},{3,1},{4,6},{5,7},{6,4},{7,5},{8,10},{9,11},{10,... | collective-permute-start | bytes 1179656 | tf_op jit(solution)/shard_map/ppermute | solution.py:1029
  239.3 14.7 %collective-permute-start.34 = (bf16[208,768]{1,0:T(8,128)(2,1)S(1)}, bf16[208,768]{1,0:T(8,128)(2,1)S(1)}, u32[]{:S(2)}, u32[]{:S(2)}) collective-permute-start(bf16[208,768]{1,0:T(8,128)(2,1)S(1)} %settle_local.3.refs_0_), channel_id=1, source_target_pairs={{0,16},{1,17},{2,18},{3,19},{4,20},{5,21},{6,22},{7,23},{8,24},{9,... | collective-permute-start | bytes 958472 | tf_op jit(solution)/shard_map/ppermute | solution.py:1029
  255.3 14.8 %collective-permute-start.36 = (bf16[512,768]{1,0:T(8,128)(2,1)S(1)}, bf16[512,768]{1,0:T(8,128)(2,1)S(1)}, u32[]{:S(2)}, u32[]{:S(2)}) collective-permute-start(bf16[512,768]{1,0:T(8,128)(2,1)S(1)} %get-tuple-element.398.refs_0_), channel_id=1, source_target_pairs={{0,2},{1,5},{2,0},{3,7},{4,6},{5,1},{6,4},{7,3},{8,10},{9,13},{10,... | collective-permute-start | bytes 2359304 | tf_op jit(solution)/shard_map/ppermute | solution.py:1029
  258.1 25.4 %collective-permute-start.39 = (bf16[512,768]{1,0:T(8,128)(2,1)S(1)}, bf16[512,768]{1,0:T(8,128)(2,1)S(1)}, u32[]{:S(2)}, u32[]{:S(2)}) collective-permute-start(bf16[512,768]{1,0:T(8,128)(2,1)S(1)} %get-tuple-element.403.refs_2_), channel_id=1, source_target_pairs={{0,2},{1,5},{2,0},{3,7},{4,6},{5,1},{6,4},{7,3},{8,10},{9,13},{10,... | collective-permute-start | bytes 2359304 | tf_op jit(solution)/shard_map/ppermute | solution.py:1029
  284.4 16.7 %collective-permute-start.42 = (bf16[3072,768]{1,0:T(8,128)(2,1)S(1)}, bf16[3072,768]{1,0:T(8,128)(2,1)S(1)}, u32[]{:S(2)}, u32[]{:S(2)}) collective-permute-start(bf16[3072,768]{1,0:T(8,128)(2,1)S(1)} %join_local.11.half_ref), channel_id=1, source_target_pairs={{0,1},{1,0},{2,3},{3,2},{4,5},{5,4},{6,7},{7,6},{8,9},{9,8},{10,11... | collective-permute-start | bytes 14155784 | tf_op jit(solution)/shard_map/ppermute | solution.py:1029
  284.5 16.5 %collective-permute-start.43 = (bf16[784,768]{1,0:T(8,128)(2,1)S(1)}, bf16[784,768]{1,0:T(8,128)(2,1)S(1)}, u32[]{:S(2)}, u32[]{:S(2)}) collective-permute-start(bf16[784,768]{1,0:T(8,128)(2,1)S(1)} %join_local.12.refs_0_), channel_id=1, source_target_pairs={{0,2},{1,5},{2,0},{3,7},{4,6},{5,1},{6,4},{7,3},{8,10},{9,13},{10,... | collective-permute-start | bytes 3612680 | tf_op jit(solution)/shard_map/ppermute | solution.py:1029
  (47 other events, 355.7 us)

commit v3 on v2

--- a/solution.py
+++ b/solution.py
@@ -244,14 +244,21 @@
 ):
     upstream_refs = refs[:held]
     hat_out, scale_ref, normed_out, active_t_ref, slope_ref = refs[held : held + 5]
-    d_down_ref, sums_ref = refs[held + 5 : held + 7]
-    out_refs = refs[held + 7 : 2 * held + 7]
-    total, hat_ref, normed_ref, sems = refs[2 * held + 7 :]
+    d_down_out, sums_ref = refs[held + 5 : held + 7]
+    outs = refs[held + 7 : 2 * held + 7]
+    total, hat_ref, normed_ref, d_down_ref, out_ref, sems = refs[2 * held + 7 :]
     block = total.shape[0] // held
     early = [
         pltpu.make_async_copy(hat_ref, hat_out, sems.at[0]),
         pltpu.make_async_copy(normed_ref, normed_out, sems.at[1]),
     ]
+    late = []
+    for index, out in enumerate(outs):
+        rows = pl.ds(index * block, block)
+        late.append(pltpu.make_async_copy(out_ref.at[rows], out, sems.at[2 + 2 * index]))
+        late.append(
+            pltpu.make_async_copy(d_down_ref.at[rows], d_down_out.at[rows], sems.at[3 + 2 * index])
+        )
     step = pl.program_id(0)
     tokens = total.shape[0]
     pieces = [slice(start, start + block) for start in range(0, tokens, block)]
@@ -287,17 +294,19 @@
         d_gain = jnp.zeros((1, total.shape[1]), F32)
         d_shift = d_gain
         d_bias = d_gain
-        for here, upstream_ref, out_ref in zip(pieces, upstream_refs, out_refs):
+        for index, (here, upstream_ref) in enumerate(zip(pieces, upstream_refs)):
             hat, scale = normalise(total[here, :])
-            out_ref[...] = (gain * hat + shift_two_ref[...].astype(F32)).astype(BF16)
+            out_ref[here, :] = (gain * hat + shift_two_ref[...].astype(F32)).astype(BF16)
+            late[2 * index].start()
             upstream = upstream_ref[...].astype(F32)
             d_gain += jnp.sum(upstream * hat, 0, keepdims=True)
             d_shift += jnp.sum(upstream, 0, keepdims=True)
             d_down = norm_back(upstream, hat, scale, gain).astype(BF16)
             d_down_ref[here, :] = d_down
+            late[2 * index + 1].start()
             d_bias += jnp.sum(d_down.astype(F32), 0, keepdims=True)
         sums_ref[...] = stack_rows([d_gain, d_shift, d_bias])
-        for copy in early:
+        for copy in early + late:
             copy.wait()
 
 
@@ -344,10 +353,10 @@
             pl.BlockSpec(memory_space=pl.ANY),
             pl.BlockSpec((block, tokens), lambda i: (i, 0)),
             pl.BlockSpec((tokens, block), lambda i: (0, i)),
-            fixed(tokens, width),
+            pl.BlockSpec(memory_space=pl.ANY),
             fixed(8, width),
         ]
-        + [fixed(piece, width)] * held,
+        + [pl.BlockSpec(memory_space=pl.ANY)] * held,
         out_shape=hbm_shapes(
             ((tokens, width), BF16),
             ((tokens, PAIR), F32),
@@ -356,13 +365,15 @@
             ((tokens, units), BF16),
             ((tokens, width), BF16),
             ((8, width), F32),
-        )
-        + shapes(*[((piece, width), BF16)] * held),
+            *[((piece, width), BF16)] * held,
+        ),
         scratch_shapes=[
             pltpu.VMEM((tokens, width), F32),
             pltpu.VMEM((tokens, width), BF16),
             pltpu.VMEM((tokens, width), BF16),
-            pltpu.SemaphoreType.DMA((2,)),
+            pltpu.VMEM((tokens, width), BF16),
+            pltpu.VMEM((tokens, width), BF16),
+            pltpu.SemaphoreType.DMA((2 + 2 * held,)),
         ],
         compiler_params=pltpu.CompilerParams(vmem_limit_bytes=36 * 2**20),
         cost_estimate=BRIEF,

time: 317 us -> 317 us (level)
  no operation moved by 1% of the time
where the time goes in v3:
time: 317 us; the launch traced here: 313 us
  Pallas kernels  169 us (53%)
  waiting for transfers between devices  88.3 us (28%)
  starting transfers between devices  41.9 us (13%)
  local copies, waits for them, and re-layouts  6.34 us (2%)
  matrix products  4.18 us (1%)
    ppermute x29, waiting for transfers between devices, swap(): return lax.ppermute(values, ('rows', 'seq'), self.pairs)  60.8 us
    pallas_call x2, Pallas kernels, feed_back(): pl.pallas_call(functools.partial(feed_back_kernel, steps=steps, block=min...  36.4 us
    pallas_call x1, Pallas kernels, attention_backward(): pl.pallas_call(functools.partial(backward_kernel, block=min(512, keys)),...  36 us
    ppermute x29, starting transfers between devices, swap(): return lax.ppermute(values, ('rows', 'seq'), self.pairs)  31.6 us
    pallas_call x1, Pallas kernels, feed_forward(): pl.pallas_call(functools.partial(feed_forward_kernel, steps=steps, held=h...  23.5 us
    pallas_call x1, Pallas kernels, attention_forward(): pl.pallas_call(functools.partial(forward_kernel, block=min(512, queries))...  22.4 us
    ppermute x8, waiting for transfers between devices, send_pieces(): lax.ppermute(values[part], 'seq', trade(False, part))  14.5 us
    ppermute x4, waiting for transfers between devices, body(): lax.ppermute(value, 'seq', trade(True, part))  13.1 us
  transfers between devices with their start and end apart: 45, of which 16 were waited for; matrix products, arithmetic and copies ran while one was open for 3% of the time, Pallas kernels for 36%

profile of v3, /device:TPU:0, one launch (start us, length us, event | category | flops | bytes accessed | tf_op | source)
XLA Modules:
  0.0 313.2 jit_solution(10175928143626227621)
XLA Ops:
  11.9 4.6 %collective-permute-done.2.refs_2_ = bf16[272,768]{1,0:T(8,128)(2,1)S(1)} collective-permute-done((bf16[272,768]{1,0:T(8,128)(2,1)S(1)}, bf16[272,768]{1,0:T(8,128)(2,1)S(1)}, u32[]{:S(2)}, u32[]{:S(2)}) %collective-permute-start.2) | collective-permute-done | bytes 417824 | tf_op jit(solution)/shard_map/ppermute | solution.py:1222
  16.5 8.4 %collective-permute-done.3.refs_3_ = bf16[272,768]{1,0:T(8,128)(2,1)S(1)} collective-permute-done((bf16[272,768]{1,0:T(8,128)(2,1)S(1)}, bf16[272,768]{1,0:T(8,128)(2,1)S(1)}, u32[]{:S(2)}, u32[]{:S(2)}) %collective-permute-start.3) | collective-permute-done | bytes 417824 | tf_op jit(solution)/shard_map/ppermute | solution.py:1222
  32.8 22.4 %attention_forward.1 = (bf16[1024,768]{1,0:T(8,128)(2,1)}, bf16[12,1024,128]{2,1,0:T(8,128)(2,1)}) custom-call(bf16[1024,768]{1,0:T(8,128)(2,1)S(1)} %multiply_convert_fusion.q_ref, bf16[1024,768]{1,0:T(8,128)(2,1)S(1)} %convolution_convert_fusion.k_ref, bf16[1024,768]{1,0:T(8,128)(2,1)S(1)} %add_convert_fusion.v_ref, bf16[1024,128]{1,0:T(8,128)(2,1)S(1)} %copy-done.3, ...), custom_call_target="tpu_custom_call" | custom-call | flops 1 | bytes 1 | tf_op jit(solution)/shard_map/attention_forward/pallas_call | solution.py:90
  55.2 23.5 %feed_forward.1 = (bf16[1024,768]{1,0:T(8,128)(2,1)}, f32[1024,128]{1,0:T(8,128)}, bf16[1024,768]{1,0:T(8,128)(2,1)}, bf16[3072,1024]{1,0:T(8,128)(2,1)}, bf16[1...) custom-call(bf16[1024,768]{1,0:T(8,128)(2,1)S(1)} %copy-done, ...), custom_call_target="tpu_custom_call" | custom-call | flops 1 | bytes 1 | tf_op jit(solution)/shard_map/feed_forward/pallas_call | solution.py:336
  78.7 16.7 %feed_back.1 = (bf16[2,1536,768]{2,1,0:T(8,128)(2,1)}, f32[8,512]{1,0:T(8,128)}, bf16[1024,768]{1,0:T(8,128)(2,1)}) custom-call(s32[1]{0:T(128)S(6)} %sub.2.which_ref, bf16[1024,768]{1,0:T(8,128)(2,1)} %get-tuple-element.239.d_down_ref, bf16[1024,3072]{1,0:T(8,128)(2,1)} %get-tuple-element.240.slope_ref, bf16[3072,1024]{1,0:T(8,128)(2,1)} %get-tuple-element.241.active_t_ref, ...), custom_call_target="tpu_custom_call" | custom-call | flops 1 | bytes 1 | tf_op jit(solution)/shard_map/feed_back/pallas_call | solution.py:507
  98.7 19.8 %feed_back_last.1 = (bf16[2,1536,768]{2,1,0:T(8,128)(2,1)}, f32[8,512]{1,0:T(8,128)}, bf16[1024,768]{1,0:T(8,128)(2,1)}, bf16[1024,768]{1,0:T(8,128)(2,1)}, f32[8,768]{1,0:T(8,128)}) custom-call(s32[1]{0:T(128)} %bitcast.1.which_ref.core_ref, bf16[1024,768]{1,0:T(8,128)(2,1)} %get-tuple-element.239.d_down_ref, ...), custom_call_target="tpu_custom_call" | custom-call | flops 1 | bytes 1 | tf_op jit(solution)/shard_map/feed_back_last/pallas_call | solution.py:507
  118.6 4.9 %scatter_first.1 = (bf16[1024,768]{1,0:T(8,128)(2,1)S(1)}, bf16[1024,768]{1,0:T(8,128)(2,1)S(1)}, bf16[512,768]{1,0:T(8,128)(2,1)S(1)}, bf16[512,768]{1,0:T(8,128)(2,1)S(1)}) custom-call(s32[2]{0:T(128)S(1)} %get-tuple-element.453.bits_ref, bf16[3072,768]{1,0:T(8,128)(2,1)} %bitcast.30, bf16[3072,768]{1,0:T(8,128)(2,1)} %collective-permute-done.8.got_at), custom_call_target="tpu_custom_call" | custom-call | flops 1 | bytes 1 | tf_op jit(solution)/shard_map/scatter_first/pallas_call | solution.py:883
  126.9 36.0 %attention_backward.1 = (bf16[1024,768]{1,0:T(8,128)(2,1)}, bf16[1024,768]{1,0:T(8,128)(2,1)}, bf16[1024,768]{1,0:T(8,128)(2,1)}) custom-call(bf16[12,1024,128]{2,1,0:T(8,128)(2,1)} %get-tuple-element.261.query_ref, bf16[1024,768]{1,0:T(8,128)(2,1)S(1)} %convolution_convert_fusion.k_ref, bf16[1024,768]{1,0:T(8,128)(2,1)S(1)} %copy-done.2, ...), custom_call_target="tpu_custom_call" | custom-call | flops 1 | bytes 1 | tf_op jit(solution)/shard_map/attention_backward/pallas_call | solution.py:168
  166.8 8.0 %weight_halves.1 = (bf16[1536,768]{1,0:T(8,128)(2,1)S(1)}, bf16[1536,768]{1,0:T(8,128)(2,1)S(1)}, f32[16,768]{1,0:T(8,128)S(1)}) custom-call(s32[1]{0:T(128)} %bitcast.1.which_ref.core_ref, f32[8,768]{1,0:T(8,128)S(1)} %copy-done.6, f32[8,768]{1,0:T(8,128)S(1)} %copy-done.5, f32[8,512]{1,0:T(8,128)S(1)} %copy-done.8, f32[8,512]{1,0:T(8,128)S(1)} %copy-done.7, ...), custom_call_target="tpu_custom_call" | custom-call | flops 1 | bytes 1 | tf_op jit(solution)/shard_map/weight_halves/pallas_call | solution.py:642
  179.6 6.6 %input_grad.1 = (bf16[256,768]{1,0:T(8,128)(2,1)S(1)}, bf16[256,768]{1,0:T(8,128)(2,1)S(1)}, bf16[256,768]{1,0:T(8,128)(2,1)S(1)}, bf16[256,768]{1,0:T(8,128)(2,1)S(1)}) custom-call(bf16[1024,768]{1,0:T(8,128)(2,1)} %get-tuple-element.287.refs_5_.refs_0_, bf16[1024,768]{1,0:T(8,128)(2,1)} %get-tuple-element.310.refs_1_, bf16[768,768]{1,0:T(8,128)(2,1)} %refs_2_.1, ...), custom_call_target="tpu_custom_call" | custom-call | flops 1 | bytes 1 | tf_op jit(solution)/shard_map/input_grad/pallas_call | solution.py:687
  191.2 3.2 %place.2 = bf16[4,256,768]{2,1,0:T(8,128)(2,1)} custom-call(s32[1]{0:T(128)} %bitcast.at_ref, bf16[256,768]{1,0:T(8,128)(2,1)} %copy-done.12, bf16[256,768]{1,0:T(8,128)(2,1)} %copy-done.13, bf16[256,768]{1,0:T(8,128)(2,1)} %copy-done.14, bf16[256,768]{1,0:T(8,128)(2,1)} %copy-done.15), custom_call_target="tpu_custom_call" | custom-call | flops 1 | bytes 1 | tf_op jit(solution)/shard_map/place/pallas_call | solution.py:785
  194.5 9.5 %collective-permute-done.21.refs_3_ = bf16[64,768]{1,0:T(8,128)(2,1)S(1)} collective-permute-done((bf16[64,768]{1,0:T(8,128)(2,1)S(1)}, bf16[64,768]{1,0:T(8,128)(2,1)S(1)}, u32[]{:S(2)}, u32[]{:S(2)}) %collective-permute-start.21) | collective-permute-done | bytes 98336 | tf_op jit(solution)/shard_map/ppermute | solution.py:1040
  210.9 5.8 %collective-permute-done.28.refs_3_ = bf16[256,768]{1,0:T(8,128)(2,1)S(1)} collective-permute-done((bf16[256,768]{1,0:T(8,128)(2,1)S(1)}, bf16[256,768]{1,0:T(8,128)(2,1)S(1)}, u32[]{:S(2)}, u32[]{:S(2)}) %collective-permute-start.28) | collective-permute-done | bytes 393248 | tf_op jit(solution)/shard_map/ppermute | solution.py:1193
  216.7 7.5 %collective-permute-done.24.refs_3_ = bf16[64,768]{1,0:T(8,128)(2,1)S(1)} collective-permute-done((bf16[64,768]{1,0:T(8,128)(2,1)S(1)}, bf16[64,768]{1,0:T(8,128)(2,1)S(1)}, u32[]{:S(2)}, u32[]{:S(2)}) %collective-permute-start.24) | collective-permute-done | bytes 98336 | tf_op jit(solution)/shard_map/ppermute | solution.py:1040
  227.8 5.0 %collective-permute-done.30.refs_3_ = bf16[128,768]{1,0:T(8,128)(2,1)S(1)} collective-permute-done((bf16[128,768]{1,0:T(8,128)(2,1)S(1)}, bf16[128,768]{1,0:T(8,128)(2,1)S(1)}, u32[]{:S(2)}, u32[]{:S(2)}) %collective-permute-start.30) | collective-permute-done | bytes 196640 | tf_op jit(solution)/shard_map/ppermute | solution.py:1040
  232.8 3.0 collective-permute-done.31.refs_1_
  240.6 8.6 %collective-permute-done.35.refs_2_ = bf16[256,768]{1,0:T(8,128)(2,1)S(1)} collective-permute-done((bf16[256,768]{1,0:T(8,128)(2,1)S(1)}, bf16[256,768]{1,0:T(8,128)(2,1)S(1)}, u32[]{:S(2)}, u32[]{:S(2)}) %collective-permute-start.35) | collective-permute-done | bytes 393248 | tf_op jit(solution)/shard_map/ppermute | solution.py:1193
  249.2 4.8 %collective-permute-done.34.refs_1_ = bf16[208,768]{1,0:T(8,128)(2,1)S(1)} collective-permute-done((bf16[208,768]{1,0:T(8,128)(2,1)S(1)}, bf16[208,768]{1,0:T(8,128)(2,1)S(1)}, u32[]{:S(2)}, u32[]{:S(2)}) %collective-permute-start.34) | collective-permute-done | bytes 319520 | tf_op jit(solution)/shard_map/ppermute | solution.py:1040
  261.2 7.8 %collective-permute-done.38.refs_1_ = bf16[208,768]{1,0:T(8,128)(2,1)S(1)} collective-permute-done((bf16[208,768]{1,0:T(8,128)(2,1)S(1)}, bf16[208,768]{1,0:T(8,128)(2,1)S(1)}, u32[]{:S(2)}, u32[]{:S(2)}) %collective-permute-start.38) | collective-permute-done | bytes 319520 | tf_op jit(solution)/shard_map/ppermute | solution.py:1040
  273.9 9.5 %collective-permute-done.40.refs_7_ = bf16[256,768]{1,0:T(8,128)(2,1)S(1)} collective-permute-done((bf16[256,768]{1,0:T(8,128)(2,1)S(1)}, bf16[256,768]{1,0:T(8,128)(2,1)S(1)}, u32[]{:S(2)}, u32[]{:S(2)}) %collective-permute-start.40) | collective-permute-done | bytes 393248 | tf_op jit(solution)/shard_map/ppermute | solution.py:1040
  285.5 5.2 %feed_out.2 = (f32[3072,768]{1,0:T(8,128)}, f32[768,3072]{1,0:T(8,128)}) custom-call(s32[1]{0:T(128)} %bitcast.1.which_ref.core_ref, bf16[3072,768]{1,0:T(8,128)(2,1)S(1)} %join_local.11.half_ref), custom_call_target="tpu_custom_call" | custom-call | flops 1 | bytes 1 | tf_op jit(solution)/shard_map/feed_out/pallas_call | solution.py:717
  290.6 10.4 %collective-permute-done.43.refs_1_ = bf16[784,768]{1,0:T(8,128)(2,1)S(1)} collective-permute-done((bf16[784,768]{1,0:T(8,128)(2,1)S(1)}, bf16[784,768]{1,0:T(8,128)(2,1)S(1)}, u32[]{:S(2)}, u32[]{:S(2)}) %collective-permute-start.43) | collective-permute-done | bytes 1204256 | tf_op jit(solution)/shard_map/ppermute | solution.py:1040
  301.2 2.6 attn_out.2
  303.9 5.1 %feed_out.3 = (f32[3072,768]{1,0:T(8,128)}, f32[768,3072]{1,0:T(8,128)}) custom-call(s32[1]{0:T(128)S(6)} %sub.2.which_ref, bf16[3072,768]{1,0:T(8,128)(2,1)S(1)} %collective-permute-done.42.half_ref, f32[3072,768]{1,0:T(8,128)} %get-tuple-element.437.refs_0_, f32[768,3072]{1,0:T(8,128)} %get-tuple-element.438.refs_1_), custom_call_target="tpu_custom_call", output_to_operand_aliasing={{0}: (2, {}), {1}: (3, {})} | custom-call | flops 1 | bytes 1 | tf_op jit(solution)/shard_map/feed_out/pallas_call | solution.py:717
  (172 shorter events, 72.7 us)
Async XLA Ops:
  6.0 18.9 %collective-permute-start.3 = (bf16[272,768]{1,0:T(8,128)(2,1)S(1)}, bf16[272,768]{1,0:T(8,128)(2,1)S(1)}, u32[]{:S(2)}, u32[]{:S(2)}) collective-permute-start(bf16[272,768]{1,0:T(8,128)(2,1)S(1)} %get-tuple-element.232), channel_id=1, source_target_pairs={{0,3},{1,2},{2,1},{3,0},{4,7},{5,6},{6,5},{7,4},{8,11},{9,10},{10,... | collective-permute-start | bytes 1253384 | tf_op jit(solution)/shard_map/ppermute | solution.py:1222
  26.5 28.7 %collective-permute-start.7 = (bf16[256,768]{1,0:T(8,128)(2,1)S(1)}, bf16[256,768]{1,0:T(8,128)(2,1)S(1)}, u32[]{:S(2)}, u32[]{:S(2)}) collective-permute-start(bf16[256,768]{1,0:T(8,128)(2,1)S(1)} %get-tuple-element.449), channel_id=1, source_target_pairs={{0,3},{1,2},{2,1},{3,0},{4,7},{5,6},{6,5},{7,4},{8,11},{9,10},{10,... | collective-permute-start | bytes 1179656 | tf_op jit(solution)/shard_map/ppermute | solution.py:1181
  28.0 27.2 %collective-permute-start.6 = (bf16[256,768]{1,0:T(8,128)(2,1)S(1)}, bf16[256,768]{1,0:T(8,128)(2,1)S(1)}, u32[]{:S(2)}, u32[]{:S(2)}) collective-permute-start(bf16[256,768]{1,0:T(8,128)(2,1)S(1)} %get-tuple-element.450), channel_id=1, source_target_pairs={{0,2},{1,3},{2,0},{3,1},{4,6},{5,7},{6,4},{7,5},{8,10},{9,11},{10,... | collective-permute-start | bytes 1179656 | tf_op jit(solution)/shard_map/ppermute | solution.py:1181
  28.3 26.9 %collective-permute-start.5 = (bf16[256,768]{1,0:T(8,128)(2,1)S(1)}, bf16[256,768]{1,0:T(8,128)(2,1)S(1)}, u32[]{:S(2)}, u32[]{:S(2)}) collective-permute-start(bf16[256,768]{1,0:T(8,128)(2,1)S(1)} %get-tuple-element.451), channel_id=1, source_target_pairs={{0,1},{1,0},{2,3},{3,2},{4,5},{5,4},{6,7},{7,6},{8,9},{9,8},{10,11... | collective-permute-start | bytes 1179656 | tf_op jit(solution)/shard_map/ppermute | solution.py:1181
  28.4 26.8 %collective-permute-start.4 = (bf16[256,768]{1,0:T(8,128)(2,1)S(1)}, bf16[256,768]{1,0:T(8,128)(2,1)S(1)}, u32[]{:S(2)}, u32[]{:S(2)}) collective-permute-start(bf16[256,768]{1,0:T(8,128)(2,1)S(1)} %get-tuple-element.452), channel_id=1, source_target_pairs={{0,0},{1,1},{2,2},{3,3},{4,4},{5,5},{6,6},{7,7},{8,8},{9,9},{10,10... | collective-permute-start | bytes 1179656 | tf_op jit(solution)/shard_map/ppermute | solution.py:1181
  95.4 23.2 %collective-permute-start.8 = (bf16[3072,768]{1,0:T(8,128)(2,1)}, bf16[3072,768]{1,0:T(8,128)(2,1)}, u32[]{:S(2)}, u32[]{:S(2)}) collective-permute-start(bf16[3072,768]{1,0:T(8,128)(2,1)} %bitcast.34), channel_id=1, source_target_pairs={{0,1},{1,0},{2,3},{3,2},{4,5},{5,4},{6,7},{7,6},{8,9},{9,8},{10,11... | collective-permute-start | bytes 14155784 | tf_op jit(solution)/shard_map/ppermute | solution.py:1040
  95.8 22.7 %collective-permute-start.9 = (bf16[256,768]{1,0:T(8,128)(2,1)}, bf16[256,768]{1,0:T(8,128)(2,1)S(1)}, u32[]{:S(2)}, u32[]{:S(2)}) collective-permute-start(bf16[256,768]{1,0:T(8,128)(2,1)} %get-tuple-element.249), channel_id=1, source_target_pairs={{0,0},{1,1},{2,2},{3,3},{4,4},{5,5},{6,6},{7,7},{8,8},{9,9},{10,10... | collective-permute-start | bytes 1179656 | tf_op jit(solution)/shard_map/ppermute | solution.py:1193
  96.8 21.7 %collective-permute-start.10 = (bf16[256,768]{1,0:T(8,128)(2,1)}, bf16[256,768]{1,0:T(8,128)(2,1)S(1)}, u32[]{:S(2)}, u32[]{:S(2)}) collective-permute-start(bf16[256,768]{1,0:T(8,128)(2,1)} %get-tuple-element.250), channel_id=1, source_target_pairs={{1,0},{0,1},{3,2},{2,3},{5,4},{4,5},{7,6},{6,7},{9,8},{8,9},{11,10... | collective-permute-start | bytes 1179656 | tf_op jit(solution)/shard_map/ppermute | solution.py:1193
  96.9 21.6 %collective-permute-start.11 = (bf16[256,768]{1,0:T(8,128)(2,1)}, bf16[256,768]{1,0:T(8,128)(2,1)S(1)}, u32[]{:S(2)}, u32[]{:S(2)}) collective-permute-start(bf16[256,768]{1,0:T(8,128)(2,1)} %get-tuple-element.251), channel_id=1, source_target_pairs={{2,0},{3,1},{0,2},{1,3},{6,4},{7,5},{4,6},{5,7},{10,8},{11,9},{8,1... | collective-permute-start | bytes 1179656 | tf_op jit(solution)/shard_map/ppermute | solution.py:1193
  98.5 20.0 %collective-permute-start.12 = (bf16[256,768]{1,0:T(8,128)(2,1)}, bf16[256,768]{1,0:T(8,128)(2,1)S(1)}, u32[]{:S(2)}, u32[]{:S(2)}) collective-permute-start(bf16[256,768]{1,0:T(8,128)(2,1)} %get-tuple-element.252), channel_id=1, source_target_pairs={{3,0},{2,1},{1,2},{0,3},{7,4},{6,5},{5,6},{4,7},{11,8},{10,9},{9,1... | collective-permute-start | bytes 1179656 | tf_op jit(solution)/shard_map/ppermute | solution.py:1193
  123.5 39.3 %collective-permute-start.13 = (bf16[1024,768]{1,0:T(8,128)(2,1)S(1)}, bf16[1024,768]{1,0:T(8,128)(2,1)S(1)}, u32[]{:S(2)}, u32[]{:S(2)}) collective-permute-start(bf16[1024,768]{1,0:T(8,128)(2,1)S(1)} %get-tuple-element.272), channel_id=1, source_target_pairs={{0,2},{1,5},{2,0},{3,7},{4,6},{5,1},{6,4},{7,3},{8,10},{9,13},{10,... | collective-permute-start | bytes 4718600 | tf_op jit(solution)/shard_map/ppermute | solution.py:1040
  125.3 37.5 %collective-permute-start.14 = (bf16[512,768]{1,0:T(8,128)(2,1)S(1)}, bf16[512,768]{1,0:T(8,128)(2,1)S(1)}, u32[]{:S(2)}, u32[]{:S(2)}) collective-permute-start(bf16[512,768]{1,0:T(8,128)(2,1)S(1)} %get-tuple-element.274), channel_id=1, source_target_pairs={{0,8},{1,9},{2,10},{3,11},{4,12},{5,13},{6,14},{7,15},{8,0},{9,1},... | collective-permute-start | bytes 2359304 | tf_op jit(solution)/shard_map/ppermute | solution.py:1040
  187.5 16.5 %collective-permute-start.22 = (bf16[768,768]{1,0:T(8,128)(2,1)S(1)}, bf16[768,768]{1,0:T(8,128)(2,1)S(1)}, u32[]{:S(2)}, u32[]{:S(2)}) collective-permute-start(bf16[768,768]{1,0:T(8,128)(2,1)S(1)} %get-tuple-element.341), channel_id=1, source_target_pairs={{0,2},{1,5},{2,0},{3,7},{4,6},{5,1},{6,4},{7,3},{8,10},{9,13},{10,... | collective-permute-start | bytes 3538952 | tf_op jit(solution)/shard_map/ppermute | solution.py:1040
  188.3 15.7 %collective-permute-start.20 = (bf16[128,768]{1,0:T(8,128)(2,1)S(1)}, bf16[128,768]{1,0:T(8,128)(2,1)S(1)}, u32[]{:S(2)}, u32[]{:S(2)}) collective-permute-start(bf16[128,768]{1,0:T(8,128)(2,1)S(1)} %get-tuple-element.335), channel_id=1, source_target_pairs={{0,16},{1,17},{2,18},{3,19},{4,20},{5,21},{6,22},{7,23},{8,24},{9,... | collective-permute-start | bytes 589832 | tf_op jit(solution)/shard_map/ppermute | solution.py:1040
  204.3 19.9 %collective-permute-start.25 = (bf16[384,768]{1,0:T(8,128)(2,1)S(1)}, bf16[384,768]{1,0:T(8,128)(2,1)S(1)}, u32[]{:S(2)}, u32[]{:S(2)}) collective-permute-start(bf16[384,768]{1,0:T(8,128)(2,1)S(1)} %get-tuple-element.360), channel_id=1, source_target_pairs={{0,4},{1,9},{2,6},{3,11},{4,0},{5,13},{6,2},{7,15},{8,12},{9,1},{1... | collective-permute-start | bytes 1769480 | tf_op jit(solution)/shard_map/ppermute | solution.py:1040
  207.9 16.3 %collective-permute-start.23 = (bf16[128,768]{1,0:T(8,128)(2,1)S(1)}, bf16[128,768]{1,0:T(8,128)(2,1)S(1)}, u32[]{:S(2)}, u32[]{:S(2)}) collective-permute-start(bf16[128,768]{1,0:T(8,128)(2,1)S(1)} %get-tuple-element.363.refs_0_), channel_id=1, source_target_pairs={{0,16},{1,17},{2,18},{3,19},{4,20},{5,21},{6,22},{7,23},{8,24},{9,... | collective-permute-start | bytes 589832 | tf_op jit(solution)/shard_map/ppermute | solution.py:1040
  209.9 14.3 %collective-permute-start.24 = (bf16[64,768]{1,0:T(8,128)(2,1)S(1)}, bf16[64,768]{1,0:T(8,128)(2,1)S(1)}, u32[]{:S(2)}, u32[]{:S(2)}) collective-permute-start(bf16[64,768]{1,0:T(8,128)(2,1)S(1)} %get-tuple-element.365.refs_2_), channel_id=1, source_target_pairs={{0,16},{1,17},{2,18},{3,19},{4,20},{5,21},{6,22},{7,23},{8,24},{9,... | collective-permute-start | bytes 294920 | tf_op jit(solution)/shard_map/ppermute | solution.py:1040
  236.4 18.1 %collective-permute-start.32 = (bf16[512,768]{1,0:T(8,128)(2,1)S(1)}, bf16[512,768]{1,0:T(8,128)(2,1)S(1)}, u32[]{:S(2)}, u32[]{:S(2)}) collective-permute-start(bf16[512,768]{1,0:T(8,128)(2,1)S(1)} %get-tuple-element.384.refs_0_), channel_id=1, source_target_pairs={{0,4},{1,9},{2,6},{3,11},{4,0},{5,13},{6,2},{7,15},{8,12},{9,1},{1... | collective-permute-start | bytes 2359304 | tf_op jit(solution)/shard_map/ppermute | solution.py:1040
  237.8 16.7 %collective-permute-start.33 = (bf16[256,768]{1,0:T(8,128)(2,1)S(1)}, bf16[256,768]{1,0:T(8,128)(2,1)S(1)}, u32[]{:S(2)}, u32[]{:S(2)}) collective-permute-start(bf16[256,768]{1,0:T(8,128)(2,1)S(1)} %get-tuple-element.386.refs_2_), channel_id=1, source_target_pairs={{0,2},{1,3},{2,0},{3,1},{4,6},{5,7},{6,4},{7,5},{8,10},{9,11},{10,... | collective-permute-start | bytes 1179656 | tf_op jit(solution)/shard_map/ppermute | solution.py:1040
  239.3 14.7 %collective-permute-start.34 = (bf16[208,768]{1,0:T(8,128)(2,1)S(1)}, bf16[208,768]{1,0:T(8,128)(2,1)S(1)}, u32[]{:S(2)}, u32[]{:S(2)}) collective-permute-start(bf16[208,768]{1,0:T(8,128)(2,1)S(1)} %settle_local.3.refs_0_), channel_id=1, source_target_pairs={{0,16},{1,17},{2,18},{3,19},{4,20},{5,21},{6,22},{7,23},{8,24},{9,... | collective-permute-start | bytes 958472 | tf_op jit(solution)/shard_map/ppermute | solution.py:1040
  255.3 14.8 %collective-permute-start.36 = (bf16[512,768]{1,0:T(8,128)(2,1)S(1)}, bf16[512,768]{1,0:T(8,128)(2,1)S(1)}, u32[]{:S(2)}, u32[]{:S(2)}) collective-permute-start(bf16[512,768]{1,0:T(8,128)(2,1)S(1)} %get-tuple-element.398.refs_0_), channel_id=1, source_target_pairs={{0,2},{1,5},{2,0},{3,7},{4,6},{5,1},{6,4},{7,3},{8,10},{9,13},{10,... | collective-permute-start | bytes 2359304 | tf_op jit(solution)/shard_map/ppermute | solution.py:1040
  258.0 25.4 %collective-permute-start.39 = (bf16[512,768]{1,0:T(8,128)(2,1)S(1)}, bf16[512,768]{1,0:T(8,128)(2,1)S(1)}, u32[]{:S(2)}, u32[]{:S(2)}) collective-permute-start(bf16[512,768]{1,0:T(8,128)(2,1)S(1)} %get-tuple-element.403.refs_2_), channel_id=1, source_target_pairs={{0,2},{1,5},{2,0},{3,7},{4,6},{5,1},{6,4},{7,3},{8,10},{9,13},{10,... | collective-permute-start | bytes 2359304 | tf_op jit(solution)/shard_map/ppermute | solution.py:1040
  284.3 16.7 %collective-permute-start.42 = (bf16[3072,768]{1,0:T(8,128)(2,1)S(1)}, bf16[3072,768]{1,0:T(8,128)(2,1)S(1)}, u32[]{:S(2)}, u32[]{:S(2)}) collective-permute-start(bf16[3072,768]{1,0:T(8,128)(2,1)S(1)} %join_local.11.half_ref), channel_id=1, source_target_pairs={{0,1},{1,0},{2,3},{3,2},{4,5},{5,4},{6,7},{7,6},{8,9},{9,8},{10,11... | collective-permute-start | bytes 14155784 | tf_op jit(solution)/shard_map/ppermute | solution.py:1040
  284.5 16.5 %collective-permute-start.43 = (bf16[784,768]{1,0:T(8,128)(2,1)S(1)}, bf16[784,768]{1,0:T(8,128)(2,1)S(1)}, u32[]{:S(2)}, u32[]{:S(2)}) collective-permute-start(bf16[784,768]{1,0:T(8,128)(2,1)S(1)} %join_local.12.refs_0_), channel_id=1, source_target_pairs={{0,2},{1,5},{2,0},{3,7},{4,6},{5,1},{6,4},{7,3},{8,10},{9,13},{10,... | collective-permute-start | bytes 3612680 | tf_op jit(solution)/shard_map/ppermute | solution.py:1040
  (47 other events, 355.7 us)

commit v4 on v2

--- a/solution.py
+++ b/solution.py
@@ -699,7 +699,7 @@
         expand_ref[...] = half_ref[...].T.astype(F32)
 
 
-def feed_out(which, values, before=(), block=512):
+def feed_out(which, values, before=(), block=768):
     width = values.shape[1]
     half = values.shape[0] // 2
     steps = half // block
@@ -723,7 +723,7 @@
         ),
         out_shape=shapes(((2 * half, width), F32), ((width, 2 * half), F32)),
         input_output_aliases={2 + i: i for i in range(len(before))},
-        compiler_params=pltpu.CompilerParams(vmem_limit_bytes=16 * 2**20),
+        compiler_params=pltpu.CompilerParams(vmem_limit_bytes=28 * 2**20),
         cost_estimate=BRIEF,
         name="feed_out",
     )(which, values, *before)

time: 317 us -> 317 us (level)
  transfers between devices with their start and end apart: 45 -> 45, of which waited for: 16 -> 16; matrix products, arithmetic and copies ran while one was open for 3% -> 3% of each run, Pallas kernels for 36% -> 35%
where the time goes in v4:
time: 317 us; the launch traced here: 313 us
  Pallas kernels  169 us (53%)
  waiting for transfers between devices  88.6 us (28%)
  starting transfers between devices  41.9 us (13%)
  local copies, waits for them, and re-layouts  6.34 us (2%)
  matrix products  4.18 us (1%)
    ppermute x29, waiting for transfers between devices, swap(): return lax.ppermute(values, ('rows', 'seq'), self.pairs)  61.1 us
    pallas_call x2, Pallas kernels, feed_back(): pl.pallas_call(functools.partial(feed_back_kernel, steps=steps, block=min...  36.4 us
    pallas_call x1, Pallas kernels, attention_backward(): pl.pallas_call(functools.partial(backward_kernel, block=min(512, keys)),...  36 us
    ppermute x29, starting transfers between devices, swap(): return lax.ppermute(values, ('rows', 'seq'), self.pairs)  31.6 us
    pallas_call x1, Pallas kernels, feed_forward(): pl.pallas_call(functools.partial(feed_forward_kernel, steps=steps, held=h...  23.5 us
    pallas_call x1, Pallas kernels, attention_forward(): pl.pallas_call(functools.partial(forward_kernel, block=min(512, queries))...  22.4 us
    ppermute x8, waiting for transfers between devices, send_pieces(): lax.ppermute(values[part], 'seq', trade(False, part))  14.5 us
    ppermute x4, waiting for transfers between devices, body(): lax.ppermute(value, 'seq', trade(True, part))  13.1 us
  transfers between devices with their start and end apart: 45, of which 16 were waited for; matrix products, arithmetic and copies ran while one was open for 3% of the time, Pallas kernels for 35%

profile of v4, /device:TPU:0, one launch (start us, length us, event | category | flops | bytes accessed | tf_op | source)
XLA Modules:
  0.0 313.0 jit_solution(287036513344154176)
XLA Ops:
  11.9 4.6 %collective-permute-done.2.refs_2_ = bf16[272,768]{1,0:T(8,128)(2,1)S(1)} collective-permute-done((bf16[272,768]{1,0:T(8,128)(2,1)S(1)}, bf16[272,768]{1,0:T(8,128)(2,1)S(1)}, u32[]{:S(2)}, u32[]{:S(2)}) %collective-permute-start.2) | collective-permute-done | bytes 417824 | tf_op jit(solution)/shard_map/ppermute | solution.py:1211
  16.5 8.4 %collective-permute-done.3.refs_3_ = bf16[272,768]{1,0:T(8,128)(2,1)S(1)} collective-permute-done((bf16[272,768]{1,0:T(8,128)(2,1)S(1)}, bf16[272,768]{1,0:T(8,128)(2,1)S(1)}, u32[]{:S(2)}, u32[]{:S(2)}) %collective-permute-start.3) | collective-permute-done | bytes 417824 | tf_op jit(solution)/shard_map/ppermute | solution.py:1211
  32.8 22.4 %attention_forward.1 = (bf16[1024,768]{1,0:T(8,128)(2,1)}, bf16[12,1024,128]{2,1,0:T(8,128)(2,1)}) custom-call(bf16[1024,768]{1,0:T(8,128)(2,1)S(1)} %multiply_convert_fusion.q_ref, bf16[1024,768]{1,0:T(8,128)(2,1)S(1)} %convolution_convert_fusion.k_ref, bf16[1024,768]{1,0:T(8,128)(2,1)S(1)} %add_convert_fusion.v_ref, bf16[1024,128]{1,0:T(8,128)(2,1)S(1)} %copy-done.3, ...), custom_call_target="tpu_custom_call" | custom-call | flops 1 | bytes 1 | tf_op jit(solution)/shard_map/attention_forward/pallas_call | solution.py:90
  55.2 23.5 %feed_forward.1 = (bf16[1024,768]{1,0:T(8,128)(2,1)}, f32[1024,128]{1,0:T(8,128)}, bf16[1024,768]{1,0:T(8,128)(2,1)}, bf16[3072,1024]{1,0:T(8,128)(2,1)}, bf16[1...) custom-call(bf16[1024,768]{1,0:T(8,128)(2,1)S(1)} %copy-done, ...), custom_call_target="tpu_custom_call" | custom-call | flops 1 | bytes 1 | tf_op jit(solution)/shard_map/feed_forward/pallas_call | solution.py:327
  78.7 16.7 %feed_back.1 = (bf16[2,1536,768]{2,1,0:T(8,128)(2,1)}, f32[8,512]{1,0:T(8,128)}, bf16[1024,768]{1,0:T(8,128)(2,1)}) custom-call(s32[1]{0:T(128)S(6)} %sub.2.which_ref, bf16[1024,768]{1,0:T(8,128)(2,1)} %get-tuple-element.239.d_down_ref, bf16[1024,3072]{1,0:T(8,128)(2,1)} %get-tuple-element.240.slope_ref, bf16[3072,1024]{1,0:T(8,128)(2,1)} %get-tuple-element.241.active_t_ref, ...), custom_call_target="tpu_custom_call" | custom-call | flops 1 | bytes 1 | tf_op jit(solution)/shard_map/feed_back/pallas_call | solution.py:496
  98.8 19.7 %feed_back_last.1 = (bf16[2,1536,768]{2,1,0:T(8,128)(2,1)}, f32[8,512]{1,0:T(8,128)}, bf16[1024,768]{1,0:T(8,128)(2,1)}, bf16[1024,768]{1,0:T(8,128)(2,1)}, f32[8,768]{1,0:T(8,128)}) custom-call(s32[1]{0:T(128)} %bitcast.1.which_ref.core_ref, bf16[1024,768]{1,0:T(8,128)(2,1)} %get-tuple-element.239.d_down_ref, ...), custom_call_target="tpu_custom_call" | custom-call | flops 1 | bytes 1 | tf_op jit(solution)/shard_map/feed_back_last/pallas_call | solution.py:496
  118.7 4.9 %scatter_first.1 = (bf16[1024,768]{1,0:T(8,128)(2,1)S(1)}, bf16[1024,768]{1,0:T(8,128)(2,1)S(1)}, bf16[512,768]{1,0:T(8,128)(2,1)S(1)}, bf16[512,768]{1,0:T(8,128)(2,1)S(1)}) custom-call(s32[2]{0:T(128)S(1)} %get-tuple-element.453.bits_ref, bf16[3072,768]{1,0:T(8,128)(2,1)} %bitcast.30, bf16[3072,768]{1,0:T(8,128)(2,1)} %collective-permute-done.8.got_at), custom_call_target="tpu_custom_call" | custom-call | flops 1 | bytes 1 | tf_op jit(solution)/shard_map/scatter_first/pallas_call | solution.py:872
  126.9 36.0 %attention_backward.1 = (bf16[1024,768]{1,0:T(8,128)(2,1)}, bf16[1024,768]{1,0:T(8,128)(2,1)}, bf16[1024,768]{1,0:T(8,128)(2,1)}) custom-call(bf16[12,1024,128]{2,1,0:T(8,128)(2,1)} %get-tuple-element.261.query_ref, bf16[1024,768]{1,0:T(8,128)(2,1)S(1)} %convolution_convert_fusion.k_ref, bf16[1024,768]{1,0:T(8,128)(2,1)S(1)} %copy-done.2, ...), custom_call_target="tpu_custom_call" | custom-call | flops 1 | bytes 1 | tf_op jit(solution)/shard_map/attention_backward/pallas_call | solution.py:168
  166.9 8.0 %weight_halves.1 = (bf16[1536,768]{1,0:T(8,128)(2,1)S(1)}, bf16[1536,768]{1,0:T(8,128)(2,1)S(1)}, f32[16,768]{1,0:T(8,128)S(1)}) custom-call(s32[1]{0:T(128)} %bitcast.1.which_ref.core_ref, f32[8,768]{1,0:T(8,128)S(1)} %copy-done.6, f32[8,768]{1,0:T(8,128)S(1)} %copy-done.5, f32[8,512]{1,0:T(8,128)S(1)} %copy-done.8, f32[8,512]{1,0:T(8,128)S(1)} %copy-done.7, ...), custom_call_target="tpu_custom_call" | custom-call | flops 1 | bytes 1 | tf_op jit(solution)/shard_map/weight_halves/pallas_call | solution.py:631
  179.7 6.6 %input_grad.1 = (bf16[256,768]{1,0:T(8,128)(2,1)S(1)}, bf16[256,768]{1,0:T(8,128)(2,1)S(1)}, bf16[256,768]{1,0:T(8,128)(2,1)S(1)}, bf16[256,768]{1,0:T(8,128)(2,1)S(1)}) custom-call(bf16[1024,768]{1,0:T(8,128)(2,1)} %get-tuple-element.287.refs_5_.refs_0_, bf16[1024,768]{1,0:T(8,128)(2,1)} %get-tuple-element.310.refs_1_, bf16[768,768]{1,0:T(8,128)(2,1)} %refs_2_.1, ...), custom_call_target="tpu_custom_call" | custom-call | flops 1 | bytes 1 | tf_op jit(solution)/shard_map/input_grad/pallas_call | solution.py:676
  191.3 3.2 %place.2 = bf16[4,256,768]{2,1,0:T(8,128)(2,1)} custom-call(s32[1]{0:T(128)} %bitcast.at_ref, bf16[256,768]{1,0:T(8,128)(2,1)} %copy-done.12, bf16[256,768]{1,0:T(8,128)(2,1)} %copy-done.13, bf16[256,768]{1,0:T(8,128)(2,1)} %copy-done.14, bf16[256,768]{1,0:T(8,128)(2,1)} %copy-done.15), custom_call_target="tpu_custom_call" | custom-call | flops 1 | bytes 1 | tf_op jit(solution)/shard_map/place/pallas_call | solution.py:774
  194.6 9.5 %collective-permute-done.21.refs_3_ = bf16[64,768]{1,0:T(8,128)(2,1)S(1)} collective-permute-done((bf16[64,768]{1,0:T(8,128)(2,1)S(1)}, bf16[64,768]{1,0:T(8,128)(2,1)S(1)}, u32[]{:S(2)}, u32[]{:S(2)}) %collective-permute-start.21) | collective-permute-done | bytes 98336 | tf_op jit(solution)/shard_map/ppermute | solution.py:1029
  211.0 5.8 %collective-permute-done.28.refs_3_ = bf16[256,768]{1,0:T(8,128)(2,1)S(1)} collective-permute-done((bf16[256,768]{1,0:T(8,128)(2,1)S(1)}, bf16[256,768]{1,0:T(8,128)(2,1)S(1)}, u32[]{:S(2)}, u32[]{:S(2)}) %collective-permute-start.28) | collective-permute-done | bytes 393248 | tf_op jit(solution)/shard_map/ppermute | solution.py:1182
  216.8 7.5 %collective-permute-done.24.refs_3_ = bf16[64,768]{1,0:T(8,128)(2,1)S(1)} collective-permute-done((bf16[64,768]{1,0:T(8,128)(2,1)S(1)}, bf16[64,768]{1,0:T(8,128)(2,1)S(1)}, u32[]{:S(2)}, u32[]{:S(2)}) %collective-permute-start.24) | collective-permute-done | bytes 98336 | tf_op jit(solution)/shard_map/ppermute | solution.py:1029
  227.8 5.0 %collective-permute-done.30.refs_3_ = bf16[128,768]{1,0:T(8,128)(2,1)S(1)} collective-permute-done((bf16[128,768]{1,0:T(8,128)(2,1)S(1)}, bf16[128,768]{1,0:T(8,128)(2,1)S(1)}, u32[]{:S(2)}, u32[]{:S(2)}) %collective-permute-start.30) | collective-permute-done | bytes 196640 | tf_op jit(solution)/shard_map/ppermute | solution.py:1029
  232.8 3.0 collective-permute-done.31.refs_1_
  240.7 8.6 %collective-permute-done.35.refs_2_ = bf16[256,768]{1,0:T(8,128)(2,1)S(1)} collective-permute-done((bf16[256,768]{1,0:T(8,128)(2,1)S(1)}, bf16[256,768]{1,0:T(8,128)(2,1)S(1)}, u32[]{:S(2)}, u32[]{:S(2)}) %collective-permute-start.35) | collective-permute-done | bytes 393248 | tf_op jit(solution)/shard_map/ppermute | solution.py:1182
  249.3 4.8 %collective-permute-done.34.refs_1_ = bf16[208,768]{1,0:T(8,128)(2,1)S(1)} collective-permute-done((bf16[208,768]{1,0:T(8,128)(2,1)S(1)}, bf16[208,768]{1,0:T(8,128)(2,1)S(1)}, u32[]{:S(2)}, u32[]{:S(2)}) %collective-permute-start.34) | collective-permute-done | bytes 319520 | tf_op jit(solution)/shard_map/ppermute | solution.py:1029
  261.3 7.8 %collective-permute-done.38.refs_1_ = bf16[208,768]{1,0:T(8,128)(2,1)S(1)} collective-permute-done((bf16[208,768]{1,0:T(8,128)(2,1)S(1)}, bf16[208,768]{1,0:T(8,128)(2,1)S(1)}, u32[]{:S(2)}, u32[]{:S(2)}) %collective-permute-start.38) | collective-permute-done | bytes 319520 | tf_op jit(solution)/shard_map/ppermute | solution.py:1029
  274.0 9.5 %collective-permute-done.40.refs_7_ = bf16[256,768]{1,0:T(8,128)(2,1)S(1)} collective-permute-done((bf16[256,768]{1,0:T(8,128)(2,1)S(1)}, bf16[256,768]{1,0:T(8,128)(2,1)S(1)}, u32[]{:S(2)}, u32[]{:S(2)}) %collective-permute-start.40) | collective-permute-done | bytes 393248 | tf_op jit(solution)/shard_map/ppermute | solution.py:1029
  285.6 4.9 %feed_out.2 = (f32[3072,768]{1,0:T(8,128)}, f32[768,3072]{1,0:T(8,128)}) custom-call(s32[1]{0:T(128)} %bitcast.1.which_ref.core_ref, bf16[3072,768]{1,0:T(8,128)(2,1)S(1)} %join_local.11.half_ref), custom_call_target="tpu_custom_call" | custom-call | flops 1 | bytes 1 | tf_op jit(solution)/shard_map/feed_out/pallas_call | solution.py:706
  290.4 10.6 %collective-permute-done.43.refs_1_ = bf16[784,768]{1,0:T(8,128)(2,1)S(1)} collective-permute-done((bf16[784,768]{1,0:T(8,128)(2,1)S(1)}, bf16[784,768]{1,0:T(8,128)(2,1)S(1)}, u32[]{:S(2)}, u32[]{:S(2)}) %collective-permute-start.43) | collective-permute-done | bytes 1204256 | tf_op jit(solution)/shard_map/ppermute | solution.py:1029
  301.3 2.6 attn_out.2
  304.0 4.9 %feed_out.3 = (f32[3072,768]{1,0:T(8,128)}, f32[768,3072]{1,0:T(8,128)}) custom-call(s32[1]{0:T(128)S(6)} %sub.2.which_ref, bf16[3072,768]{1,0:T(8,128)(2,1)S(1)} %collective-permute-done.42.half_ref, f32[3072,768]{1,0:T(8,128)} %get-tuple-element.437.refs_0_, f32[768,3072]{1,0:T(8,128)} %get-tuple-element.438.refs_1_), custom_call_target="tpu_custom_call", output_to_operand_aliasing={{0}: (2, {}), {1}: (3, {})} | custom-call | flops 1 | bytes 1 | tf_op jit(solution)/shard_map/feed_out/pallas_call | solution.py:706
  (172 shorter events, 72.7 us)
Async XLA Ops:
  6.0 18.9 %collective-permute-start.3 = (bf16[272,768]{1,0:T(8,128)(2,1)S(1)}, bf16[272,768]{1,0:T(8,128)(2,1)S(1)}, u32[]{:S(2)}, u32[]{:S(2)}) collective-permute-start(bf16[272,768]{1,0:T(8,128)(2,1)S(1)} %get-tuple-element.232), channel_id=1, source_target_pairs={{0,3},{1,2},{2,1},{3,0},{4,7},{5,6},{6,5},{7,4},{8,11},{9,10},{10,... | collective-permute-start | bytes 1253384 | tf_op jit(solution)/shard_map/ppermute | solution.py:1211
  26.5 28.7 %collective-permute-start.7 = (bf16[256,768]{1,0:T(8,128)(2,1)S(1)}, bf16[256,768]{1,0:T(8,128)(2,1)S(1)}, u32[]{:S(2)}, u32[]{:S(2)}) collective-permute-start(bf16[256,768]{1,0:T(8,128)(2,1)S(1)} %get-tuple-element.449), channel_id=1, source_target_pairs={{0,3},{1,2},{2,1},{3,0},{4,7},{5,6},{6,5},{7,4},{8,11},{9,10},{10,... | collective-permute-start | bytes 1179656 | tf_op jit(solution)/shard_map/ppermute | solution.py:1170
  28.0 27.2 %collective-permute-start.6 = (bf16[256,768]{1,0:T(8,128)(2,1)S(1)}, bf16[256,768]{1,0:T(8,128)(2,1)S(1)}, u32[]{:S(2)}, u32[]{:S(2)}) collective-permute-start(bf16[256,768]{1,0:T(8,128)(2,1)S(1)} %get-tuple-element.450), channel_id=1, source_target_pairs={{0,2},{1,3},{2,0},{3,1},{4,6},{5,7},{6,4},{7,5},{8,10},{9,11},{10,... | collective-permute-start | bytes 1179656 | tf_op jit(solution)/shard_map/ppermute | solution.py:1170
  28.3 26.9 %collective-permute-start.5 = (bf16[256,768]{1,0:T(8,128)(2,1)S(1)}, bf16[256,768]{1,0:T(8,128)(2,1)S(1)}, u32[]{:S(2)}, u32[]{:S(2)}) collective-permute-start(bf16[256,768]{1,0:T(8,128)(2,1)S(1)} %get-tuple-element.451), channel_id=1, source_target_pairs={{0,1},{1,0},{2,3},{3,2},{4,5},{5,4},{6,7},{7,6},{8,9},{9,8},{10,11... | collective-permute-start | bytes 1179656 | tf_op jit(solution)/shard_map/ppermute | solution.py:1170
  28.4 26.8 %collective-permute-start.4 = (bf16[256,768]{1,0:T(8,128)(2,1)S(1)}, bf16[256,768]{1,0:T(8,128)(2,1)S(1)}, u32[]{:S(2)}, u32[]{:S(2)}) collective-permute-start(bf16[256,768]{1,0:T(8,128)(2,1)S(1)} %get-tuple-element.452), channel_id=1, source_target_pairs={{0,0},{1,1},{2,2},{3,3},{4,4},{5,5},{6,6},{7,7},{8,8},{9,9},{10,10... | collective-permute-start | bytes 1179656 | tf_op jit(solution)/shard_map/ppermute | solution.py:1170
  95.4 23.2 %collective-permute-start.8 = (bf16[3072,768]{1,0:T(8,128)(2,1)}, bf16[3072,768]{1,0:T(8,128)(2,1)}, u32[]{:S(2)}, u32[]{:S(2)}) collective-permute-start(bf16[3072,768]{1,0:T(8,128)(2,1)} %bitcast.34), channel_id=1, source_target_pairs={{0,1},{1,0},{2,3},{3,2},{4,5},{5,4},{6,7},{7,6},{8,9},{9,8},{10,11... | collective-permute-start | bytes 14155784 | tf_op jit(solution)/shard_map/ppermute | solution.py:1029
  95.8 22.7 %collective-permute-start.9 = (bf16[256,768]{1,0:T(8,128)(2,1)}, bf16[256,768]{1,0:T(8,128)(2,1)S(1)}, u32[]{:S(2)}, u32[]{:S(2)}) collective-permute-start(bf16[256,768]{1,0:T(8,128)(2,1)} %get-tuple-element.249), channel_id=1, source_target_pairs={{0,0},{1,1},{2,2},{3,3},{4,4},{5,5},{6,6},{7,7},{8,8},{9,9},{10,10... | collective-permute-start | bytes 1179656 | tf_op jit(solution)/shard_map/ppermute | solution.py:1182
  96.8 21.7 %collective-permute-start.10 = (bf16[256,768]{1,0:T(8,128)(2,1)}, bf16[256,768]{1,0:T(8,128)(2,1)S(1)}, u32[]{:S(2)}, u32[]{:S(2)}) collective-permute-start(bf16[256,768]{1,0:T(8,128)(2,1)} %get-tuple-element.250), channel_id=1, source_target_pairs={{1,0},{0,1},{3,2},{2,3},{5,4},{4,5},{7,6},{6,7},{9,8},{8,9},{11,10... | collective-permute-start | bytes 1179656 | tf_op jit(solution)/shard_map/ppermute | solution.py:1182
  97.0 21.6 %collective-permute-start.11 = (bf16[256,768]{1,0:T(8,128)(2,1)}, bf16[256,768]{1,0:T(8,128)(2,1)S(1)}, u32[]{:S(2)}, u32[]{:S(2)}) collective-permute-start(bf16[256,768]{1,0:T(8,128)(2,1)} %get-tuple-element.251), channel_id=1, source_target_pairs={{2,0},{3,1},{0,2},{1,3},{6,4},{7,5},{4,6},{5,7},{10,8},{11,9},{8,1... | collective-permute-start | bytes 1179656 | tf_op jit(solution)/shard_map/ppermute | solution.py:1182
  98.6 20.0 %collective-permute-start.12 = (bf16[256,768]{1,0:T(8,128)(2,1)}, bf16[256,768]{1,0:T(8,128)(2,1)S(1)}, u32[]{:S(2)}, u32[]{:S(2)}) collective-permute-start(bf16[256,768]{1,0:T(8,128)(2,1)} %get-tuple-element.252), channel_id=1, source_target_pairs={{3,0},{2,1},{1,2},{0,3},{7,4},{6,5},{5,6},{4,7},{11,8},{10,9},{9,1... | collective-permute-start | bytes 1179656 | tf_op jit(solution)/shard_map/ppermute | solution.py:1182
  123.6 39.3 %collective-permute-start.13 = (bf16[1024,768]{1,0:T(8,128)(2,1)S(1)}, bf16[1024,768]{1,0:T(8,128)(2,1)S(1)}, u32[]{:S(2)}, u32[]{:S(2)}) collective-permute-start(bf16[1024,768]{1,0:T(8,128)(2,1)S(1)} %get-tuple-element.272), channel_id=1, source_target_pairs={{0,2},{1,5},{2,0},{3,7},{4,6},{5,1},{6,4},{7,3},{8,10},{9,13},{10,... | collective-permute-start | bytes 4718600 | tf_op jit(solution)/shard_map/ppermute | solution.py:1029
  125.4 37.5 %collective-permute-start.14 = (bf16[512,768]{1,0:T(8,128)(2,1)S(1)}, bf16[512,768]{1,0:T(8,128)(2,1)S(1)}, u32[]{:S(2)}, u32[]{:S(2)}) collective-permute-start(bf16[512,768]{1,0:T(8,128)(2,1)S(1)} %get-tuple-element.274), channel_id=1, source_target_pairs={{0,8},{1,9},{2,10},{3,11},{4,12},{5,13},{6,14},{7,15},{8,0},{9,1},... | collective-permute-start | bytes 2359304 | tf_op jit(solution)/shard_map/ppermute | solution.py:1029
  187.5 16.5 %collective-permute-start.22 = (bf16[768,768]{1,0:T(8,128)(2,1)S(1)}, bf16[768,768]{1,0:T(8,128)(2,1)S(1)}, u32[]{:S(2)}, u32[]{:S(2)}) collective-permute-start(bf16[768,768]{1,0:T(8,128)(2,1)S(1)} %get-tuple-element.341), channel_id=1, source_target_pairs={{0,2},{1,5},{2,0},{3,7},{4,6},{5,1},{6,4},{7,3},{8,10},{9,13},{10,... | collective-permute-start | bytes 3538952 | tf_op jit(solution)/shard_map/ppermute | solution.py:1029
  188.4 15.7 %collective-permute-start.20 = (bf16[128,768]{1,0:T(8,128)(2,1)S(1)}, bf16[128,768]{1,0:T(8,128)(2,1)S(1)}, u32[]{:S(2)}, u32[]{:S(2)}) collective-permute-start(bf16[128,768]{1,0:T(8,128)(2,1)S(1)} %get-tuple-element.335), channel_id=1, source_target_pairs={{0,16},{1,17},{2,18},{3,19},{4,20},{5,21},{6,22},{7,23},{8,24},{9,... | collective-permute-start | bytes 589832 | tf_op jit(solution)/shard_map/ppermute | solution.py:1029
  204.3 19.9 %collective-permute-start.25 = (bf16[384,768]{1,0:T(8,128)(2,1)S(1)}, bf16[384,768]{1,0:T(8,128)(2,1)S(1)}, u32[]{:S(2)}, u32[]{:S(2)}) collective-permute-start(bf16[384,768]{1,0:T(8,128)(2,1)S(1)} %get-tuple-element.360), channel_id=1, source_target_pairs={{0,4},{1,9},{2,6},{3,11},{4,0},{5,13},{6,2},{7,15},{8,12},{9,1},{1... | collective-permute-start | bytes 1769480 | tf_op jit(solution)/shard_map/ppermute | solution.py:1029
  208.0 16.3 %collective-permute-start.23 = (bf16[128,768]{1,0:T(8,128)(2,1)S(1)}, bf16[128,768]{1,0:T(8,128)(2,1)S(1)}, u32[]{:S(2)}, u32[]{:S(2)}) collective-permute-start(bf16[128,768]{1,0:T(8,128)(2,1)S(1)} %get-tuple-element.363.refs_0_), channel_id=1, source_target_pairs={{0,16},{1,17},{2,18},{3,19},{4,20},{5,21},{6,22},{7,23},{8,24},{9,... | collective-permute-start | bytes 589832 | tf_op jit(solution)/shard_map/ppermute | solution.py:1029
  209.9 14.3 %collective-permute-start.24 = (bf16[64,768]{1,0:T(8,128)(2,1)S(1)}, bf16[64,768]{1,0:T(8,128)(2,1)S(1)}, u32[]{:S(2)}, u32[]{:S(2)}) collective-permute-start(bf16[64,768]{1,0:T(8,128)(2,1)S(1)} %get-tuple-element.365.refs_2_), channel_id=1, source_target_pairs={{0,16},{1,17},{2,18},{3,19},{4,20},{5,21},{6,22},{7,23},{8,24},{9,... | collective-permute-start | bytes 294920 | tf_op jit(solution)/shard_map/ppermute | solution.py:1029
  236.5 18.1 %collective-permute-start.32 = (bf16[512,768]{1,0:T(8,128)(2,1)S(1)}, bf16[512,768]{1,0:T(8,128)(2,1)S(1)}, u32[]{:S(2)}, u32[]{:S(2)}) collective-permute-start(bf16[512,768]{1,0:T(8,128)(2,1)S(1)} %get-tuple-element.384.refs_0_), channel_id=1, source_target_pairs={{0,4},{1,9},{2,6},{3,11},{4,0},{5,13},{6,2},{7,15},{8,12},{9,1},{1... | collective-permute-start | bytes 2359304 | tf_op jit(solution)/shard_map/ppermute | solution.py:1029
  237.9 16.7 %collective-permute-start.33 = (bf16[256,768]{1,0:T(8,128)(2,1)S(1)}, bf16[256,768]{1,0:T(8,128)(2,1)S(1)}, u32[]{:S(2)}, u32[]{:S(2)}) collective-permute-start(bf16[256,768]{1,0:T(8,128)(2,1)S(1)} %get-tuple-element.386.refs_2_), channel_id=1, source_target_pairs={{0,2},{1,3},{2,0},{3,1},{4,6},{5,7},{6,4},{7,5},{8,10},{9,11},{10,... | collective-permute-start | bytes 1179656 | tf_op jit(solution)/shard_map/ppermute | solution.py:1029
  239.3 14.7 %collective-permute-start.34 = (bf16[208,768]{1,0:T(8,128)(2,1)S(1)}, bf16[208,768]{1,0:T(8,128)(2,1)S(1)}, u32[]{:S(2)}, u32[]{:S(2)}) collective-permute-start(bf16[208,768]{1,0:T(8,128)(2,1)S(1)} %settle_local.3.refs_0_), channel_id=1, source_target_pairs={{0,16},{1,17},{2,18},{3,19},{4,20},{5,21},{6,22},{7,23},{8,24},{9,... | collective-permute-start | bytes 958472 | tf_op jit(solution)/shard_map/ppermute | solution.py:1029
  255.3 14.8 %collective-permute-start.36 = (bf16[512,768]{1,0:T(8,128)(2,1)S(1)}, bf16[512,768]{1,0:T(8,128)(2,1)S(1)}, u32[]{:S(2)}, u32[]{:S(2)}) collective-permute-start(bf16[512,768]{1,0:T(8,128)(2,1)S(1)} %get-tuple-element.398.refs_0_), channel_id=1, source_target_pairs={{0,2},{1,5},{2,0},{3,7},{4,6},{5,1},{6,4},{7,3},{8,10},{9,13},{10,... | collective-permute-start | bytes 2359304 | tf_op jit(solution)/shard_map/ppermute | solution.py:1029
  258.1 25.4 %collective-permute-start.39 = (bf16[512,768]{1,0:T(8,128)(2,1)S(1)}, bf16[512,768]{1,0:T(8,128)(2,1)S(1)}, u32[]{:S(2)}, u32[]{:S(2)}) collective-permute-start(bf16[512,768]{1,0:T(8,128)(2,1)S(1)} %get-tuple-element.403.refs_2_), channel_id=1, source_target_pairs={{0,2},{1,5},{2,0},{3,7},{4,6},{5,1},{6,4},{7,3},{8,10},{9,13},{10,... | collective-permute-start | bytes 2359304 | tf_op jit(solution)/shard_map/ppermute | solution.py:1029
  284.4 16.7 %collective-permute-start.42 = (bf16[3072,768]{1,0:T(8,128)(2,1)S(1)}, bf16[3072,768]{1,0:T(8,128)(2,1)S(1)}, u32[]{:S(2)}, u32[]{:S(2)}) collective-permute-start(bf16[3072,768]{1,0:T(8,128)(2,1)S(1)} %join_local.11.half_ref), channel_id=1, source_target_pairs={{0,1},{1,0},{2,3},{3,2},{4,5},{5,4},{6,7},{7,6},{8,9},{9,8},{10,11... | collective-permute-start | bytes 14155784 | tf_op jit(solution)/shard_map/ppermute | solution.py:1029
  284.5 16.5 %collective-permute-start.43 = (bf16[784,768]{1,0:T(8,128)(2,1)S(1)}, bf16[784,768]{1,0:T(8,128)(2,1)S(1)}, u32[]{:S(2)}, u32[]{:S(2)}) collective-permute-start(bf16[784,768]{1,0:T(8,128)(2,1)S(1)} %join_local.12.refs_0_), channel_id=1, source_target_pairs={{0,2},{1,5},{2,0},{3,7},{4,6},{5,1},{6,4},{7,3},{8,10},{9,13},{10,... | collective-permute-start | bytes 3612680 | tf_op jit(solution)/shard_map/ppermute | solution.py:1029
  (47 other events, 355.4 us)
